TPU v7x, 128 devices: a whole 4x4x4 slice. The times are simulated.
128 devices in a mesh: dom: 128 (over y, z, x, core).
Axes of the slice: x: 4, y: 4, z: 4, core: 2. Of those that a mesh axis runs over, the one named last changes fastest.
Arguments:
- rest_pos: float32 [3, 524288], P(None, 'dom'), may hold values from -6 to 6
- displacement: float32 [3, 524288], P(None, 'dom'), may hold values from -3 to 3
- velocity: float32 [3, 524288], P(None, 'dom'), may hold values from -6 to 6
- ext_force: float32 [3, 524288], P(None, 'dom'), may hold values from -6 to 6
- node_mass: float32 [524288], P('dom'), may hold values from 0.5 to 2
- body_accel: float32 [3], replicated, may hold values from -2 to 2
- connectivity: int32 [8, 524288], P(None, 'dom'), may hold values from 0 to 4095
- elem_material: int32 [4096], P('dom'), may hold values from 0 to 7
- stiffness: float32 [8, 24, 24], replicated, may hold values from -1.25 to 1.25
- shared_nodes: int32 [128, 5, 128], P('dom'), may hold values from 0 to 4095, as said below
- contact_slave: int32 [262144], P('dom'), may hold values from 0 to 4095
- contact_owner: int32 [262144, 1], P('dom'), may hold values from 0 to 127; in each aligned block of 2048 rows (0 to 2047, 2048 to 4095, ...) at most 64 rows name the same one
- contact_master: int32 [262144], P('dom'), may hold values from 0 to 4095
- contact_normal: float32 [3, 262144], P(None, 'dom'), may hold values from -4 to 4
- part_of_node: int32 [524288], P('dom'), may hold values from 0 to 799
- part_mass: float32 [400], replicated, may hold values from 327 to 1310
- part_center: float32 [3, 400], replicated, may hold values from -1 to 1
- part_inertia: float32 [3, 400], replicated, may hold values from 327 to 1310
Outputs:
- nodal_velocity: float32 [3, 524288], P(None, 'dom')
- part_motion: float32 [6, 400], replicated
Inputs may be any that keep to these rules, and one draw needn't show every extreme that they name: `connectivity`: offsets are taken modulo 4096 after adding the element's own local number. `shared_nodes`: on each partition d the 5 x 128 entries are distinct interface copies; entry k of list b on d and entry k of list b on d XOR 2**b are copies of one node. `contact_slave`: slave indices are local copies of the contact's own partition. `contact_owner`: among the 2048 contacts of one partition no owner appears more than 64 times, and some owner appears exactly 64 times. `contact_master`: master indices are local copies of the owner partition. `part_of_node`: values of 400 or more mark copies of no rigid part.
All inputs are finite; a program needn't handle non-finite values.
Results may differ from a plain program's by a relative error of at most 0.0001.
Values sent between devices are 32-bit elements; how exact they have to be, the bound alone decides.
No kernel may reach another device: no remote copies, remote signals or barrier semaphores. Data moves between devices by JAX's collectives and lax.ppermute only.
A program may use at most 128 MiB of HBM per device.

v0:
```python
import jax
import jax.numpy as jnp
from jax import lax
from jax.sharding import PartitionSpec as P

CYCLES = 3
PARTS_SIZE = 400


TIME_STEP = 0.1
DAMP_RATIO = 0.05
PENALTY = 2.0
GAP_WIDTH = 0.5
CONTACT_DAMP = 0.2


def partner(block, axis, apart):
    count = lax.axis_size(axis)
    route = []
    for low in range(count):
        high = low | 1 << apart
        if high != low and high < count:
            route += [(low, high), (high, low)]
    return lax.ppermute(block, axis, route)


def element_forces(corners, material, stiffness, nodal_field):
    blocks = corners.shape[1] // 128
    material_count = stiffness.shape[0]
    onehot = (material[:, None] == jnp.arange(material_count, dtype=jnp.int32)[None, :]).astype(
        jnp.float32
    )
    block_matrix = jnp.dot(
        onehot, stiffness.reshape(material_count, 576), precision=lax.Precision.HIGHEST
    ).reshape(blocks, 24, 24)
    gathered = nodal_field[:, corners].reshape(24, blocks, 128)
    forces = jnp.einsum("bij,jbk->ibk", block_matrix, gathered, precision=lax.Precision.HIGHEST)
    return (
        jnp.zeros_like(nodal_field)
        .at[:, corners.reshape(-1)]
        .add(forces.reshape(3, 8 * corners.shape[1]))
    )


def contact_push(slave_pos, slave_vel, master_pos, master_vel, normal):
    gap_size = jnp.sum((slave_pos - master_pos) * normal, axis=0)
    closing = jnp.sum((slave_vel - master_vel) * normal, axis=0)
    push_size = (
        PENALTY * GAP_WIDTH * jax.nn.softplus(-gap_size / GAP_WIDTH) - CONTACT_DAMP * closing
    )
    return push_size[None] * normal


def cross_product(left, right):
    return jnp.stack(
        [
            left[1] * right[2] - left[2] * right[1],
            left[2] * right[0] - left[0] * right[2],
            left[0] * right[1] - left[1] * right[0],
        ]
    )


def per_device(
    rest_pos,
    displacement,
    velocity,
    ext_force,
    node_mass,
    body_accel,
    connectivity,
    elem_material,
    stiffness,
    shared_nodes,
    contact_slave,
    contact_owner,
    contact_master,
    contact_normal,
    part_of_node,
    part_mass,
    part_center,
    part_inertia,
):
    domains = lax.axis_size("dom")
    neighbours = shared_nodes.shape[1]
    shared_count = shared_nodes.shape[2]
    shared_flat = shared_nodes.reshape(-1)
    accel_column = body_accel[:, None]
    node_count = displacement.shape[1]
    local_elem = jnp.arange(connectivity.shape[1], dtype=jnp.int32)
    corners = (connectivity + local_elem[None, :]) % node_count
    displaced = displacement
    speeds = velocity
    assembled = jnp.zeros_like(displacement)
    for cycle_index in range(CYCLES):
        internal = element_forces(
            corners, elem_material, stiffness, displaced + DAMP_RATIO * speeds
        )
        own_values = internal[:, shared_flat].reshape(3, neighbours, shared_count)
        received = []
        for bit_number in range(neighbours):
            received.append(partner(own_values[:, bit_number], "dom", bit_number))
        assembled = internal.at[:, shared_flat].add(
            jnp.stack(received, axis=1).reshape(3, neighbours * shared_count)
        )
        speeds = speeds + TIME_STEP * ((ext_force - assembled) / node_mass[None] - accel_column)
        displaced = displaced + TIME_STEP * speeds
    positions = rest_pos + displaced
    contacts = contact_slave.shape[0]
    capacity = 4 * contacts // domains
    owners = contact_owner[:, 0]
    owner_hits = (owners[:, None] == jnp.arange(domains, dtype=jnp.int32)[None, :]).astype(
        jnp.int32
    )
    slot_rank = jnp.sum(jnp.cumsum(owner_hits, axis=0) * owner_hits, axis=1) - 1
    slot_index = owners * capacity + slot_rank
    slave_pos = positions[:, contact_slave]
    slave_vel = speeds[:, contact_slave]
    contact_force = jnp.zeros_like(positions)
    payload = jnp.zeros((10, domains * capacity), jnp.float32).at[9].set(-1.0)
    payload = payload.at[:, slot_index].set(
        jnp.concatenate(
            [slave_pos, slave_vel, contact_normal, contact_master[None].astype(jnp.float32)], 0
        )
    )
    payload = payload.reshape(10, domains, capacity)
    arrived = lax.all_to_all(payload, "dom", split_axis=1, concat_axis=1, tiled=True)
    valid_slot = (arrived[9] >= 0.0).astype(jnp.float32)
    master_index = jnp.maximum(arrived[9], 0.0).astype(jnp.int32)
    pushed = (
        contact_push(
            arrived[0:3],
            arrived[3:6],
            positions[:, master_index],
            speeds[:, master_index],
            arrived[6:9],
        )
        * valid_slot[None]
    )
    returned = lax.all_to_all(pushed, "dom", split_axis=1, concat_axis=1, tiled=True)
    returned, pushed, master_float = (returned, pushed, arrived[9:10])
    master_index = jnp.maximum(master_float, 0.0).astype(jnp.int32)
    contact_force = contact_force.at[:, master_index.reshape(-1)].add(-pushed.reshape(3, -1))
    slave_push = returned.reshape(3, domains * capacity)[:, slot_index]
    contact_force = contact_force.at[:, contact_slave].add(slave_push)
    nodal_velocity = speeds + TIME_STEP * contact_force / node_mass[None]
    net_force = ext_force - assembled + contact_force - node_mass[None] * accel_column
    part_index = jnp.minimum(part_of_node, PARTS_SIZE)

    def segment_rows(columns_in):
        return jax.ops.segment_sum(columns_in.T, part_index, PARTS_SIZE + 1)[:PARTS_SIZE].T

    weighted = jnp.concatenate([node_mass[None], node_mass[None] * positions], 0)
    mass_moments = lax.psum(segment_rows(weighted), "dom")
    mass_total = part_mass + mass_moments[0]
    centre = (part_mass[None] * part_center + mass_moments[1:4]) / mass_total[None]
    centre_ext = jnp.concatenate([centre, jnp.zeros((3, 1), jnp.float32)], 1)
    lever_arm = positions - centre_ext[:, part_index]
    load_sums = lax.psum(
        segment_rows(jnp.concatenate([net_force, cross_product(lever_arm, net_force)], 0)), "dom"
    )
    force_sum = load_sums[0:3]
    torque = load_sums[3:6]
    part_motion = jnp.concatenate([force_sum / mass_total[None], torque / part_inertia], 0)
    return (nodal_velocity, part_motion)


def solution(mesh):
    placed = (
        P(None, "dom"),
        P(None, "dom"),
        P(None, "dom"),
        P(None, "dom"),
        P("dom"),
        P(),
        P(None, "dom"),
        P("dom"),
        P(),
        P("dom", None, None),
        P("dom"),
        P("dom", None),
        P("dom"),
        P(None, "dom"),
        P("dom"),
        P(),
        P(),
        P(),
    )
    return jax.shard_map(
        per_device, mesh=mesh, in_specs=placed, out_specs=(P(None, "dom"), P()), check_vma=False
    )
```

profile of v0, /device:TPU:1, one launch (start us, length us, event | category | flops | bytes accessed | tf_op | source)
XLA Modules:
  0.0 1388.3 jit_solution(15940693511649986868)
XLA Ops:
  0.7 1.0 fusion.22
  2.0 1.0 reshape.248
  3.1 1.1 fusion.27
  5.2 108.4 %gather_fusion = f32[32768,3]{1,0:T(8,128)} fusion(f32[3,4096]{0,1:T(8,128)S(1)} %copy.319, s32[32768]{0:T(1024)S(1)} %broadcast_clamp_fusion), kind=kCustom, calls=%fused_computation | custom fusion | bytes 917504 | tf_op jit(solution)/shard_map/gather | solution.py:36
  113.5 9.8 copy.320
  123.4 1.0 convolution_bitcast_fusion.2
  124.7 8.6 copy.325
  133.9 174.7 %scatter_custom_fusion = f32[3,4096]{0,1:T(8,128)S(1)} fusion(s32[32768]{0:T(1024)S(1)} %bitcast.185, f32[32768,3]{1,0:T(8,128)} %copy.325, f32[]{:T(128)} %constant.80.clone.1), kind=kCustom, calls=%fused_computation.40 | custom fusion | flops 98304 | bytes 49664 | tf_op jit(solution)/shard_map/scatter-add | solution.py:41
  308.6 1.7 gather_fusion.1
  311.0 1.4 collective-permute-start
  313.1 1.3 collective-permute-start.1
  315.0 2.5 collective-permute-start.2
  318.1 1.6 collective-permute-start.3
  320.4 3.3 collective-permute-start.4
  324.4 1.2 fusion.3
  331.9 7.3 scatter_fusion
  340.7 108.4 %gather_fusion.2 = f32[32768,3]{1,0:T(8,128)} fusion(f32[3,4096]{0,1:T(8,128)S(1)} %copy.333, s32[32768]{0:T(1024)S(1)} %copy-done.1), kind=kCustom, calls=%fused_computation.2 | custom fusion | bytes 917504 | tf_op jit(solution)/shard_map/gather | solution.py:36
  449.0 9.8 copy.334
  458.8 1.0 convolution_bitcast_fusion.1
  460.1 8.6 copy.338
  468.7 174.7 %scatter_custom_fusion.2 = f32[3,4096]{0,1:T(8,128)S(1)} fusion(s32[32768]{0:T(1024)} %bitcast.186, f32[32768,3]{1,0:T(8,128)} %copy.338, f32[]{:T(128)} %constant.80.clone.1), kind=kCustom, calls=%fused_computation.38 | custom fusion | flops 98304 | bytes 49664 | tf_op jit(solution)/shard_map/scatter-add | solution.py:41
  643.4 1.7 gather_fusion.3
  645.2 1.2 collective-permute-start.5
  647.1 1.4 collective-permute-start.7
  649.5 1.6 collective-permute-done.7
  651.4 1.3 collective-permute-done.9
  652.9 7.0 scatter_fusion.1
  661.2 108.4 %gather_fusion.4 = f32[32768,3]{1,0:T(8,128)} fusion(f32[3,4096]{0,1:T(8,128)S(1)} %copy.346, s32[32768]{0:T(1024)S(1)} %copy-done.1), kind=kCustom, calls=%fused_computation.4 | custom fusion | bytes 917504 | tf_op jit(solution)/shard_map/gather | solution.py:36
  769.6 9.8 copy.347
  779.4 1.0 convolution_bitcast_fusion
  780.7 8.6 copy.351
  789.3 174.7 %scatter_custom_fusion.4 = f32[3,4096]{0,1:T(8,128)S(1)} fusion(s32[32768]{0:T(1024)} %bitcast.187, f32[32768,3]{1,0:T(8,128)} %copy.351, f32[]{:T(128)} %constant.80.clone.1), kind=kCustom, calls=%fused_computation.36 | custom fusion | flops 98304 | bytes 49664 | tf_op jit(solution)/shard_map/scatter-add | solution.py:41
  964.0 1.7 gather_fusion.5
  965.7 1.8 collective-permute-start.10
  968.1 4.4 copy.436
  973.3 3.7 collective-permute-start.12
  977.1 1.8 collective-permute-start.13
  979.8 3.1 collective-permute-done.14
  983.1 7.0 scatter_fusion.2
  992.0 5.5 gather_fusion.7
  997.9 2.0 copy.361
  999.8 7.0 gather_fusion.6
  1008.4 9.8 scatter_fusion.3
  1018.2 3.0 copy.366
  1021.2 1.2 reshape.484
  1022.4 6.1 all-to-all-start
  1028.6 2.0 copy.380
  1030.6 22.7 %scatter_custom_fusion.9 = f32[401,4]{1,0:T(8,128)S(1)} fusion(s32[4096]{0:T(1024)} %get-tuple-element.61, f32[4096,4]{1,0:T(8,128)} %copy.380, f32[]{:T(128)} %constant.80.clone.1), kind=kCustom, calls=%fused_computation.65 | custom fusion | flops 16384 | bytes 6928 | tf_op jit(solution)/shard_map/scatter-add | solution.py:151
  1053.4 67.5 %psum.14 = f32[4,400]{1,0:T(4,128)S(1)} all-reduce(f32[4,400]{1,0:T(4,128)S(1)} %bitcast.196), channel_id=1, replica_groups=mesh['dom'=128] {'dom'}, use_global_device_ids=true, to_apply=%region_15.16 | all-reduce | flops 1600 | bytes 12800 | tf_op jit(solution)/shard_map/psum | solution.py:154
  1121.6 14.1 %gather_fusion.10 = f32[4096,3]{1,0:T(8,128)} fusion(f32[3,401]{0,1:T(8,128)S(1)} %concatenate.19.clone, s32[4096]{0:T(1024)S(1)} %copy-done.17), kind=kCustom, calls=%fused_computation.11 | custom fusion | bytes 114688 | tf_op jit(solution)/shard_map/gather | solution.py:158
  1135.7 2.2 copy.383
  1139.1 1.4 reduce.4
  1141.1 29.3 %gather_fusion.8 = f32[8192,3]{1,0:T(8,128)} fusion(f32[3,4096]{0,1:T(8,128)} %copy.361, s32[8192]{0:T(1024)S(1)} %broadcast_clamp_fusion.1), kind=kCustom, calls=%fused_computation.8 | custom fusion | bytes 229376 | tf_op jit(solution)/shard_map/gather | solution.py:134
  1170.4 27.7 %gather_fusion.9 = f32[8192,3]{1,0:T(8,128)} fusion(f32[3,4096]{0,1:T(8,128)S(1)} %copy.362, s32[8192]{0:T(1024)S(1)} %broadcast_clamp_fusion.1), kind=kCustom, calls=%fused_computation.9 | custom fusion | bytes 229376 | tf_op jit(solution)/shard_map/gather | solution.py:135
  1198.4 3.0 copy.371
  1201.4 3.0 copy.373
  1206.0 4.7 all-to-all-start.1
  1210.8 2.6 copy.376
  1213.5 54.0 %scatter_custom_fusion.7 = f32[3,4096]{0,1:T(8,128)S(1)} fusion(s32[8192]{0:T(1024)S(1)} %bitcast.195, f32[8192,3]{1,0:T(8,128)} %copy.376, f32[]{:T(128)} %constant.80.clone.1), kind=kCustom, calls=%fused_computation.34 | custom fusion | flops 24576 | bytes 49664 | tf_op jit(solution)/shard_map/scatter-add | solution.py:143
  1267.5 1.0 reduce.5
  1268.6 2.7 copy.377
  1271.4 24.2 %scatter_custom_fusion.8 = f32[3,4096]{0,1:T(8,128)S(1)} fusion(f32[3,4096]{0,1:T(8,128)S(1)} %scatter_custom_fusion.7, s32[2048]{0:T(1024)} %get-tuple-element.62, f32[3,8192]{0,1:T(8,128)} %bitcast.164, s32[2048]{0:T(1024)} %get-tuple-element.64), kind=kCustom, calls=%fused_computation.28 | custom fusion | flops 6144 | bytes 49152 | tf_op jit(solution)/shard_map/scatter-add | solution.py:145
  1297.7 22.5 %scatter_custom_fusion.10 = f32[401,6]{1,0:T(8,128)S(1)} fusion(s32[4096]{0:T(1024)} %get-tuple-element.61, f32[4096,6]{1,0:T(8,128)S(1)} %copy.384, f32[]{:T(128)} %constant.80.clone.1), kind=kCustom, calls=%fused_computation.67 | custom fusion | flops 24576 | bytes 10136 | tf_op jit(solution)/shard_map/scatter-add | solution.py:151
  1320.3 66.8 %psum.15 = f32[6,400]{1,0:T(8,128)S(1)} all-reduce(f32[6,400]{1,0:T(8,128)S(1)} %bitcast.193), channel_id=1, replica_groups=mesh['dom'=128] {'dom'}, use_global_device_ids=true, to_apply=%region_17.18 | all-reduce | flops 2400 | bytes 19200 | tf_op jit(solution)/shard_map/psum | solution.py:159
  (202 shorter events, 32.1 us)
Async XLA Ops:
  0.6 3.8 copy-start.2
  0.6 3.8 copy-start.6
  2.0 131.4 %copy-start.10 = (s32[32768,1]{0,1:T(1,128)}, s32[32768,1]{0,1:T(1,128)S(1)}, u32[]{:S(2)}) copy-start(s32[32768,1]{0,1:T(1,128)S(1)} %compare_select_fusion) | copy-start | bytes 393220
  5.2 118.1 %copy-start = (s32[32768]{0:T(1024)}, s32[32768]{0:T(1024)S(1)}, u32[]{:S(2)}) copy-start(s32[32768]{0:T(1024)S(1)} %broadcast_clamp_fusion) | copy-start | bytes 393220
  124.7 8.6 copy-start.31
  133.3 190.4 %copy-start.13 = (s32[2048,1]{0,1:T(1,128)S(1)}, s32[2048,1]{0,1:T(1,128)}, u32[]{:S(2)}) copy-start(s32[2048,1]{0,1:T(1,128)} %param.31) | copy-start | bytes 24580
  133.3 0.6 copy-start.11
  133.3 177.0 %copy-start.18 = (s32[1024]{0:T(1024)}, s32[1024]{0:T(1024)S(1)}, u32[]{:S(2)}) copy-start(s32[1024]{0:T(1024)S(1)} %pad_clamp_fusion) | copy-start | bytes 12292
  311.0 17.3 %collective-permute-start = (f32[3,128]{1,0:T(4,128)}, f32[3,128]{1,0:T(4,128)}, u32[]{:S(2)}, u32[]{:S(2)}) collective-permute-start(f32[3,128]{1,0:T(4,128)} %bitcast.10), channel_id=1, source_target_pairs={{0,1},{1,0},{2,3},{3,2},{4,5},{5,4},{6,7},{7,6},{8,9},{9,8},{10,11... | collective-permute-start | bytes 4616 | tf_op jit(solution)/shard_map/ppermute | solution.py:24
  313.1 15.9 %collective-permute-start.1 = (f32[3,128]{1,0:T(4,128)}, f32[3,128]{1,0:T(4,128)}, u32[]{:S(2)}, u32[]{:S(2)}) collective-permute-start(f32[3,128]{1,0:T(4,128)} %bitcast.13), channel_id=1, source_target_pairs={{0,2},{2,0},{1,3},{3,1},{4,6},{6,4},{5,7},{7,5},{8,10},{10,8},{9,1... | collective-permute-start | bytes 4616 | tf_op jit(solution)/shard_map/ppermute | solution.py:24
  315.0 14.7 %collective-permute-start.2 = (f32[3,128]{1,0:T(4,128)}, f32[3,128]{1,0:T(4,128)}, u32[]{:S(2)}, u32[]{:S(2)}) collective-permute-start(f32[3,128]{1,0:T(4,128)} %bitcast.15), channel_id=1, source_target_pairs={{0,4},{4,0},{1,5},{5,1},{2,6},{6,2},{3,7},{7,3},{8,12},{12,8},{9,1... | collective-permute-start | bytes 4616 | tf_op jit(solution)/shard_map/ppermute | solution.py:24
  318.1 12.3 collective-permute-start.3
  320.4 10.7 collective-permute-start.4
  326.9 0.7 copy-start.14
  327.0 4.9 copy-start.12
  327.4 12.4 copy-start.3
  327.4 12.4 copy-start.4
  327.4 12.4 copy-start.5
  327.4 12.4 copy-start.7
  327.4 12.4 copy-start.23
  328.3 639.2 %copy-start.15 = (s32[2048,1]{0,1:T(1,128)}, s32[2048,1]{0,1:T(1,128)S(1)}, u32[]{:S(2)}) copy-start(s32[2048,1]{0,1:T(1,128)S(1)} %compare_select_fusion.5) | copy-start | bytes 24580
  339.2 1.4 copy-start.1
  468.7 174.7 %copy-start.19 = (s32[1024]{0:T(1024)S(1)}, s32[1024]{0:T(1024)}, u32[]{:S(2)}) copy-start(s32[1024]{0:T(1024)} %copy-done.18) | copy-start | bytes 12292
  468.7 177.6 %copy-start.22 = (s32[4096]{0:T(1024)S(1)}, s32[4096]{0:T(1024)}, u32[]{:S(2)}) copy-start(s32[4096]{0:T(1024)} %param.34) | copy-start | bytes 49156
  645.2 3.6 collective-permute-start.5
  647.0 2.5 collective-permute-start.6
  647.1 4.0 collective-permute-start.7
  648.6 2.8 collective-permute-start.8
  648.7 4.0 collective-permute-start.9
  789.3 178.2 %copy-start.27 = (s32[2048]{0:T(1024)S(1)}, s32[2048]{0:T(1024)}, u32[]{:S(2)}) copy-start(s32[2048]{0:T(1024)} %param.30) | copy-start | bytes 24580
  965.7 13.5 collective-permute-start.10
  968.1 4.4 copy-start.29
  972.5 18.2 %copy-start.16 = (f32[3,4096]{1,0:T(4,128)S(1)}, f32[3,4096]{1,0:T(4,128)}, u32[]{:S(2)}) copy-start(f32[3,4096]{1,0:T(4,128)} %param.20) | copy-start | bytes 147460
  972.5 18.2 %copy-start.24 = (f32[3]{0:T(128)S(1)}, f32[3]{0:T(128)}, u32[]{:S(2)}) copy-start(f32[3]{0:T(128)} %param.25) | copy-start | bytes 40
  973.2 6.1 collective-permute-start.11
  973.3 6.0 collective-permute-start.12
  977.1 2.7 collective-permute-start.13
  978.9 4.0 collective-permute-start.14
  1022.4 98.4 %copy-start.26 = (f32[400]{0:T(512)S(1)}, f32[400]{0:T(512)}, u32[]{:S(2)}) copy-start(f32[400]{0:T(512)} %param.35) | copy-start | bytes 4804
  1022.4 98.5 %copy-start.28 = (f32[3,400]{1,0:T(4,128)S(1)}, f32[3,400]{1,0:T(4,128)}, u32[]{:S(2)}) copy-start(f32[3,400]{1,0:T(4,128)} %param.36) | copy-start | bytes 14404
  1022.4 99.2 %copy-start.17 = (s32[4096]{0:T(1024)S(1)}, s32[4096]{0:T(1024)}, u32[]{:S(2)}) copy-start(s32[4096]{0:T(1024)} %get-tuple-element.60) | copy-start | bytes 49156
  1022.4 116.1 %all-to-all-start = ((f32[128,1,640]{2,1,0:T(1,128)}), f32[128,1,640]{2,1,0:T(1,128)S(1)}, u32[]{:S(2)}, u32[]{:S(2)}) async-start(f32[128,1,640]{2,1,0:T(1,128)} %reshape.484), calls=%async_computation | async-start | bytes 655360 | tf_op jit(solution)/shard_map/all_to_all | solution.py:127
  1120.9 0.6 copy-start.20
  1206.0 61.5 %all-to-all-start.1 = ((f32[128,1,192]{2,1,0:T(1,128)}), f32[128,1,192]{2,1,0:T(1,128)S(1)}, u32[]{:S(2)}, u32[]{:S(2)}) async-start(f32[128,1,192]{2,1,0:T(1,128)} %reshape.486), calls=%async_computation.1 | async-start | bytes 262144 | tf_op jit(solution)/shard_map/all_to_all | solution.py:140
  1271.4 24.8 %copy-start.8 = (f32[3,4096]{1,0:T(4,128)S(1)}, f32[3,4096]{1,0:T(4,128)}, u32[]{:S(2)}) copy-start(f32[3,4096]{1,0:T(4,128)} %get-tuple-element.29) | copy-start | bytes 147460
  1271.4 24.8 %copy-start.25 = (f32[3]{0:T(128)S(1)}, f32[3]{0:T(128)}, u32[]{:S(2)}) copy-start(f32[3]{0:T(128)} %param.25) | copy-start | bytes 40
  1271.4 25.5 %copy-start.9 = (f32[3,4096]{1,0:T(4,128)S(1)}, f32[3,4096]{1,0:T(4,128)}, u32[]{:S(2)}) copy-start(f32[3,4096]{1,0:T(4,128)} %bitcast_subtract_fusion) | copy-start | bytes 147460
  1296.2 91.0 %copy-start.21 = (f32[400]{0:T(512)S(1)}, f32[400]{0:T(512)}, u32[]{:S(2)}) copy-start(f32[400]{0:T(512)} %copy-done.20) | copy-start | bytes 4804
  1296.2 91.0 %copy-start.30 = (f32[3,400]{1,0:T(4,128)S(1)}, f32[3,400]{1,0:T(4,128)}, u32[]{:S(2)}) copy-start(f32[3,400]{1,0:T(4,128)} %param.37) | copy-start | bytes 14404
where the time goes:
time: 1400 us; the launch traced here: 1390 us
  other arithmetic  681 us (49%)
  local copies, waits for them, and re-layouts  528 us (38%)
  blocking collectives  134 us (10%)
  starting transfers between devices  31.3 us (2%)
    scatter-add x3, other arithmetic, element_forces(): return jnp.zeros_like(nodal_field).at[:, corners.reshape(-1)].add(forces....  524 us
    gather x6, local copies, waits for them, and re-layouts, element_forces(): gathered = nodal_field[:, corners].reshape(24, blocks, 128)  354 us
    psum x1, blocking collectives, per_device(): mass_moments = lax.psum(segment_rows(weighted), 'dom')  67.5 us
    psum x1, blocking collectives, per_device(): lax.psum(segment_rows(jnp.concatenate([net_force, cross_product(lever_arm...  66.8 us
    scatter-add x1, other arithmetic, per_device(): contact_force.at[:, master_index.reshape(-1)].add(-pushed.reshape(3, -1))  54 us
    scatter-add x2, other arithmetic, segment_rows(): jax.ops.segment_sum(columns_in.T, part_index, PARTS_SIZE + 1)[:PARTS_SIZE]  45.2 us
    gather x2, local copies, waits for them, and re-layouts, per_device(): positions[:, master_index]  32.3 us
    gather x2, local copies, waits for them, and re-layouts, per_device(): speeds[:, master_index]  30.7 us
  transfers between devices with their start and end apart: 17, of which 6 were waited for; matrix products, arithmetic and copies ran while one was open for 8% of the time, Pallas kernels for 0%

commit v1 on v0

v1 whole, which is shorter than its diff:
```python
import jax
import jax.numpy as jnp
from jax import lax
from jax.experimental import pallas as pl
from jax.experimental.pallas import tpu as pltpu
from jax.sharding import PartitionSpec as P

CYCLES = 3
PARTS_SIZE = 400

TIME_STEP = 0.1
DAMP_RATIO = 0.05
PENALTY = 2.0
GAP_WIDTH = 0.5
CONTACT_DAMP = 0.2

BF = jnp.bfloat16
F32 = jnp.float32
NT = (((1,), (1,)), ((), ()))
LANES = 128
ROWS = 32
NBR = 5
TOGETHER = 4

VMEM = pl.BlockSpec(memory_space=pltpu.VMEM)
SMEM = pl.BlockSpec(memory_space=pltpu.SMEM)


def call(body, outs, in_specs, name, scratch=(), flops=0):
    return pl.pallas_call(
        body,
        out_shape=[jax.ShapeDtypeStruct(s, d) for s, d in outs],
        in_specs=in_specs,
        out_specs=[VMEM] * len(outs),
        scratch_shapes=list(scratch),
        compiler_params=pltpu.CompilerParams(vmem_limit_bytes=40 << 20),
        cost_estimate=pl.CostEstimate(flops=flops, bytes_accessed=1 << 20, transcendentals=0),
        name=name,
    )


def lanes_of(row, idx):
    return jnp.take_along_axis(row, idx, axis=1, mode="promise_in_bounds")


def gather(tab, bases, lo, hi):
    acc = [None] * len(bases)
    for h in range(ROWS):
        here = hi == h
        for c, base in enumerate(bases):
            row = jnp.broadcast_to(tab[base + h : base + h + 1, :], (8, LANES))
            val = lanes_of(row, lo)
            acc[c] = val if h == 0 else jnp.where(here, val, acc[c])
    return acc


def halves(x):
    first = x.astype(BF)
    return first, (x - first.astype(F32)).astype(BF)


def wide(x, a, n):
    row = jnp.broadcast_to(x[a : a + 1, :].astype(F32), (16, LANES)).astype(BF)
    return jnp.concatenate([row] * (n // 16), 0)


def iota_rows(n):
    return lax.broadcasted_iota(jnp.int32, (n, LANES), 0).astype(F32).astype(BF)


def place(lo, hi, vals):
    lof, hif = lo.astype(F32), hi.astype(F32)
    it = iota_rows(LANES)
    split = [halves(v) for v in vals]
    one, zero = jnp.ones((LANES, LANES), BF), jnp.zeros((LANES, LANES), BF)
    left, right = [], []
    for a in range(8):
        right.append(jnp.where(wide(lof, a, LANES) == it, one, zero))
        mask = wide(hif, a, ROWS) == it[:ROWS]
        left.append(
            jnp.concatenate(
                [
                    jnp.where(mask, wide(split[c][s], a, ROWS), zero[:ROWS])
                    for s in range(2)
                    for c in range(len(vals))
                ],
                0,
            )
        )
    return jnp.concatenate(left, 1), jnp.concatenate(right, 1)


def add_placed(acc, lo, hi, vals):
    left, right = place(lo, hi, vals)
    acc[...] += lax.dot_general(left, right, NT, preferred_element_type=F32)


def to_rows(src, dst):
    for c in range(3):
        for h in range(ROWS):
            dst[c * ROWS + h : c * ROWS + h + 1, :] = src[c : c + 1, h * LANES : (h + 1) * LANES]


def shared_split(shared):
    idx = jnp.concatenate([shared[...], jnp.zeros((8 - NBR, LANES), jnp.int32)], 0)
    return idx & 127, idx >> 7


def elements(conn, mat, tab, cols, g, acc):
    acc[...] = jnp.zeros_like(acc)
    lane = lax.broadcasted_iota(jnp.int32, (8, LANES), 1)

    def step(i, carry):
        for q in range(TOGETHER):
            b = i * TOGETHER + q
            off = pl.multiple_of(b * LANES, LANES)
            idx = (conn[:, pl.ds(off, LANES)] + lane + off) & 4095
            lo, hi = idx & 127, idx >> 7
            vals = gather(tab, (0, ROWS, 2 * ROWS), lo, hi)
            for c in range(3):
                g[q * 24 + 8 * c : q * 24 + 8 * c + 8, :] = vals[c]
            first = mat[b] * 24
            force = [jnp.zeros((8, LANES), F32)] * 3
            for j in range(24):
                col = cols.at[first + j]
                row = jnp.broadcast_to(g[q * 24 + j : q * 24 + j + 1, :], (8, LANES))
                force = [force[c] + col[8 * c : 8 * c + 8, :] * row for c in range(3)]
            add_placed(acc, lo, hi, force)
        return carry

    lax.fori_loop(0, ROWS // TOGETHER, step, 0)


def finish_internal(acc, internal, shared, own):
    internal[...] = acc[0:96, :] + acc[96:192, :]
    lo, hi = shared_split(shared)
    vals = gather(internal, (0, ROWS, 2 * ROWS), lo, hi)
    for b in range(NBR):
        for c in range(3):
            own[b][c : c + 1, :] = vals[c][b : b + 1, :]


def first_kernel(disp, vel, force, conn, mat, stiff, shared, *rest):
    u, v, f, internal, inv, cols = rest[:6]
    own = rest[6:11]
    tab, g, acc, small = rest[11:]
    to_rows(disp, u)
    to_rows(vel, v)
    to_rows(force, f)
    tab[...] = u[...] + DAMP_RATIO * v[...]
    for m in range(8):
        for j in range(24):
            cols[m * 24 + j] = jnp.broadcast_to(stiff[m * 24 : (m + 1) * 24, j : j + 1], (24, LANES))
    lo, hi = shared_split(shared)
    lane = lax.broadcasted_iota(jnp.int32, (8, LANES), 1).astype(F32)
    row = lax.broadcasted_iota(jnp.int32, (8, LANES), 0).astype(F32)
    small[...] = jnp.zeros_like(small)
    held = row < NBR
    add_placed(small, lo, hi, [jnp.where(held, lane, 0.0), jnp.where(held, row + 1.0, 0.0)])
    inv[...] = (small[0:64, :] + small[64:128, :]).astype(jnp.int32)
    elements(conn, mat, tab, cols, g, acc)
    finish_internal(acc, internal, shared, own)


def update(u, v, internal, inv, f, mass, accel, recv, c, r):
    at = slice(c * ROWS + r, c * ROWS + r + 8)
    slot, which = inv[r : r + 8, :], inv[ROWS + r : ROWS + r + 8, :]
    total = internal[at, :]
    for b in range(NBR):
        row = jnp.broadcast_to(recv[b][c : c + 1, :], (8, LANES))
        total = total + jnp.where(which == b + 1, lanes_of(row, slot), 0.0)
    speed = v[at, :] + TIME_STEP * ((f[at, :] - total) / mass[r : r + 8, :] - accel[c])
    return at, u[at, :] + TIME_STEP * speed, speed, total


def next_kernel(u, v, internal, inv, f, mass, accel, conn, mat, cols, shared, *rest):
    recv = rest[:5]
    u2, v2, internal2 = rest[5:8]
    own = rest[8:13]
    tab, g, acc = rest[13:]
    for c in range(3):
        for r in range(0, ROWS, 8):
            at, disp, speed, _ = update(u, v, internal, inv, f, mass, accel, recv, c, r)
            u2[at, :] = disp
            v2[at, :] = speed
            tab[at, :] = disp + DAMP_RATIO * speed
    elements(conn, mat, tab, cols, g, acc)
    finish_internal(acc, internal2, shared, own)


def slot_kernel(slave, owner, master, normal, send, sidx, acc):
    acc[...] = jnp.zeros_like(acc)
    down = lax.broadcasted_iota(jnp.int32, (LANES, LANES), 0)
    across = lax.broadcasted_iota(jnp.int32, (LANES, LANES), 1)
    before = jnp.where(down < across, 1.0, 0.0).astype(BF)
    carry = jnp.zeros((LANES, 1), F32)
    for t in range(16):
        hit = jnp.where(jnp.broadcast_to(owner[t : t + 1, :], (LANES, LANES)) == down, 1.0, 0.0)
        hitb = hit.astype(BF)
        count = jnp.dot(hitb, before, preferred_element_type=F32) + carry
        rank = jnp.sum(hit * count, axis=0, keepdims=True)
        carry = carry + jnp.sum(hit, axis=1, keepdims=True)
        mine = jnp.broadcast_to(rank, (64, LANES)) == down[:64].astype(F32)
        vals = [normal[c : c + 1, t * LANES : (t + 1) * LANES] for c in range(3)]
        vals += [master[t : t + 1, :].astype(F32), slave[t : t + 1, :].astype(F32)]
        left = [jnp.broadcast_to(x, (64, LANES)) for x in vals]
        for s in range(3):
            piece = [jnp.where(mine, x, 0.0).astype(BF) for x in left]
            left = [x - x.astype(BF).astype(F32) for x in left]
            acc[:, 0:320] += lax.dot_general(
                hitb, jnp.concatenate(piece, 0), NT, preferred_element_type=F32
            )
    send[...] = acc[:, 0:256]
    sidx[...] = acc[:, 256:384]


def dots_kernel(u, v, internal, inv, f, mass, accel, pos, send, sidx, got, *rest):
    recv = rest[:5]
    x2, v2, net, dots, idx, nrm = rest[5:11]
    tab = rest[11]
    to_rows(pos, x2)
    for c in range(3):
        for r in range(0, ROWS, 8):
            at, disp, speed, total = update(u, v, internal, inv, f, mass, accel, recv, c, r)
            place_now = x2[at, :] + disp
            x2[at, :] = place_now
            v2[at, :] = speed
            net[at, :] = f[at, :] - total - mass[r : r + 8, :] * accel[c]
            tab[at, :] = place_now
            tab[c * ROWS + 96 + r : c * ROWS + 96 + r + 8, :] = speed
    left = lax.broadcasted_iota(jnp.int32, (LANES, LANES), 1) < 64
    own0, own1 = send[:, 0:128], send[:, 128:256]
    got0, got1 = got[:, 0:128], got[:, 128:256]
    nrm[0] = jnp.where(left, own0, pltpu.roll(got0, 64, 1))
    nrm[1] = jnp.where(left, pltpu.roll(own0, 64, 1), got0)
    nrm[2] = jnp.where(left, own1, pltpu.roll(got1, 64, 1))
    idx[...] = jnp.where(left, sidx[...], got1).astype(jnp.int32)

    def step(i, carry):
        for q in range(2):
            off = pl.multiple_of(i * 16 + q * 8, 8)
            here = idx[pl.ds(off, 8), :]
            vals = gather(tab, tuple(range(0, 192, ROWS)), here & 127, here >> 7)
            w = [nrm[c, pl.ds(off, 8), :] for c in range(3)]
            dots[pl.ds(off, 8), 0:128] = vals[0] * w[0] + vals[1] * w[1] + vals[2] * w[2]
            dots[pl.ds(off, 8), 128:256] = vals[3] * w[0] + vals[4] * w[1] + vals[5] * w[2]
        return carry

    lax.fori_loop(0, 8, step, 0)


def part_sums(part, vals, acc):
    it = iota_rows(LANES)
    it8 = (lax.broadcasted_iota(jnp.int32, (16, LANES), 0) & 7).astype(F32).astype(BF)
    one, zero = jnp.ones((LANES, LANES), BF), jnp.zeros((LANES, LANES), BF)
    for r in range(0, ROWS, 8):
        here = part[r : r + 8, :]
        lof, hif = (here & 127).astype(F32), (here >> 7).astype(F32)
        val = vals(r)
        first = [x.astype(BF).astype(F32) for x in val]
        split = (first, [x - y for x, y in zip(val, first)])
        left, right = [], []
        for a in range(8):
            right.append(jnp.where(wide(lof, a, LANES) == it, one, zero))
            mask = wide(hif, a, 16) == it8
            rows = []
            for s in range(2):
                for k in range(0, len(val), 2):
                    two = [jnp.broadcast_to(split[s][k + d][a : a + 1, :], (8, LANES)) for d in range(2)]
                    rows.append(jnp.where(mask, jnp.concatenate(two, 0).astype(BF), zero[:16]))
            left.append(jnp.concatenate(rows, 0))
        acc[...] += lax.dot_general(
            jnp.concatenate(left, 1), jnp.concatenate(right, 1), NT, preferred_element_type=F32
        )


def contact_kernel(dots, got, idx, nrm, x, v, net, mass, part, nodal, sums, acc, tot, acc2):
    acc[...] = jnp.zeros_like(acc)
    acc2[...] = jnp.zeros_like(acc2)
    sign = jnp.where(lax.broadcasted_iota(jnp.int32, (8, LANES), 1) < 64, 1.0, -1.0)

    def step(i, carry):
        for q in range(4):
            off = pl.multiple_of(i * 32 + q * 8, 8)
            at = pl.ds(off, 8)
            gap = sign * (dots[at, 0:128] - pltpu.roll(got[at, 0:128], 64, 1))
            closing = sign * (dots[at, 128:256] - pltpu.roll(got[at, 128:256], 64, 1))
            z = -gap / GAP_WIDTH
            soft = jnp.maximum(z, 0.0) + jnp.log1p(jnp.exp(-jnp.abs(z)))
            push = sign * (PENALTY * GAP_WIDTH * soft - CONTACT_DAMP * closing)
            here = idx[at, :]
            add_placed(acc, here & 127, here >> 7, [push * nrm[c, at, :] for c in range(3)])
        return carry

    lax.fori_loop(0, 4, step, 0)
    contact = acc[0:96, :] + acc[96:192, :]
    tot[...] = net[...] + contact
    for c in range(3):
        speed = v[c * ROWS : (c + 1) * ROWS, :] + TIME_STEP * contact[c * ROWS : (c + 1) * ROWS, :] / mass[...]
        for h in range(ROWS):
            nodal[c : c + 1, h * LANES : (h + 1) * LANES] = speed[h : h + 1, :]

    def vals(r):
        m = mass[r : r + 8, :]
        p = [x[c * ROWS + r : c * ROWS + r + 8, :] for c in range(3)]
        n = [tot[c * ROWS + r : c * ROWS + r + 8, :] for c in range(3)]
        return [
            m,
            *[m * y for y in p],
            *n,
            p[1] * n[2] - p[2] * n[1],
            p[2] * n[0] - p[0] * n[2],
            p[0] * n[1] - p[1] * n[0],
        ]

    part_sums(part, vals, acc2)
    all_sums = acc2[0:80, :] + acc2[80:160, :]
    sums[...] = jnp.concatenate([all_sums, jnp.zeros((48, LANES), F32)], 0).T


def total_kernel(got, out):
    out[...] = jnp.broadcast_to(jnp.sum(got[...], axis=0, keepdims=True), (LANES, LANES))


def motion_kernel(got, pmass, pcenter, pinertia, out, pm, pc, pi):
    spans = [(h, min(LANES, PARTS_SIZE - h * LANES)) for h in range(4)]
    for ref in (pm, pc, pi):
        ref[...] = jnp.ones_like(ref)
    for h, n in spans:
        lanes = slice(h * LANES, h * LANES + n)
        pm[h : h + 1, 0:n] = pmass[0:1, lanes]
        for c in range(3):
            pc[8 * c + h : 8 * c + h + 1, 0:n] = pcenter[c : c + 1, lanes]
            pi[8 * c + h : 8 * c + h + 1, 0:n] = pinertia[c : c + 1, lanes]
    by = got[...].T
    val = [by[8 * k : 8 * k + 8, :] for k in range(10)]
    mass = pm[...] + val[0]
    centre = [(pm[...] * pc[8 * c : 8 * c + 8, :] + val[1 + c]) / mass for c in range(3)]
    force, turn = val[4:7], val[7:10]
    rows = [y / mass for y in force]
    for c in range(3):
        a, b = (c + 1) % 3, (c + 2) % 3
        moment = turn[c] - (centre[a] * force[b] - centre[b] * force[a])
        rows.append(moment / pi[8 * c : 8 * c + 8, :])
    for r, row in enumerate(rows):
        for h, n in spans:
            out[r : r + 1, h * LANES : h * LANES + n] = row[h : h + 1, 0:n]


def partner(block, apart):
    count = lax.axis_size("dom")
    return lax.ppermute(block, "dom", [(i, i ^ (1 << apart)) for i in range(count)])


def swap(block):
    return lax.all_to_all(block, "dom", 0, 0, tiled=True)


def per_device(
    rest_pos,
    displacement,
    velocity,
    ext_force,
    node_mass,
    body_accel,
    connectivity,
    elem_material,
    stiffness,
    shared_nodes,
    contact_slave,
    contact_owner,
    contact_master,
    contact_normal,
    part_of_node,
    part_mass,
    part_center,
    part_inertia,
):
    mass = node_mass.reshape(ROWS, LANES)
    shared = shared_nodes.reshape(NBR, LANES)
    state = ((96, LANES), F32)
    own = [((3, LANES), F32)] * NBR
    square = ((LANES, LANES), F32)
    double = ((LANES, 2 * LANES), F32)

    send, sidx = call(
        slot_kernel,
        [double, square],
        [VMEM] * 4,
        "contact_slots",
        [pltpu.VMEM((LANES, 384), F32)],
    )(
        contact_slave.reshape(16, LANES),
        contact_owner.reshape(16, LANES),
        contact_master.reshape(16, LANES),
        contact_normal,
    )
    got = swap(send)

    work = [
        pltpu.VMEM((96, LANES), F32),
        pltpu.VMEM((24 * TOGETHER, LANES), F32),
        pltpu.VMEM((192, LANES), F32),
    ]
    u, v, f, internal, inv, cols, *mine = call(
        first_kernel,
        [state, state, state, state, ((64, LANES), jnp.int32), ((192, 24, LANES), F32), *own],
        [VMEM] * 4 + [SMEM] + [VMEM] * 2,
        "first_cycle",
        [*work, pltpu.VMEM((128, LANES), F32)],
    )(displacement, velocity, ext_force, connectivity, elem_material, stiffness.reshape(192, 24), shared)
    recv = [partner(mine[b], b) for b in range(NBR)]
    for _ in range(CYCLES - 1):
        u, v, internal, *mine = call(
            next_kernel,
            [state, state, state, *own],
            [VMEM] * 6 + [SMEM, VMEM, SMEM] + [VMEM] * 7,
            "next_cycle",
            work,
        )(u, v, internal, inv, f, mass, body_accel, connectivity, elem_material, cols, shared, *recv)
        recv = [partner(mine[b], b) for b in range(NBR)]

    x, v, net, dots, idx, nrm = call(
        dots_kernel,
        [state, state, state, double, ((LANES, LANES), jnp.int32), ((3, LANES, LANES), F32)],
        [VMEM] * 6 + [SMEM] + [VMEM] * 9,
        "contact_dots",
        [pltpu.VMEM((192, LANES), F32)],
    )(u, v, internal, inv, f, mass, body_accel, rest_pos, send, sidx, got, *recv)
    other = swap(dots)
    nodal_velocity, sums = call(
        contact_kernel,
        [((3, 4096), F32), square],
        [VMEM] * 9,
        "contact_forces",
        [pltpu.VMEM((192, LANES), F32), pltpu.VMEM((96, LANES), F32), pltpu.VMEM((160, LANES), F32)],
    )(dots, other, idx, nrm, x, v, net, mass, part_of_node.reshape(ROWS, LANES))
    (total,) = call(total_kernel, [square], [VMEM], "part_totals")(swap(sums))
    (motion,) = call(
        motion_kernel,
        [((6, PARTS_SIZE), F32)],
        [VMEM] * 4,
        "part_motion",
        [pltpu.VMEM((8, LANES), F32), pltpu.VMEM((24, LANES), F32), pltpu.VMEM((24, LANES), F32)],
    )(swap(total), part_mass.reshape(1, PARTS_SIZE), part_center, part_inertia)
    return nodal_velocity, motion


def solution(mesh):
    placed = (
        P(None, "dom"),
        P(None, "dom"),
        P(None, "dom"),
        P(None, "dom"),
        P("dom"),
        P(),
        P(None, "dom"),
        P("dom"),
        P(),
        P("dom", None, None),
        P("dom"),
        P("dom", None),
        P("dom"),
        P(None, "dom"),
        P("dom"),
        P(),
        P(),
        P(),
    )
    return jax.shard_map(
        per_device, mesh=mesh, in_specs=placed, out_specs=(P(None, "dom"), P()), check_vma=False
    )
```

time: 1400 us -> 141 us (0.10)
  other arithmetic: 681 us -> 0 us
  local copies, waits for them, and re-layouts: 528 us -> 11.7 us
  blocking collectives: 134 us -> 46.2 us
  Pallas kernels: 0 us -> 42.2 us
    scatter-add x10 -> x0, other arithmetic: 669 us -> none  [the longest x3 524 us: element_forces(): return jnp.zeros_like(nodal_field).at[:, corners.reshape(-1)].add(forces....]
    gather x19 -> x0, local copies, waits for them, and re-layouts: 452 us -> none  [the longest x6 354 us: element_forces(): gathered = nodal_field[:, corners].reshape(24, blocks, 128)]
    psum x2 -> x0, blocking collectives: 134 us -> none  [the longest x1 67.5 us: per_device(): mass_moments = lax.psum(segment_rows(weighted), 'dom')]
    all_to_all x0 -> x3, blocking collectives: none -> 46.2 us  [swap(): return lax.all_to_all(block, 'dom', 0, 0, tiled=True)]
    pallas_call x0 -> x8, Pallas kernels: none -> 42.2 us  [the longest x2 18.9 us: per_device(): call(next_kernel, [state, state, state, *own], [VMEM] * 6 + [SMEM, VMEM,...]
    reshape x12 -> x0, local copies, waits for them, and re-layouts: 31 us -> none  [the longest x6 26.3 us: element_forces(): forces.reshape(3, 8 * corners.shape[1])]
  transfers between devices with their start and end apart: 17 -> 16, of which waited for: 6 -> 3; matrix products, arithmetic and copies ran while one was open for 8% -> 0% of each run, Pallas kernels for 0% -> 21%
where the time goes in v1:
time: 141 us
  blocking collectives  46.2 us (33%)
  Pallas kernels  42.2 us (30%)
  starting transfers between devices  36.4 us (26%)
  local copies, waits for them, and re-layouts  11.7 us (8%)
  waiting for transfers between devices  3.22 us (2%)
    all_to_all x3, blocking collectives, swap(): return lax.all_to_all(block, 'dom', 0, 0, tiled=True)  46.2 us
    ppermute x15, starting transfers between devices, partner(): lax.ppermute(block, 'dom', [(i, i ^ 1 << apart) for i in range(count)])  25 us
    pallas_call x2, Pallas kernels, per_device(): call(next_kernel, [state, state, state, *own], [VMEM] * 6 + [SMEM, VMEM,...  18.9 us
    all_to_all x1, starting transfers between devices, swap(): return lax.all_to_all(block, 'dom', 0, 0, tiled=True)  11.4 us
    unnamed x43, local copies, waits for them, and re-layouts  10.8 us
    pallas_call x1, Pallas kernels, per_device(): call(first_kernel, [state, state, state, state, ((64, LANES), jnp.int32),...  10.3 us
    pallas_call x1, Pallas kernels, per_device(): call(dots_kernel, [state, state, state, double, ((LANES, LANES), jnp.int3...  4.63 us
    pallas_call x1, Pallas kernels, per_device(): call(slot_kernel, [double, square], [VMEM] * 4, 'contact_slots', [pltpu.V...  4.2 us
  transfers between devices with their start and end apart: 16, of which 3 were waited for; matrix products, arithmetic and copies ran while one was open for 0% of the time, Pallas kernels for 21%

profile of v1, /device:TPU:1, one launch (start us, length us, event | category | flops | bytes accessed | tf_op | source)
XLA Modules:
  0.0 140.6 jit_solution(3538529554476886850)
XLA Ops:
  0.6 0.0 copy-start.9
  0.6 0.7 copy-done.9
  1.4 0.7 copy-done.11
  2.1 0.7 copy-done.12
  2.8 0.7 copy-done.13
  3.5 4.2 %contact_slots.1 = (f32[128,256]{1,0:T(8,128)S(1)}, f32[128,128]{1,0:T(8,128)S(1)}) custom-call(s32[16,128]{1,0:T(8,128)S(1)} %bitcast.43, s32[16,128]{1,0:T(8,128)S(1)} %bitcast.44, s32[16,128]{1,0:T(8,128)S(1)} %bitcast.45, f32[3,2048]{1,0:T(4,128)S(1)} %copy-done.9), custom_call_target="tpu_custom_call" | custom-call | bytes 1048576 | tf_op jit(solution)/shard_map/contact_slots/pallas_call | solution.py:386
  7.7 0.8 copy.20
  8.5 11.4 %all-to-all-start = ((f32[128,1,256]{2,1,0:T(1,128)}), f32[128,1,256]{2,1,0:T(1,128)S(1)}, u32[]{:S(2)}, u32[]{:S(2)}) async-start(f32[128,1,256]{2,1,0:T(1,128)} %copy.20), calls=%async_computation | async-start | bytes 262144 | tf_op jit(solution)/shard_map/all_to_all | solution.py:356
  19.9 0.7 copy.32
  20.6 0.9 copy-done
  21.5 0.9 copy-done.4
  22.4 0.8 copy-done.6
  23.2 0.8 copy-done.7
  24.1 0.8 copy-done.8
  24.9 0.7 copy-done.16
  25.6 10.3 %first_cycle.1 = (f32[96,128]{1,0:T(8,128)S(1)}, f32[96,128]{1,0:T(8,128)S(1)}, f32[96,128]{1,0:T(8,128)S(1)}, f32[96,128]{1,0:T(8,128)S(1)}, s32[64,128]{1,0:T(...) custom-call(f32[3,4096]{1,0:T(4,128)S(1)} %copy-done.6, ...), custom_call_target="tpu_custom_call" | custom-call | bytes 1048576 | tf_op jit(solution)/shard_map/first_cycle/pallas_call | solution.py:405
  35.9 1.2 collective-permute-start
  37.0 0.7 collective-permute-start.1
  37.7 2.4 %collective-permute-start.2 = (f32[3,128]{1,0:T(4,128)S(1)}, f32[3,128]{1,0:T(4,128)S(1)}, u32[]{:S(2)}, u32[]{:S(2)}) collective-permute-start(f32[3,128]{1,0:T(4,128)S(1)} %get-tuple-element.47), channel_id=1, source_target_pairs={{0,4},{1,5},{2,6},{3,7},{4,0},{5,1},{6,2},{7,3},{8,12},{9,13},{10,... | collective-permute-start | bytes 4616 | tf_op jit(solution)/shard_map/ppermute | solution.py:352
  40.1 1.4 collective-permute-start.3
  41.5 2.9 %collective-permute-start.4 = (f32[3,128]{1,0:T(4,128)S(1)}, f32[3,128]{1,0:T(4,128)S(1)}, u32[]{:S(2)}, u32[]{:S(2)}) collective-permute-start(f32[3,128]{1,0:T(4,128)S(1)} %get-tuple-element.49), channel_id=1, source_target_pairs={{0,16},{1,17},{2,18},{3,19},{4,20},{5,21},{6,22},{7,23},{8,24},{9,... | collective-permute-start | bytes 4616 | tf_op jit(solution)/shard_map/ppermute | solution.py:352
  44.4 0.0 collective-permute-done.rest_0_
  44.4 0.0 collective-permute-done.1.rest_1_
  44.4 0.0 collective-permute-done.2.rest_2_
  44.4 0.0 collective-permute-done.3.rest_3_
  44.4 1.0 collective-permute-done.4.rest_4_
  45.4 0.9 copy-done.1
  46.3 0.7 copy-done.2
  47.0 0.7 copy-done.17
  47.7 9.5 %next_cycle.2 = (f32[96,128]{1,0:T(8,128)S(1)}, f32[96,128]{1,0:T(8,128)S(1)}, f32[96,128]{1,0:T(8,128)S(1)}, f32[3,128]{1,0:T(4,128)S(1)}, f32[3,128]{1,0:T(4,1...) custom-call(f32[96,128]{1,0:T(8,128)S(1)} %get-tuple-element.39.u, ...), custom_call_target="tpu_custom_call" | custom-call | bytes 1048576 | tf_op jit(solution)/shard_map/next_cycle/pallas_call | solution.py:414
  57.1 0.0 copy-start.10
  57.1 2.2 %collective-permute-start.5 = (f32[3,128]{1,0:T(4,128)S(1)}, f32[3,128]{1,0:T(4,128)S(1)}, u32[]{:S(2)}, u32[]{:S(2)}) collective-permute-start(f32[3,128]{1,0:T(4,128)S(1)} %get-tuple-element.53), channel_id=1, source_target_pairs={{0,1},{1,0},{2,3},{3,2},{4,5},{5,4},{6,7},{7,6},{8,9},{9,8},{10,11... | collective-permute-start | bytes 4616 | tf_op jit(solution)/shard_map/ppermute | solution.py:352
  59.4 0.0 collective-permute-start.6
  59.4 1.4 %collective-permute-start.7 = (f32[3,128]{1,0:T(4,128)S(1)}, f32[3,128]{1,0:T(4,128)S(1)}, u32[]{:S(2)}, u32[]{:S(2)}) collective-permute-start(f32[3,128]{1,0:T(4,128)S(1)} %get-tuple-element.55), channel_id=1, source_target_pairs={{0,4},{1,5},{2,6},{3,7},{4,0},{5,1},{6,2},{7,3},{8,12},{9,13},{10,... | collective-permute-start | bytes 4616 | tf_op jit(solution)/shard_map/ppermute | solution.py:352
  60.8 0.6 collective-permute-start.8
  61.4 2.6 %collective-permute-start.9 = (f32[3,128]{1,0:T(4,128)S(1)}, f32[3,128]{1,0:T(4,128)S(1)}, u32[]{:S(2)}, u32[]{:S(2)}) collective-permute-start(f32[3,128]{1,0:T(4,128)S(1)} %get-tuple-element.57), channel_id=1, source_target_pairs={{0,16},{1,17},{2,18},{3,19},{4,20},{5,21},{6,22},{7,23},{8,24},{9,... | collective-permute-start | bytes 4616 | tf_op jit(solution)/shard_map/ppermute | solution.py:352
  64.1 0.0 collective-permute-done.5.rest_0_
  64.1 0.0 collective-permute-done.6.rest_1_
  64.1 0.0 collective-permute-done.7.rest_2_
  64.1 0.0 collective-permute-done.8.rest_3_
  64.1 1.3 collective-permute-done.9.rest_4_
  65.4 9.5 %next_cycle.3 = (f32[96,128]{1,0:T(8,128)S(1)}, f32[96,128]{1,0:T(8,128)S(1)}, f32[96,128]{1,0:T(8,128)S(1)}, f32[3,128]{1,0:T(4,128)S(1)}, f32[3,128]{1,0:T(4,1...) custom-call(f32[96,128]{1,0:T(8,128)S(1)} %get-tuple-element.50.u, ...), custom_call_target="tpu_custom_call" | custom-call | bytes 1048576 | tf_op jit(solution)/shard_map/next_cycle/pallas_call | solution.py:414
  74.8 2.1 %collective-permute-start.10 = (f32[3,128]{1,0:T(4,128)S(1)}, f32[3,128]{1,0:T(4,128)S(1)}, u32[]{:S(2)}, u32[]{:S(2)}) collective-permute-start(f32[3,128]{1,0:T(4,128)S(1)} %get-tuple-element.63), channel_id=1, source_target_pairs={{0,1},{1,0},{2,3},{3,2},{4,5},{5,4},{6,7},{7,6},{8,9},{9,8},{10,11... | collective-permute-start | bytes 4616 | tf_op jit(solution)/shard_map/ppermute | solution.py:352
  77.0 0.0 collective-permute-start.11
  77.0 3.1 %collective-permute-start.12 = (f32[3,128]{1,0:T(4,128)S(1)}, f32[3,128]{1,0:T(4,128)S(1)}, u32[]{:S(2)}, u32[]{:S(2)}) collective-permute-start(f32[3,128]{1,0:T(4,128)S(1)} %get-tuple-element.65), channel_id=1, source_target_pairs={{0,4},{1,5},{2,6},{3,7},{4,0},{5,1},{6,2},{7,3},{8,12},{9,13},{10,... | collective-permute-start | bytes 4616 | tf_op jit(solution)/shard_map/ppermute | solution.py:352
  80.1 1.3 collective-permute-start.13
  81.5 2.9 %collective-permute-start.14 = (f32[3,128]{1,0:T(4,128)S(1)}, f32[3,128]{1,0:T(4,128)S(1)}, u32[]{:S(2)}, u32[]{:S(2)}) collective-permute-start(f32[3,128]{1,0:T(4,128)S(1)} %get-tuple-element.67), channel_id=1, source_target_pairs={{0,16},{1,17},{2,18},{3,19},{4,20},{5,21},{6,22},{7,23},{8,24},{9,... | collective-permute-start | bytes 4616 | tf_op jit(solution)/shard_map/ppermute | solution.py:352
  84.4 0.0 all-to-all-done
  84.4 0.0 collective-permute-done.10.rest_0_
  84.4 0.0 collective-permute-done.11.rest_1_
  84.4 0.0 collective-permute-done.12.rest_2_
  84.5 0.0 collective-permute-done.13.rest_3_
  84.5 0.9 collective-permute-done.14.rest_4_
  85.4 0.0 copy-done.5
  85.4 4.6 %contact_dots.1 = (f32[96,128]{1,0:T(8,128)S(1)}, f32[96,128]{1,0:T(8,128)S(1)}, f32[96,128]{1,0:T(8,128)S(1)}, f32[128,256]{1,0:T(8,128)S(1)}, s32[128,128]{1,0:T(8,128)S(1)}, /*index=5*/f32[3,128,128]{2,1,0:T(8,128)S(1)}) custom-call(f32[96,128]{1,0:T(8,128)S(1)} %get-tuple-element.58.u, f32[96,128]{1,0:T(8,128)S(1)} %get-tuple-element.59.v, ...), custom_call_target="tpu_custom_call" | custom-call | bytes 1048576 | tf_op jit(solution)/shard_map/contact_dots/pallas_call | solution.py:423
  90.1 0.1 copy.21
  90.2 18.6 %all_to_all.44 = f32[128,1,256]{2,1,0:T(1,128)S(1)} all-to-all(f32[128,1,256]{2,1,0:T(1,128)S(1)} %copy.21), channel_id=1, replica_groups=mesh['dom'=128] {'dom'}, dimensions={0} | all-to-all | bytes 262144 | tf_op jit(solution)/shard_map/all_to_all | solution.py:356
  108.8 0.0 copy-done.10
  108.8 3.5 %contact_forces.1 = (f32[3,4096]{1,0:T(4,128)}, f32[128,128]{1,0:T(8,128)S(1)}) custom-call(f32[128,256]{1,0:T(8,128)S(1)} %get-tuple-element.68.dots, f32[128,256]{1,0:T(8,128)S(1)} %bitcast.29, s32[128,128]{1,0:T(8,128)S(1)} %get-tuple-element.69.idx, f32[3,128,128]{2,1,0:T(8,128)S(1)} %get-tuple-element.70.nrm, f32[96,128]{1,0:T(8,128)S(1)} %get-tuple-element.71.x, ...), custom_call_target="tpu_custom_call" | custom-call | bytes 1048576 | tf_op jit(solution)/shard_map/contact_forces/pallas_call | solution.py:431
  112.2 13.7 %all_to_all.45 = f32[128,1,128]{2,1,0:T(1,128)S(1)} all-to-all(f32[128,1,128]{2,1,0:T(1,128)S(1)} %bitcast.41), channel_id=1, replica_groups=mesh['dom'=128] {'dom'}, dimensions={0} | all-to-all | bytes 131072 | tf_op jit(solution)/shard_map/all_to_all | solution.py:356
  126.0 13.9 %all_to_all.46 = f32[128,1,128]{2,1,0:T(1,128)S(1)} all-to-all(f32[128,1,128]{2,1,0:T(1,128)S(1)} %bitcast.35), channel_id=1, replica_groups=mesh['dom'=128] {'dom'}, dimensions={0} | all-to-all | bytes 131072 | tf_op jit(solution)/shard_map/all_to_all | solution.py:356
  139.9 0.0 copy-done.14
  139.9 0.0 copy-done.19
  139.9 0.7 part_motion.1
  (24 shorter events, 0.1 us)
Async XLA Ops:
  0.6 0.8 copy-start.9
  1.4 0.7 copy-start.11
  2.1 0.7 copy-start.12
  2.8 0.7 copy-start.13
  8.5 75.9 %all-to-all-start = ((f32[128,1,256]{2,1,0:T(1,128)}), f32[128,1,256]{2,1,0:T(1,128)S(1)}, u32[]{:S(2)}, u32[]{:S(2)}) async-start(f32[128,1,256]{2,1,0:T(1,128)} %copy.20), calls=%async_computation | async-start | bytes 262144 | tf_op jit(solution)/shard_map/all_to_all | solution.py:356
  20.6 0.9 copy-start
  21.5 0.9 copy-start.4
  22.4 0.8 copy-start.6
  23.2 0.8 copy-start.7
  24.1 0.8 copy-start.8
  24.9 0.7 copy-start.16
  35.9 8.5 %collective-permute-start = (f32[3,128]{1,0:T(4,128)S(1)}, f32[3,128]{1,0:T(4,128)S(1)}, u32[]{:S(2)}, u32[]{:S(2)}) collective-permute-start(f32[3,128]{1,0:T(4,128)S(1)} %get-tuple-element.45), channel_id=1, source_target_pairs={{0,1},{1,0},{2,3},{3,2},{4,5},{5,4},{6,7},{7,6},{8,9},{9,8},{10,11... | collective-permute-start | bytes 4616 | tf_op jit(solution)/shard_map/ppermute | solution.py:352
  37.0 7.4 %collective-permute-start.1 = (f32[3,128]{1,0:T(4,128)S(1)}, f32[3,128]{1,0:T(4,128)S(1)}, u32[]{:S(2)}, u32[]{:S(2)}) collective-permute-start(f32[3,128]{1,0:T(4,128)S(1)} %get-tuple-element.46), channel_id=1, source_target_pairs={{0,2},{1,3},{2,0},{3,1},{4,6},{5,7},{6,4},{7,5},{8,10},{9,11},{10,... | collective-permute-start | bytes 4616 | tf_op jit(solution)/shard_map/ppermute | solution.py:352
  37.7 6.7 %collective-permute-start.2 = (f32[3,128]{1,0:T(4,128)S(1)}, f32[3,128]{1,0:T(4,128)S(1)}, u32[]{:S(2)}, u32[]{:S(2)}) collective-permute-start(f32[3,128]{1,0:T(4,128)S(1)} %get-tuple-element.47), channel_id=1, source_target_pairs={{0,4},{1,5},{2,6},{3,7},{4,0},{5,1},{6,2},{7,3},{8,12},{9,13},{10,... | collective-permute-start | bytes 4616 | tf_op jit(solution)/shard_map/ppermute | solution.py:352
  40.1 4.3 %collective-permute-start.3 = (f32[3,128]{1,0:T(4,128)S(1)}, f32[3,128]{1,0:T(4,128)S(1)}, u32[]{:S(2)}, u32[]{:S(2)}) collective-permute-start(f32[3,128]{1,0:T(4,128)S(1)} %get-tuple-element.48), channel_id=1, source_target_pairs={{0,8},{1,9},{2,10},{3,11},{4,12},{5,13},{6,14},{7,15},{8,0},{9,1},... | collective-permute-start | bytes 4616 | tf_op jit(solution)/shard_map/ppermute | solution.py:352
  41.5 3.9 %collective-permute-start.4 = (f32[3,128]{1,0:T(4,128)S(1)}, f32[3,128]{1,0:T(4,128)S(1)}, u32[]{:S(2)}, u32[]{:S(2)}) collective-permute-start(f32[3,128]{1,0:T(4,128)S(1)} %get-tuple-element.49), channel_id=1, source_target_pairs={{0,16},{1,17},{2,18},{3,19},{4,20},{5,21},{6,22},{7,23},{8,24},{9,... | collective-permute-start | bytes 4616 | tf_op jit(solution)/shard_map/ppermute | solution.py:352
  45.4 0.9 copy-start.1
  46.3 0.7 copy-start.2
  47.0 0.7 copy-start.17
  47.7 37.7 %copy-start.3 = (f32[4096]{0:T(1024)S(1)}, f32[4096]{0:T(1024)}, u32[]{:S(2)}) copy-start(f32[4096]{0:T(1024)} %param.22) | copy-start | bytes 49156
  47.7 37.7 %copy-start.5 = (f32[3,4096]{1,0:T(4,128)S(1)}, f32[3,4096]{1,0:T(4,128)}, u32[]{:S(2)}) copy-start(f32[3,4096]{1,0:T(4,128)} %pos.1) | copy-start | bytes 147460
  47.7 37.7 %copy-start.18 = (f32[3]{0:T(128)S(1)}, f32[3]{0:T(128)}, u32[]{:S(2)}) copy-start(f32[3]{0:T(128)} %accel.5) | copy-start | bytes 40
  57.1 51.6 %copy-start.10 = (s32[4096]{0:T(1024)S(1)}, s32[4096]{0:T(1024)}, u32[]{:S(2)}) copy-start(s32[4096]{0:T(1024)} %param.32) | copy-start | bytes 49156
  57.1 6.9 %collective-permute-start.5 = (f32[3,128]{1,0:T(4,128)S(1)}, f32[3,128]{1,0:T(4,128)S(1)}, u32[]{:S(2)}, u32[]{:S(2)}) collective-permute-start(f32[3,128]{1,0:T(4,128)S(1)} %get-tuple-element.53), channel_id=1, source_target_pairs={{0,1},{1,0},{2,3},{3,2},{4,5},{5,4},{6,7},{7,6},{8,9},{9,8},{10,11... | collective-permute-start | bytes 4616 | tf_op jit(solution)/shard_map/ppermute | solution.py:352
  59.4 4.7 %collective-permute-start.6 = (f32[3,128]{1,0:T(4,128)S(1)}, f32[3,128]{1,0:T(4,128)S(1)}, u32[]{:S(2)}, u32[]{:S(2)}) collective-permute-start(f32[3,128]{1,0:T(4,128)S(1)} %get-tuple-element.54), channel_id=1, source_target_pairs={{0,2},{1,3},{2,0},{3,1},{4,6},{5,7},{6,4},{7,5},{8,10},{9,11},{10,... | collective-permute-start | bytes 4616 | tf_op jit(solution)/shard_map/ppermute | solution.py:352
  59.4 4.7 %collective-permute-start.7 = (f32[3,128]{1,0:T(4,128)S(1)}, f32[3,128]{1,0:T(4,128)S(1)}, u32[]{:S(2)}, u32[]{:S(2)}) collective-permute-start(f32[3,128]{1,0:T(4,128)S(1)} %get-tuple-element.55), channel_id=1, source_target_pairs={{0,4},{1,5},{2,6},{3,7},{4,0},{5,1},{6,2},{7,3},{8,12},{9,13},{10,... | collective-permute-start | bytes 4616 | tf_op jit(solution)/shard_map/ppermute | solution.py:352
  60.8 3.3 %collective-permute-start.8 = (f32[3,128]{1,0:T(4,128)S(1)}, f32[3,128]{1,0:T(4,128)S(1)}, u32[]{:S(2)}, u32[]{:S(2)}) collective-permute-start(f32[3,128]{1,0:T(4,128)S(1)} %get-tuple-element.56), channel_id=1, source_target_pairs={{0,8},{1,9},{2,10},{3,11},{4,12},{5,13},{6,14},{7,15},{8,0},{9,1},... | collective-permute-start | bytes 4616 | tf_op jit(solution)/shard_map/ppermute | solution.py:352
  61.4 3.9 %collective-permute-start.9 = (f32[3,128]{1,0:T(4,128)S(1)}, f32[3,128]{1,0:T(4,128)S(1)}, u32[]{:S(2)}, u32[]{:S(2)}) collective-permute-start(f32[3,128]{1,0:T(4,128)S(1)} %get-tuple-element.57), channel_id=1, source_target_pairs={{0,16},{1,17},{2,18},{3,19},{4,20},{5,21},{6,22},{7,23},{8,24},{9,... | collective-permute-start | bytes 4616 | tf_op jit(solution)/shard_map/ppermute | solution.py:352
  65.4 74.5 %copy-start.14 = (f32[3,400]{1,0:T(4,128)S(1)}, f32[3,400]{1,0:T(4,128)}, u32[]{:S(2)}) copy-start(f32[3,400]{1,0:T(4,128)} %pcenter.1) | copy-start | bytes 14404
  65.4 74.5 %copy-start.15 = (f32[3,400]{1,0:T(4,128)S(1)}, f32[3,400]{1,0:T(4,128)}, u32[]{:S(2)}) copy-start(f32[3,400]{1,0:T(4,128)} %pinertia.1) | copy-start | bytes 14404
  65.4 74.5 %copy-start.19 = (f32[400]{0:T(512)S(1)}, f32[400]{0:T(512)}, u32[]{:S(2)}) copy-start(f32[400]{0:T(512)} %param.33) | copy-start | bytes 4804
  74.8 9.6 %collective-permute-start.10 = (f32[3,128]{1,0:T(4,128)S(1)}, f32[3,128]{1,0:T(4,128)S(1)}, u32[]{:S(2)}, u32[]{:S(2)}) collective-permute-start(f32[3,128]{1,0:T(4,128)S(1)} %get-tuple-element.63), channel_id=1, source_target_pairs={{0,1},{1,0},{2,3},{3,2},{4,5},{5,4},{6,7},{7,6},{8,9},{9,8},{10,11... | collective-permute-start | bytes 4616 | tf_op jit(solution)/shard_map/ppermute | solution.py:352
  77.0 7.5 %collective-permute-start.11 = (f32[3,128]{1,0:T(4,128)S(1)}, f32[3,128]{1,0:T(4,128)S(1)}, u32[]{:S(2)}, u32[]{:S(2)}) collective-permute-start(f32[3,128]{1,0:T(4,128)S(1)} %get-tuple-element.64), channel_id=1, source_target_pairs={{0,2},{1,3},{2,0},{3,1},{4,6},{5,7},{6,4},{7,5},{8,10},{9,11},{10,... | collective-permute-start | bytes 4616 | tf_op jit(solution)/shard_map/ppermute | solution.py:352
  77.0 7.5 %collective-permute-start.12 = (f32[3,128]{1,0:T(4,128)S(1)}, f32[3,128]{1,0:T(4,128)S(1)}, u32[]{:S(2)}, u32[]{:S(2)}) collective-permute-start(f32[3,128]{1,0:T(4,128)S(1)} %get-tuple-element.65), channel_id=1, source_target_pairs={{0,4},{1,5},{2,6},{3,7},{4,0},{5,1},{6,2},{7,3},{8,12},{9,13},{10,... | collective-permute-start | bytes 4616 | tf_op jit(solution)/shard_map/ppermute | solution.py:352
  80.1 4.3 %collective-permute-start.13 = (f32[3,128]{1,0:T(4,128)S(1)}, f32[3,128]{1,0:T(4,128)S(1)}, u32[]{:S(2)}, u32[]{:S(2)}) collective-permute-start(f32[3,128]{1,0:T(4,128)S(1)} %get-tuple-element.66), channel_id=1, source_target_pairs={{0,8},{1,9},{2,10},{3,11},{4,12},{5,13},{6,14},{7,15},{8,0},{9,1},... | collective-permute-start | bytes 4616 | tf_op jit(solution)/shard_map/ppermute | solution.py:352
  81.5 3.9 %collective-permute-start.14 = (f32[3,128]{1,0:T(4,128)S(1)}, f32[3,128]{1,0:T(4,128)S(1)}, u32[]{:S(2)}, u32[]{:S(2)}) collective-permute-start(f32[3,128]{1,0:T(4,128)S(1)} %get-tuple-element.67), channel_id=1, source_target_pairs={{0,16},{1,17},{2,18},{3,19},{4,20},{5,21},{6,22},{7,23},{8,24},{9,... | collective-permute-start | bytes 4616 | tf_op jit(solution)/shard_map/ppermute | solution.py:352

commit v2 on v1

v2 whole, which is shorter than its diff:
```python
import functools

import jax
import jax.numpy as jnp
from jax import lax
from jax.experimental import pallas as pl
from jax.experimental.pallas import tpu as pltpu
from jax.sharding import PartitionSpec as P

CYCLES = 3
PARTS_SIZE = 400

TIME_STEP = 0.1
DAMP_RATIO = 0.05
PENALTY = 2.0
GAP_WIDTH = 0.5
CONTACT_DAMP = 0.2

BF = jnp.bfloat16
F32 = jnp.float32
NT = (((1,), (1,)), ((), ()))
LANES = 128
ROWS = 32
NBR = 5
TOGETHER = 4

VMEM = pl.BlockSpec(memory_space=pltpu.VMEM)
SMEM = pl.BlockSpec(memory_space=pltpu.SMEM)
HBM = pl.BlockSpec(memory_space=pltpu.HBM)


def call(body, outs, in_specs, name, scratch=(), flops=0):
    return pl.pallas_call(
        body,
        out_shape=[jax.ShapeDtypeStruct(s, d) for s, d in outs],
        in_specs=in_specs,
        out_specs=[VMEM] * len(outs),
        scratch_shapes=list(scratch),
        compiler_params=pltpu.CompilerParams(vmem_limit_bytes=40 << 20),
        cost_estimate=pl.CostEstimate(flops=flops, bytes_accessed=1 << 20, transcendentals=0),
        name=name,
    )


def lanes_of(row, idx):
    return jnp.take_along_axis(row, idx, axis=1, mode="promise_in_bounds")


def gather(tab, bases, lo, hi):
    acc = [None] * len(bases)
    for h in range(ROWS):
        here = hi == h
        for c, base in enumerate(bases):
            row = jnp.broadcast_to(tab[base + h : base + h + 1, :], (8, LANES))
            val = lanes_of(row, lo)
            acc[c] = val if h == 0 else jnp.where(here, val, acc[c])
    return acc


def halves(x):
    first = x.astype(BF)
    return first, (x - first.astype(F32)).astype(BF)


def wide(x, a, n):
    row = jnp.broadcast_to(x[a : a + 1, :].astype(F32), (16, LANES)).astype(BF)
    return jnp.concatenate([row] * (n // 16), 0)


def iota_rows(n):
    return lax.broadcasted_iota(jnp.int32, (n, LANES), 0).astype(F32).astype(BF)


def place(lo, hi, vals):
    lof, hif = lo.astype(F32), hi.astype(F32)
    it = iota_rows(LANES)
    split = [halves(v) for v in vals]
    one, zero = jnp.ones((LANES, LANES), BF), jnp.zeros((LANES, LANES), BF)
    left, right = [], []
    for a in range(8):
        right.append(jnp.where(wide(lof, a, LANES) == it, one, zero))
        mask = wide(hif, a, ROWS) == it[:ROWS]
        left.append(
            jnp.concatenate(
                [
                    jnp.where(mask, wide(split[c][s], a, ROWS), zero[:ROWS])
                    for s in range(2)
                    for c in range(len(vals))
                ],
                0,
            )
        )
    return jnp.concatenate(left, 1), jnp.concatenate(right, 1)


def add_placed(acc, lo, hi, vals):
    left, right = place(lo, hi, vals)
    acc[...] += lax.dot_general(left, right, NT, preferred_element_type=F32)


def to_rows(src, dst):
    for c in range(3):
        for h in range(ROWS):
            dst[c * ROWS + h : c * ROWS + h + 1, :] = src[c : c + 1, h * LANES : (h + 1) * LANES]


def elements(idx, mat, tab, cols, g, acc):
    acc[...] = jnp.zeros_like(acc)
    steps = ROWS // TOGETHER

    def corners(i, q):
        here = idx[:, pl.ds(pl.multiple_of((i * TOGETHER + q) * LANES, LANES), LANES)]
        return here & 127, here >> 7

    def fetch(i):
        vals = []
        for q in range(TOGETHER):
            vals += gather(tab, (0, ROWS, 2 * ROWS), *corners(i, q))
        return tuple(vals)

    def step(i, vals):
        upcoming = fetch((i + 1) & (steps - 1))
        left, right = [], []
        for q in range(TOGETHER):
            for c in range(3):
                g[q * 24 + 8 * c : q * 24 + 8 * c + 8, :] = vals[q * 3 + c]
            first = mat[i * TOGETHER + q] * 24
            force = [jnp.zeros((8, LANES), F32)] * 3
            for j in range(24):
                col = cols.at[first + j]
                row = jnp.broadcast_to(g[q * 24 + j : q * 24 + j + 1, :], (8, LANES))
                force = [force[c] + col[8 * c : 8 * c + 8, :] * row for c in range(3)]
            one, two = place(*corners(i, q), force)
            left.append(one)
            right.append(two)
        acc[...] += lax.dot_general(
            jnp.concatenate(left, 1), jnp.concatenate(right, 1), NT, preferred_element_type=F32
        )
        return upcoming

    lax.fori_loop(0, steps, step, fetch(0))


def finish_internal(acc, internal, shared):
    internal[...] = acc[0:96, :] + acc[96:192, :]
    return gather(internal, (0, ROWS, 2 * ROWS), shared[...] & 127, shared[...] >> 7)


def slots(slave, owner, master, normal, acc):
    acc[...] = jnp.zeros_like(acc)
    down = lax.broadcasted_iota(jnp.int32, (LANES, LANES), 0)
    across = lax.broadcasted_iota(jnp.int32, (LANES, LANES), 1)
    before = jnp.where(down < across, 1.0, 0.0).astype(BF)
    carry = jnp.zeros((LANES, 1), F32)
    for t in range(16):
        hit = jnp.where(jnp.broadcast_to(owner[t : t + 1, :], (LANES, LANES)) == down, 1.0, 0.0)
        hitb = hit.astype(BF)
        count = jnp.dot(hitb, before, preferred_element_type=F32) + carry
        rank = jnp.sum(hit * count, axis=0, keepdims=True)
        carry = carry + jnp.sum(hit, axis=1, keepdims=True)
        mine = jnp.broadcast_to(rank, (64, LANES)) == down[:64].astype(F32)
        vals = [normal[c : c + 1, t * LANES : (t + 1) * LANES] for c in range(3)]
        vals += [master[t : t + 1, :].astype(F32), slave[t : t + 1, :].astype(F32)]
        left = [jnp.broadcast_to(x, (64, LANES)) for x in vals]
        for s in range(3):
            piece = [jnp.where(mine, x, 0.0).astype(BF) for x in left]
            left = [x - x.astype(BF).astype(F32) for x in left]
            acc[:, 0:320] += lax.dot_general(
                hitb, jnp.concatenate(piece, 0), NT, preferred_element_type=F32
            )


def spans():
    return [(h, min(LANES, PARTS_SIZE - h * LANES)) for h in range(4)]


def row_of_tile(row):
    here = lax.broadcasted_iota(jnp.int32, (8, LANES), 0) == (row & 7)
    return pl.ds(pl.multiple_of((row >> 3) << 3, 8), 8), here


def first_kernel(*refs):
    srcs = refs[:18]
    (u, v, fm, mass, pos, idx, inv, cols, part, shared, internal, send, sidx, rigid) = refs[18:32]
    work = refs[32:]
    (disp0, vel0, force0, pos0, shared0, slave, owner, master, normal, stiff) = work[:10]
    pmass, pcenter, pinertia, mat, accel, conn = work[10:16]
    tab, g, acc, small, table, sems = work[16:]
    dsts = (stiff, disp0, vel0, conn, mat, shared0, force0, mass, accel, slave, owner, master, normal)
    dsts = dsts + (pos0, part, pmass, pcenter, pinertia)
    copies = [pltpu.make_async_copy(a, b, sems.at[i]) for i, (a, b) in enumerate(zip(srcs, dsts))]
    for copy in copies:
        copy.start()
    small[...] = jnp.zeros_like(small)
    copies[0].wait()
    for m in range(8):
        for j in range(24):
            cols[m * 24 + j] = jnp.broadcast_to(stiff[m, :, j : j + 1], (24, LANES))
    for copy in copies[1:]:
        copy.wait()
    to_rows(disp0, u)
    to_rows(vel0, v)
    to_rows(force0, fm)
    to_rows(pos0, pos)
    tab[...] = u[...] + DAMP_RATIO * v[...]
    for c in range(3):
        at = slice(c * ROWS, (c + 1) * ROWS)
        fm[at, :] = fm[at, :] / mass[...] - accel[c]
    lane = lax.broadcasted_iota(jnp.int32, (8, LANES), 1)
    for b in range(ROWS):
        at = slice(b * LANES, (b + 1) * LANES)
        idx[:, at] = (conn[:, at] + lane + b * LANES) & 4095
    shared[...] = jnp.zeros_like(shared)
    for b in range(NBR):
        shared[b : b + 1, :] = shared0[b]
    row = lax.broadcasted_iota(jnp.int32, (8, LANES), 0).astype(F32)
    held = row < NBR
    kept = [jnp.where(held, lane.astype(F32), 0.0), jnp.where(held, row + 1.0, 0.0)]
    add_placed(small, shared[...] & 127, shared[...] >> 7, kept)
    inv[...] = (small[0:64, :] + small[64:128, :]).astype(jnp.int32)
    rigid[...] = jnp.ones_like(rigid)
    for h, n in spans():
        at = slice(h * LANES, h * LANES + n)
        rigid[h : h + 1, 0:n] = pmass[0:1, at]
        for c in range(3):
            rigid[8 + 8 * c + h : 9 + 8 * c + h, 0:n] = pcenter[c : c + 1, at]
            rigid[32 + 8 * c + h : 33 + 8 * c + h, 0:n] = pinertia[c : c + 1, at]
    slots(slave, owner, master, normal, table)
    send[:, 0:256] = table[:, 0:256]
    sidx[...] = table[:, 256:384]
    send[:, 256:640] = jnp.zeros((LANES, 384), F32)
    elements(idx, mat, tab, cols, g, acc)
    own = finish_internal(acc, internal, shared)
    me = lax.axis_index("dom")
    for b in range(NBR):
        tile, here = row_of_tile(me ^ (1 << b))
        for c in range(3):
            row = jnp.broadcast_to(own[c][b : b + 1, :], (8, LANES))
            send[tile, 256 + c * LANES : 256 + (c + 1) * LANES] += jnp.where(here, row, 0.0)


def update(u, v, internal, inv, fm, mass, recv, c, r):
    at = slice(c * ROWS + r, c * ROWS + r + 8)
    slot, which = inv[r : r + 8, :], inv[ROWS + r : ROWS + r + 8, :]
    total = internal[at, :]
    for b in range(NBR):
        row = jnp.broadcast_to(recv[b][c], (8, LANES))
        total = total + jnp.where(which == b + 1, lanes_of(row, slot), 0.0)
    speed = v[at, :] + TIME_STEP * (fm[at, :] - total / mass[r : r + 8, :])
    return at, u[at, :] + TIME_STEP * speed, speed, total


def rows_of(refs):
    return [[ref[c : c + 1, :] for c in range(3)] for ref in refs]


def next_kernel(from_table, u, v, internal, inv, fm, mass, idx, mat, cols, shared, *rest):
    if from_table:
        got, rest = rest[0], rest[1:]
        me = lax.axis_index("dom")
        recv = []
        for b in range(NBR):
            tile, here = row_of_tile(me ^ (1 << b))
            picked = [
                jnp.where(here, got[tile, 256 + c * LANES : 256 + (c + 1) * LANES], 0.0) for c in range(3)
            ]
            recv.append([jnp.sum(x, axis=0, keepdims=True) for x in picked])
    else:
        recv, rest = rows_of(rest[:NBR]), rest[NBR:]
    u2, v2, internal2 = rest[:3]
    own = rest[3:8]
    tab, g, acc = rest[8:]
    for c in range(3):
        for r in range(0, ROWS, 8):
            at, disp, speed, _ = update(u, v, internal, inv, fm, mass, recv, c, r)
            u2[at, :] = disp
            v2[at, :] = speed
            tab[at, :] = disp + DAMP_RATIO * speed
    elements(idx, mat, tab, cols, g, acc)
    vals = finish_internal(acc, internal2, shared)
    for b in range(NBR):
        for c in range(3):
            own[b][c : c + 1, :] = vals[c][b : b + 1, :]


def dots_kernel(u, v, internal, inv, fm, mass, pos, part, send, sidx, got, *rest):
    recv = rows_of(rest[:5])
    x2, v2, net, dots, idx, nrm, tab, acc = rest[5:]
    for c in range(3):
        for r in range(0, ROWS, 8):
            at, disp, speed, total = update(u, v, internal, inv, fm, mass, recv, c, r)
            place_now = pos[at, :] + disp
            x2[at, :] = place_now
            v2[at, :] = speed
            net[at, :] = mass[r : r + 8, :] * fm[at, :] - total
            tab[at, :] = place_now
            tab[c * ROWS + 96 + r : c * ROWS + 96 + r + 8, :] = speed
    left = lax.broadcasted_iota(jnp.int32, (LANES, LANES), 1) < 64
    own0, own1 = send[:, 0:128], send[:, 128:256]
    got0, got1 = got[:, 0:128], got[:, 128:256]
    nrm[0] = jnp.where(left, own0, pltpu.roll(got0, 64, 1))
    nrm[1] = jnp.where(left, pltpu.roll(own0, 64, 1), got0)
    nrm[2] = jnp.where(left, own1, pltpu.roll(got1, 64, 1))
    idx[...] = jnp.where(left, sidx[...], got1).astype(jnp.int32)

    def vals(r):
        m = mass[r : r + 8, :]
        return [m, *[m * tab[c * ROWS + r : c * ROWS + r + 8, :] for c in range(3)]]

    acc[...] = jnp.zeros_like(acc)
    part_sums(part, vals, acc, True)
    moments = jnp.concatenate([acc[0:32, :] + acc[32:64, :], jnp.zeros((96, LANES), F32)], 0)
    dots[:, 256:384] = moments.T

    def step(i, carry):
        for q in range(2):
            off = pl.multiple_of(i * 16 + q * 8, 8)
            here = idx[pl.ds(off, 8), :]
            vals = gather(tab, tuple(range(0, 192, ROWS)), here & 127, here >> 7)
            w = [nrm[c, pl.ds(off, 8), :] for c in range(3)]
            dots[pl.ds(off, 8), 0:128] = vals[0] * w[0] + vals[1] * w[1] + vals[2] * w[2]
            dots[pl.ds(off, 8), 128:256] = vals[3] * w[0] + vals[4] * w[1] + vals[5] * w[2]
        return carry

    lax.fori_loop(0, 8, step, 0)


def part_sums(part, vals, acc, by_device):
    it = iota_rows(LANES)
    it8 = (lax.broadcasted_iota(jnp.int32, (16, LANES), 0) & 7).astype(F32).astype(BF)
    one, zero = jnp.ones((LANES, LANES), BF), jnp.zeros((LANES, LANES), BF)
    for r in range(0, ROWS, 8):
        here = part[r : r + 8, :]
        lo = here & 127
        if by_device:
            lo = ((lo & 63) << 1) | (lo >> 6)
        lof, hif = lo.astype(F32), (here >> 7).astype(F32)
        val = vals(r)
        first = [x.astype(BF).astype(F32) for x in val]
        split = (first, [x - y for x, y in zip(val, first)])
        left, right = [], []
        for a in range(8):
            right.append(jnp.where(wide(lof, a, LANES) == it, one, zero))
            mask = wide(hif, a, 16) == it8
            rows = []
            for s in range(2):
                for k in range(0, len(val), 2):
                    two = [jnp.broadcast_to(split[s][k + d][a : a + 1, :], (8, LANES)) for d in range(2)]
                    rows.append(jnp.where(mask, jnp.concatenate(two, 0).astype(BF), zero[:16]))
            left.append(jnp.concatenate(rows, 0))
        acc[...] += lax.dot_general(
            jnp.concatenate(left, 1), jnp.concatenate(right, 1), NT, preferred_element_type=F32
        )


def contact_kernel(dots, got, idx, nrm, x, v, net, mass, part, nodal, keep, give, acc, tot, acc2):
    acc[...] = jnp.zeros_like(acc)
    acc2[...] = jnp.zeros_like(acc2)
    sign = jnp.where(lax.broadcasted_iota(jnp.int32, (8, LANES), 1) < 64, 1.0, -1.0)

    def step(i, carry):
        left, right = [], []
        for q in range(4):
            at = pl.ds(pl.multiple_of(i * 32 + q * 8, 8), 8)
            gap = sign * (dots[at, 0:128] - pltpu.roll(got[at, 0:128], 64, 1))
            closing = sign * (dots[at, 128:256] - pltpu.roll(got[at, 128:256], 64, 1))
            z = -gap / GAP_WIDTH
            soft = jnp.maximum(z, 0.0) + jnp.log1p(jnp.exp(-jnp.abs(z)))
            push = sign * (PENALTY * GAP_WIDTH * soft - CONTACT_DAMP * closing)
            here = idx[at, :]
            one, two = place(here & 127, here >> 7, [push * nrm[c, at, :] for c in range(3)])
            left.append(one)
            right.append(two)
        acc[...] += lax.dot_general(
            jnp.concatenate(left, 1), jnp.concatenate(right, 1), NT, preferred_element_type=F32
        )
        return carry

    lax.fori_loop(0, 4, step, 0)
    contact = acc[0:96, :] + acc[96:192, :]
    tot[...] = net[...] + contact
    for c in range(3):
        speed = v[c * ROWS : (c + 1) * ROWS, :] + TIME_STEP * contact[c * ROWS : (c + 1) * ROWS, :] / mass[...]
        for h in range(ROWS):
            nodal[c : c + 1, h * LANES : (h + 1) * LANES] = speed[h : h + 1, :]

    def vals(r):
        p = [x[c * ROWS + r : c * ROWS + r + 8, :] for c in range(3)]
        n = [tot[c * ROWS + r : c * ROWS + r + 8, :] for c in range(3)]
        return [
            *n,
            p[1] * n[2] - p[2] * n[1],
            p[2] * n[0] - p[0] * n[2],
            p[0] * n[1] - p[1] * n[0],
        ]

    part_sums(part, vals, acc2, False)
    acc2[0:48, :] = acc2[0:48, :] + acc2[48:96, :]
    even = lax.axis_index("dom") & 1 == 0
    for k in range(6):
        low, high = acc2[8 * k : 8 * k + 2, :], acc2[8 * k + 2 : 8 * k + 4, :]
        keep[2 * k : 2 * k + 2, :] = jnp.where(even, low, high)
        give[2 * k : 2 * k + 2, :] = jnp.where(even, high, low)
    keep[12:16, :] = jnp.zeros((4, LANES), F32)
    give[12:16, :] = jnp.zeros((4, LANES), F32)
    keep[12:13, :] = jnp.sum(got[:, 256:384], axis=0, keepdims=True)


def spread_kernel(keep, given, out):
    tile = keep[...] + given[...]
    for k in range(64):
        out[16 * k : 16 * k + 16, :] = tile


def total_kernel(got, out):
    total = got[0:16, :]
    for k in range(1, 64):
        total = total + got[16 * k : 16 * k + 16, :]
    out[0:16, :] = total
    for k in range(64):
        out[16 + k : 17 + k, :] = got[16 * k + 12 : 16 * k + 13, :]


def motion_kernel(mine, other, rigid, out):
    even = lax.axis_index("dom") & 1 == 0
    low = jnp.where(even, mine[...], other[...])
    high = jnp.where(even, other[...], mine[...])
    by = jnp.concatenate([low[16:80, :], high[16:80, :]], 0).T
    moments = [by[8 * k : 8 * k + 4, :] for k in range(4)]
    sums = [jnp.concatenate([low[2 * k : 2 * k + 2, :], high[2 * k : 2 * k + 2, :]], 0) for k in range(6)]
    own = rigid[0:4, :]
    mass = own + moments[0]
    centre = [(own * rigid[8 + 8 * c : 12 + 8 * c, :] + moments[1 + c]) / mass for c in range(3)]
    force, turn = sums[0:3], sums[3:6]
    rows = [y / mass for y in force]
    for c in range(3):
        a, b = (c + 1) % 3, (c + 2) % 3
        moment = turn[c] - (centre[a] * force[b] - centre[b] * force[a])
        rows.append(moment / rigid[32 + 8 * c : 36 + 8 * c, :])
    for r, row in enumerate(rows):
        for h, n in spans():
            out[r : r + 1, h * LANES : h * LANES + n] = row[h : h + 1, 0:n]


def partner(block, apart):
    count = lax.axis_size("dom")
    return lax.ppermute(block, "dom", [(i, i ^ (1 << apart)) for i in range(count)])


def swap(block, groups=None):
    return lax.all_to_all(block, "dom", 0, 0, tiled=True, axis_index_groups=groups)


def per_device(
    rest_pos,
    displacement,
    velocity,
    ext_force,
    node_mass,
    body_accel,
    connectivity,
    elem_material,
    stiffness,
    shared_nodes,
    contact_slave,
    contact_owner,
    contact_master,
    contact_normal,
    part_of_node,
    part_mass,
    part_center,
    part_inertia,
):
    state = ((96, LANES), F32)
    square = ((LANES, LANES), F32)
    table = ((LANES, 5 * LANES), F32)
    own = [((3, LANES), F32)] * NBR
    work = [
        pltpu.VMEM((96, LANES), F32),
        pltpu.VMEM((24 * TOGETHER, LANES), F32),
        pltpu.VMEM((192, LANES), F32),
    ]
    inputs = (
        stiffness,
        displacement,
        velocity,
        connectivity,
        elem_material,
        shared_nodes.transpose(1, 0, 2),
        ext_force,
        node_mass.reshape(ROWS, LANES),
        body_accel,
        contact_slave.reshape(16, LANES),
        contact_owner.reshape(16, LANES),
        contact_master.reshape(16, LANES),
        contact_normal,
        rest_pos,
        part_of_node.reshape(ROWS, LANES),
        part_mass.reshape(1, PARTS_SIZE),
        part_center,
        part_inertia,
    )
    rows, ints = ((ROWS, LANES), F32), jnp.int32
    u, v, fm, mass, pos, idx, inv, cols, part, shared, internal, send, sidx, rigid = call(
        first_kernel,
        [
            state,
            state,
            state,
            rows,
            state,
            ((8, 4096), ints),
            ((64, LANES), ints),
            ((192, 24, LANES), F32),
            ((ROWS, LANES), ints),
            ((8, LANES), ints),
            state,
            table,
            square,
            ((56, LANES), F32),
        ],
        [HBM] * 18,
        "first_cycle",
        [
            *[pltpu.VMEM((3, 4096), F32)] * 4,
            pltpu.VMEM((NBR, 1, LANES), ints),
            *[pltpu.VMEM((16, LANES), ints)] * 3,
            pltpu.VMEM((3, 2048), F32),
            pltpu.VMEM((8, 24, 24), F32),
            pltpu.VMEM((1, PARTS_SIZE), F32),
            pltpu.VMEM((3, PARTS_SIZE), F32),
            pltpu.VMEM((3, PARTS_SIZE), F32),
            pltpu.SMEM((ROWS,), ints),
            pltpu.SMEM((3,), F32),
            pltpu.VMEM((8, 4096), ints),
            *work,
            pltpu.VMEM((LANES, LANES), F32),
            pltpu.VMEM((LANES, 3 * LANES), F32),
            pltpu.SemaphoreType.DMA((18,)),
        ],
    )(*inputs)
    got = swap(send)
    recv = [got]
    for n in range(CYCLES - 1):
        u, v, internal, *mine = call(
            functools.partial(next_kernel, n == 0),
            [state, state, state, *own],
            [VMEM] * 7 + [SMEM] + [VMEM] * (2 + len(recv)),
            "next_cycle",
            work,
        )(u, v, internal, inv, fm, mass, idx, elem_material, cols, shared, *recv)
        recv = [partner(mine[b], b) for b in range(NBR)]

    trio = ((LANES, 3 * LANES), F32)
    x, v, net, dots, ends, nrm = call(
        dots_kernel,
        [state, state, state, trio, ((LANES, LANES), ints), ((3, LANES, LANES), F32)],
        [VMEM] * 16,
        "contact_dots",
        [pltpu.VMEM((192, LANES), F32), pltpu.VMEM((64, LANES), F32)],
    )(u, v, internal, inv, fm, mass, pos, part, send, sidx, got, *recv)
    half = ((16, LANES), F32)
    nodal_velocity, keep, give = call(
        contact_kernel,
        [((3, 4096), F32), half, half],
        [VMEM] * 9,
        "contact_forces",
        [pltpu.VMEM((192, LANES), F32), pltpu.VMEM((96, LANES), F32), pltpu.VMEM((96, LANES), F32)],
    )(dots, swap(dots), ends, nrm, x, v, net, mass, part)
    (spread,) = call(spread_kernel, [((1024, LANES), F32)], [VMEM] * 2, "part_spread")(keep, partner(give, 0))
    chips = lax.axis_size("dom") // 2
    groups = [[2 * i + core for i in range(chips)] for core in range(2)]
    (total,) = call(total_kernel, [((80, LANES), F32)], [VMEM], "part_totals")(swap(spread, groups))
    (motion,) = call(motion_kernel, [((6, PARTS_SIZE), F32)], [VMEM] * 3, "part_motion")(
        total, partner(total, 0), rigid
    )
    return nodal_velocity, motion


def solution(mesh):
    placed = (
        P(None, "dom"),
        P(None, "dom"),
        P(None, "dom"),
        P(None, "dom"),
        P("dom"),
        P(),
        P(None, "dom"),
        P("dom"),
        P(),
        P("dom", None, None),
        P("dom"),
        P("dom", None),
        P("dom"),
        P(None, "dom"),
        P("dom"),
        P(),
        P(),
        P(),
    )
    return jax.shard_map(
        per_device, mesh=mesh, in_specs=placed, out_specs=(P(None, "dom"), P()), check_vma=False
    )
```

time: 141 us -> 128 us (0.908)
  starting transfers between devices: 36.4 us -> 14.5 us
  blocking collectives: 46.2 us -> 56.1 us
  Pallas kernels: 42.2 us -> 34.6 us
  waiting for transfers between devices: 3.22 us -> 7.45 us
  local copies, waits for them, and re-layouts: 11.7 us -> 14.1 us
    all_to_all x1 -> x0, starting transfers between devices: 11.4 us -> none  [swap(): return lax.all_to_all(block, 'dom', 0, 0, tiled=True)]
    ppermute x15 -> x12, starting transfers between devices: 25 us -> 14.5 us  [partner(): lax.ppermute(block, 'dom', [(i, i ^ 1 << apart) for i in range(count)])]
    all_to_all x3, blocking collectives: 46.2 us -> 56.1 us  [swap(): lax.all_to_all(block, 'dom', 0, 0, tiled=True, axis_index_groups=groups)]
    pallas_call x8, Pallas kernels: 42.2 us -> 34.6 us  [the longest x2 13.5 us: per_device(): call(functools.partial(next_kernel, n == 0), [state, state, state, *own],...]
    ppermute x15 -> x12, waiting for transfers between devices: 3.22 us -> 7.45 us  [partner(): lax.ppermute(block, 'dom', [(i, i ^ 1 << apart) for i in range(count)])]
    unnamed x43 -> x38, local copies, waits for them, and re-layouts: 10.8 us -> 13.5 us
  transfers between devices with their start and end apart: 16 -> 12, of which waited for: 3 -> 7; matrix products, arithmetic and copies ran while one was open for 0% -> 0% of each run, Pallas kernels for 21% -> 0%
where the time goes in v2:
time: 128 us; the launch traced here: 127 us
  blocking collectives  56.1 us (44%)
  Pallas kernels  34.6 us (27%)
  starting transfers between devices  14.5 us (11%)
  local copies, waits for them, and re-layouts  14.1 us (11%)
  waiting for transfers between devices  7.45 us (6%)
    all_to_all x3, blocking collectives, swap(): lax.all_to_all(block, 'dom', 0, 0, tiled=True, axis_index_groups=groups)  56.1 us
    ppermute x12, starting transfers between devices, partner(): lax.ppermute(block, 'dom', [(i, i ^ 1 << apart) for i in range(count)])  14.5 us
    pallas_call x2, Pallas kernels, per_device(): call(functools.partial(next_kernel, n == 0), [state, state, state, *own],...  13.5 us
    unnamed x38, local copies, waits for them, and re-layouts  13.5 us
    pallas_call x1, Pallas kernels, per_device(): call(first_kernel, [state, state, state, rows, state, ((8, 4096), ints),...  12.3 us
    ppermute x12, waiting for transfers between devices, partner(): lax.ppermute(block, 'dom', [(i, i ^ 1 << apart) for i in range(count)])  7.45 us
    pallas_call x1, Pallas kernels, per_device(): call(dots_kernel, [state, state, state, trio, ((LANES, LANES), ints), ((3...  4.54 us
    pallas_call x1, Pallas kernels, per_device(): call(contact_kernel, [((3, 4096), F32), half, half], [VMEM] * 9, 'contact...  3.43 us
  transfers between devices with their start and end apart: 12, of which 7 were waited for; matrix products, arithmetic and copies ran while one was open for 0% of the time, Pallas kernels for 0%

profile of v2, /device:TPU:1, one launch (start us, length us, event | category | flops | bytes accessed | tf_op | source)
XLA Modules:
  0.0 127.4 jit_solution(5554595775388135859)
XLA Ops:
  0.6 0.0 copy-start
  0.6 0.9 copy-done
  1.5 0.0 copy-start.1
  1.5 0.9 copy-done.1
  2.4 0.0 copy-start.2
  2.4 0.8 copy-done.2
  3.3 0.0 copy-start.3
  3.3 0.8 copy-done.3
  4.1 0.0 copy-start.4
  4.1 0.8 copy-done.4
  5.0 0.0 copy-start.5
  5.0 0.8 copy-done.5
  5.8 0.0 copy-start.6
  5.8 0.8 copy-done.6
  6.6 0.0 copy-start.7
  6.6 0.7 copy-done.7
  7.3 0.0 copy-start.8
  7.3 0.7 copy-done.8
  8.0 0.7 copy-done.9
  8.7 0.0 copy-start.10
  8.7 0.7 copy-done.10
  9.4 0.7 copy-done.11
  10.1 0.7 copy-done.12
  10.8 0.7 copy-done.13
  11.5 0.7 copy-done.14
  12.1 0.7 copy-done.15
  12.8 0.7 copy-done.16
  13.5 0.7 copy-done.17
  14.2 12.3 %first_cycle.1 = (f32[96,128]{1,0:T(8,128)S(1)}, f32[96,128]{1,0:T(8,128)S(1)}, f32[96,128]{1,0:T(8,128)S(1)}, f32[32,128]{1,0:T(8,128)S(1)}, f32[96,128]{1,0:T(...) custom-call(f32[8,24,24]{2,1,0:T(8,128)S(1)} %copy-done.1, ...), custom_call_target="tpu_custom_call" | custom-call | bytes 1048576 | tf_op jit(solution)/shard_map/first_cycle/pallas_call | solution.py:504
  26.4 0.3 copy.20
  26.8 22.9 %all_to_all.33 = f32[128,1,640]{2,1,0:T(1,128)S(1)} all-to-all(f32[128,1,640]{2,1,0:T(1,128)S(1)} %copy.20), channel_id=1, replica_groups=mesh['dom'=128] {'dom'}, dimensions={0} | all-to-all | bytes 655360 | tf_op jit(solution)/shard_map/all_to_all | solution.py:451
  49.7 6.8 %next_cycle.2 = (f32[96,128]{1,0:T(8,128)S(1)}, f32[96,128]{1,0:T(8,128)S(1)}, f32[96,128]{1,0:T(8,128)S(1)}, f32[3,128]{1,0:T(4,128)S(1)}, f32[3,128]{1,0:T(4,1...) custom-call(f32[96,128]{1,0:T(8,128)S(1)} %get-tuple-element.41.u, ...), custom_call_target="tpu_custom_call" | custom-call | bytes 1048576 | tf_op jit(solution)/shard_map/next_cycle/pallas_call | solution.py:545
  56.5 1.0 collective-permute-start
  57.4 0.3 collective-permute-start.1
  57.7 1.6 %collective-permute-start.2 = (f32[3,128]{1,0:T(4,128)S(1)}, f32[3,128]{1,0:T(4,128)S(1)}, u32[]{:S(2)}, u32[]{:S(2)}) collective-permute-start(f32[3,128]{1,0:T(4,128)S(1)} %get-tuple-element.56), channel_id=1, source_target_pairs={{0,4},{1,5},{2,6},{3,7},{4,0},{5,1},{6,2},{7,3},{8,12},{9,13},{10,... | collective-permute-start | bytes 4616 | tf_op jit(solution)/shard_map/ppermute | solution.py:447
  59.4 0.5 collective-permute-start.3
  59.9 1.1 collective-permute-start.4
  61.0 0.0 collective-permute-done.rest_0_
  61.0 0.0 collective-permute-done.1.rest_1_
  61.0 0.7 collective-permute-done.2.rest_2_
  61.7 0.4 collective-permute-done.3.rest_3_
  62.1 1.7 %collective-permute-done.4.rest_4_ = f32[3,128]{1,0:T(4,128)S(1)} collective-permute-done((f32[3,128]{1,0:T(4,128)S(1)}, f32[3,128]{1,0:T(4,128)S(1)}, u32[]{:S(2)}, u32[]{:S(2)}) %collective-permute-start.4) | collective-permute-done | bytes 1568 | tf_op jit(solution)/shard_map/ppermute | solution.py:447
  63.8 6.8 %next_cycle.3 = (f32[96,128]{1,0:T(8,128)S(1)}, f32[96,128]{1,0:T(8,128)S(1)}, f32[96,128]{1,0:T(8,128)S(1)}, f32[3,128]{1,0:T(4,128)S(1)}, f32[3,128]{1,0:T(4,1...) custom-call(f32[96,128]{1,0:T(8,128)S(1)} %get-tuple-element.51.u, ...), custom_call_target="tpu_custom_call" | custom-call | bytes 1048576 | tf_op jit(solution)/shard_map/next_cycle/pallas_call | solution.py:545
  70.6 2.2 %collective-permute-start.5 = (f32[3,128]{1,0:T(4,128)S(1)}, f32[3,128]{1,0:T(4,128)S(1)}, u32[]{:S(2)}, u32[]{:S(2)}) collective-permute-start(f32[3,128]{1,0:T(4,128)S(1)} %get-tuple-element.65), channel_id=1, source_target_pairs={{0,1},{1,0},{2,3},{3,2},{4,5},{5,4},{6,7},{7,6},{8,9},{9,8},{10,11... | collective-permute-start | bytes 4616 | tf_op jit(solution)/shard_map/ppermute | solution.py:447
  72.9 0.0 collective-permute-start.6
  72.9 2.8 %collective-permute-start.7 = (f32[3,128]{1,0:T(4,128)S(1)}, f32[3,128]{1,0:T(4,128)S(1)}, u32[]{:S(2)}, u32[]{:S(2)}) collective-permute-start(f32[3,128]{1,0:T(4,128)S(1)} %get-tuple-element.67), channel_id=1, source_target_pairs={{0,4},{1,5},{2,6},{3,7},{4,0},{5,1},{6,2},{7,3},{8,12},{9,13},{10,... | collective-permute-start | bytes 4616 | tf_op jit(solution)/shard_map/ppermute | solution.py:447
  75.6 1.2 collective-permute-start.8
  76.9 1.1 collective-permute-start.9
  77.9 0.0 collective-permute-done.5.rest_0_
  77.9 0.0 collective-permute-done.6.rest_1_
  77.9 0.0 collective-permute-done.7.rest_2_
  77.9 0.1 collective-permute-done.8.rest_3_
  78.1 2.7 %collective-permute-done.9.rest_4_ = f32[3,128]{1,0:T(4,128)S(1)} collective-permute-done((f32[3,128]{1,0:T(4,128)S(1)}, f32[3,128]{1,0:T(4,128)S(1)}, u32[]{:S(2)}, u32[]{:S(2)}) %collective-permute-start.9) | collective-permute-done | bytes 1568 | tf_op jit(solution)/shard_map/ppermute | solution.py:447
  80.8 4.5 %contact_dots.1 = (f32[96,128]{1,0:T(8,128)S(1)}, f32[96,128]{1,0:T(8,128)S(1)}, f32[96,128]{1,0:T(8,128)S(1)}, f32[128,384]{1,0:T(8,128)S(1)}, s32[128,128]{1,0:T(8,128)S(1)}, /*index=5*/f32[3,128,128]{2,1,0:T(8,128)S(1)}) custom-call(f32[96,128]{1,0:T(8,128)S(1)} %get-tuple-element.59.u, f32[96,128]{1,0:T(8,128)S(1)} %get-tuple-element.60.v, ...), custom_call_target="tpu_custom_call" | custom-call | bytes 1048576 | tf_op jit(solution)/shard_map/contact_dots/pallas_call | solution.py:555
  85.3 0.2 copy.21
  85.6 16.0 %all_to_all.34 = f32[128,1,384]{2,1,0:T(1,128)S(1)} all-to-all(f32[128,1,384]{2,1,0:T(1,128)S(1)} %copy.21), channel_id=1, replica_groups=mesh['dom'=128] {'dom'}, dimensions={0} | all-to-all | bytes 393216 | tf_op jit(solution)/shard_map/all_to_all | solution.py:451
  101.6 3.4 %contact_forces.1 = (f32[3,4096]{1,0:T(4,128)}, f32[16,128]{1,0:T(8,128)S(1)}, f32[16,128]{1,0:T(8,128)S(1)}) custom-call(f32[128,384]{1,0:T(8,128)S(1)} %get-tuple-element.70.dots, f32[128,384]{1,0:T(8,128)S(1)} %bitcast.23, s32[128,128]{1,0:T(8,128)S(1)} %get-tuple-element.71.idx, f32[3,128,128]{2,1,0:T(8,128)S(1)} %get-tuple-element.72.nrm, ...), custom_call_target="tpu_custom_call" | custom-call | bytes 1048576 | tf_op jit(solution)/shard_map/contact_forces/pallas_call | solution.py:563
  105.0 0.7 collective-permute-start.10
  105.7 0.8 collective-permute-done.10.given
  106.6 17.2 %all_to_all.35 = f32[64,16,128]{2,1,0:T(8,128)S(1)} all-to-all(f32[64,16,128]{2,1,0:T(8,128)S(1)} %bitcast.19), channel_id=1, replica_groups={{0,2,4,6,8,10,12,14,16,18,20,22,24,26,28,30,32,34,36,38,40,42,44,46,48,..., dimensions={0} | all-to-all | bytes 1048576 | tf_op jit(solution)/shard_map/all_to_all | solution.py:451
  123.7 0.1 part_totals.1.mine
  123.8 2.0 %collective-permute-start.11 = (f32[80,128]{1,0:T(8,128)S(1)}, f32[80,128]{1,0:T(8,128)S(1)}, u32[]{:S(2)}, u32[]{:S(2)}) collective-permute-start(f32[80,128]{1,0:T(8,128)S(1)} %part_totals.1.mine), channel_id=1, source_target_pairs={{0,1},{1,0},{2,3},{3,2},{4,5},{5,4},{6,7},{7,6},{8,9},{9,8},{10,11... | collective-permute-start | bytes 122888 | tf_op jit(solution)/shard_map/ppermute | solution.py:447
  125.8 0.9 collective-permute-done.11.other
  126.7 0.7 part_motion.1
  (11 shorter events, 0.1 us)
Async XLA Ops:
  0.6 0.9 copy-start
  1.5 0.9 copy-start.1
  2.4 0.8 copy-start.2
  3.3 0.8 copy-start.3
  4.1 0.8 copy-start.4
  5.0 0.8 copy-start.5
  5.8 0.8 copy-start.6
  6.6 0.7 copy-start.7
  7.3 0.7 copy-start.8
  8.0 0.7 copy-start.9
  8.7 0.7 copy-start.10
  9.4 0.7 copy-start.11
  10.1 0.7 copy-start.12
  10.8 0.7 copy-start.13
  11.5 0.7 copy-start.14
  12.1 0.7 copy-start.15
  12.8 0.7 copy-start.16
  13.5 0.7 copy-start.17
  56.5 4.5 %collective-permute-start = (f32[3,128]{1,0:T(4,128)S(1)}, f32[3,128]{1,0:T(4,128)S(1)}, u32[]{:S(2)}, u32[]{:S(2)}) collective-permute-start(f32[3,128]{1,0:T(4,128)S(1)} %get-tuple-element.54), channel_id=1, source_target_pairs={{0,1},{1,0},{2,3},{3,2},{4,5},{5,4},{6,7},{7,6},{8,9},{9,8},{10,11... | collective-permute-start | bytes 4616 | tf_op jit(solution)/shard_map/ppermute | solution.py:447
  57.4 3.5 %collective-permute-start.1 = (f32[3,128]{1,0:T(4,128)S(1)}, f32[3,128]{1,0:T(4,128)S(1)}, u32[]{:S(2)}, u32[]{:S(2)}) collective-permute-start(f32[3,128]{1,0:T(4,128)S(1)} %get-tuple-element.55), channel_id=1, source_target_pairs={{0,2},{1,3},{2,0},{3,1},{4,6},{5,7},{6,4},{7,5},{8,10},{9,11},{10,... | collective-permute-start | bytes 4616 | tf_op jit(solution)/shard_map/ppermute | solution.py:447
  57.7 3.9 %collective-permute-start.2 = (f32[3,128]{1,0:T(4,128)S(1)}, f32[3,128]{1,0:T(4,128)S(1)}, u32[]{:S(2)}, u32[]{:S(2)}) collective-permute-start(f32[3,128]{1,0:T(4,128)S(1)} %get-tuple-element.56), channel_id=1, source_target_pairs={{0,4},{1,5},{2,6},{3,7},{4,0},{5,1},{6,2},{7,3},{8,12},{9,13},{10,... | collective-permute-start | bytes 4616 | tf_op jit(solution)/shard_map/ppermute | solution.py:447
  59.4 2.7 %collective-permute-start.3 = (f32[3,128]{1,0:T(4,128)S(1)}, f32[3,128]{1,0:T(4,128)S(1)}, u32[]{:S(2)}, u32[]{:S(2)}) collective-permute-start(f32[3,128]{1,0:T(4,128)S(1)} %get-tuple-element.57), channel_id=1, source_target_pairs={{0,8},{1,9},{2,10},{3,11},{4,12},{5,13},{6,14},{7,15},{8,0},{9,1},... | collective-permute-start | bytes 4616 | tf_op jit(solution)/shard_map/ppermute | solution.py:447
  59.9 3.9 %collective-permute-start.4 = (f32[3,128]{1,0:T(4,128)S(1)}, f32[3,128]{1,0:T(4,128)S(1)}, u32[]{:S(2)}, u32[]{:S(2)}) collective-permute-start(f32[3,128]{1,0:T(4,128)S(1)} %get-tuple-element.58), channel_id=1, source_target_pairs={{0,16},{1,17},{2,18},{3,19},{4,20},{5,21},{6,22},{7,23},{8,24},{9,... | collective-permute-start | bytes 4616 | tf_op jit(solution)/shard_map/ppermute | solution.py:447
  70.6 7.3 %collective-permute-start.5 = (f32[3,128]{1,0:T(4,128)S(1)}, f32[3,128]{1,0:T(4,128)S(1)}, u32[]{:S(2)}, u32[]{:S(2)}) collective-permute-start(f32[3,128]{1,0:T(4,128)S(1)} %get-tuple-element.65), channel_id=1, source_target_pairs={{0,1},{1,0},{2,3},{3,2},{4,5},{5,4},{6,7},{7,6},{8,9},{9,8},{10,11... | collective-permute-start | bytes 4616 | tf_op jit(solution)/shard_map/ppermute | solution.py:447
  72.9 5.1 %collective-permute-start.6 = (f32[3,128]{1,0:T(4,128)S(1)}, f32[3,128]{1,0:T(4,128)S(1)}, u32[]{:S(2)}, u32[]{:S(2)}) collective-permute-start(f32[3,128]{1,0:T(4,128)S(1)} %get-tuple-element.66), channel_id=1, source_target_pairs={{0,2},{1,3},{2,0},{3,1},{4,6},{5,7},{6,4},{7,5},{8,10},{9,11},{10,... | collective-permute-start | bytes 4616 | tf_op jit(solution)/shard_map/ppermute | solution.py:447
  72.9 5.1 %collective-permute-start.7 = (f32[3,128]{1,0:T(4,128)S(1)}, f32[3,128]{1,0:T(4,128)S(1)}, u32[]{:S(2)}, u32[]{:S(2)}) collective-permute-start(f32[3,128]{1,0:T(4,128)S(1)} %get-tuple-element.67), channel_id=1, source_target_pairs={{0,4},{1,5},{2,6},{3,7},{4,0},{5,1},{6,2},{7,3},{8,12},{9,13},{10,... | collective-permute-start | bytes 4616 | tf_op jit(solution)/shard_map/ppermute | solution.py:447
  75.6 2.4 %collective-permute-start.8 = (f32[3,128]{1,0:T(4,128)S(1)}, f32[3,128]{1,0:T(4,128)S(1)}, u32[]{:S(2)}, u32[]{:S(2)}) collective-permute-start(f32[3,128]{1,0:T(4,128)S(1)} %get-tuple-element.68), channel_id=1, source_target_pairs={{0,8},{1,9},{2,10},{3,11},{4,12},{5,13},{6,14},{7,15},{8,0},{9,1},... | collective-permute-start | bytes 4616 | tf_op jit(solution)/shard_map/ppermute | solution.py:447
  76.9 3.9 %collective-permute-start.9 = (f32[3,128]{1,0:T(4,128)S(1)}, f32[3,128]{1,0:T(4,128)S(1)}, u32[]{:S(2)}, u32[]{:S(2)}) collective-permute-start(f32[3,128]{1,0:T(4,128)S(1)} %get-tuple-element.69), channel_id=1, source_target_pairs={{0,16},{1,17},{2,18},{3,19},{4,20},{5,21},{6,22},{7,23},{8,24},{9,... | collective-permute-start | bytes 4616 | tf_op jit(solution)/shard_map/ppermute | solution.py:447
  105.0 1.5 %collective-permute-start.10 = (f32[16,128]{1,0:T(8,128)S(1)}, f32[16,128]{1,0:T(8,128)S(1)}, u32[]{:S(2)}, u32[]{:S(2)}) collective-permute-start(f32[16,128]{1,0:T(8,128)S(1)} %get-tuple-element.78), channel_id=1, source_target_pairs={{0,1},{1,0},{2,3},{3,2},{4,5},{5,4},{6,7},{7,6},{8,9},{9,8},{10,11... | collective-permute-start | bytes 24584 | tf_op jit(solution)/shard_map/ppermute | solution.py:447
  123.8 2.9 %collective-permute-start.11 = (f32[80,128]{1,0:T(8,128)S(1)}, f32[80,128]{1,0:T(8,128)S(1)}, u32[]{:S(2)}, u32[]{:S(2)}) collective-permute-start(f32[80,128]{1,0:T(8,128)S(1)} %part_totals.1.mine), channel_id=1, source_target_pairs={{0,1},{1,0},{2,3},{3,2},{4,5},{5,4},{6,7},{7,6},{8,9},{9,8},{10,11... | collective-permute-start | bytes 122888 | tf_op jit(solution)/shard_map/ppermute | solution.py:447

commit v3 on v2

--- a/solution.py
+++ b/solution.py
@@ -146,28 +146,32 @@
     return gather(internal, (0, ROWS, 2 * ROWS), shared[...] & 127, shared[...] >> 7)
 
 
-def slots(slave, owner, master, normal, acc):
+def slots(slave, owner, master, normal, acc, between):
     acc[...] = jnp.zeros_like(acc)
     down = lax.broadcasted_iota(jnp.int32, (LANES, LANES), 0)
     across = lax.broadcasted_iota(jnp.int32, (LANES, LANES), 1)
     before = jnp.where(down < across, 1.0, 0.0).astype(BF)
     carry = jnp.zeros((LANES, 1), F32)
-    for t in range(16):
-        hit = jnp.where(jnp.broadcast_to(owner[t : t + 1, :], (LANES, LANES)) == down, 1.0, 0.0)
-        hitb = hit.astype(BF)
-        count = jnp.dot(hitb, before, preferred_element_type=F32) + carry
-        rank = jnp.sum(hit * count, axis=0, keepdims=True)
-        carry = carry + jnp.sum(hit, axis=1, keepdims=True)
-        mine = jnp.broadcast_to(rank, (64, LANES)) == down[:64].astype(F32)
-        vals = [normal[c : c + 1, t * LANES : (t + 1) * LANES] for c in range(3)]
-        vals += [master[t : t + 1, :].astype(F32), slave[t : t + 1, :].astype(F32)]
-        left = [jnp.broadcast_to(x, (64, LANES)) for x in vals]
-        for s in range(3):
-            piece = [jnp.where(mine, x, 0.0).astype(BF) for x in left]
-            left = [x - x.astype(BF).astype(F32) for x in left]
-            acc[:, 0:320] += lax.dot_general(
-                hitb, jnp.concatenate(piece, 0), NT, preferred_element_type=F32
-            )
+    for pair in range(8):
+        hits, pieces = [], []
+        for t in (2 * pair, 2 * pair + 1):
+            hit = jnp.where(jnp.broadcast_to(owner[t : t + 1, :], (LANES, LANES)) == down, 1.0, 0.0)
+            hitb = hit.astype(BF)
+            count = jnp.dot(hitb, before, preferred_element_type=F32) + carry
+            rank = jnp.sum(hit * count, axis=0, keepdims=True)
+            carry = carry + jnp.sum(hit, axis=1, keepdims=True)
+            mine = jnp.broadcast_to(rank, (64, LANES)) == down[:64].astype(F32)
+            vals = [normal[c : c + 1, t * LANES : (t + 1) * LANES] for c in range(3)]
+            vals += [master[t : t + 1, :].astype(F32), slave[t : t + 1, :].astype(F32)]
+            left = [jnp.broadcast_to(x, (64, LANES)) for x in vals]
+            for s in range(3):
+                hits.append(hitb)
+                pieces.append(jnp.concatenate([jnp.where(mine, x, 0.0).astype(BF) for x in left], 0))
+                left = [x - x.astype(BF).astype(F32) for x in left]
+        between(pair)
+        acc[:, 0:320] += lax.dot_general(
+            jnp.concatenate(hits, 1), jnp.concatenate(pieces, 1), NT, preferred_element_type=F32
+        )
 
 
 def spans():
@@ -192,12 +196,13 @@
     for copy in copies:
         copy.start()
     small[...] = jnp.zeros_like(small)
-    copies[0].wait()
-    for m in range(8):
+    for copy in copies:
+        copy.wait()
+
+    def columns(m):
         for j in range(24):
             cols[m * 24 + j] = jnp.broadcast_to(stiff[m, :, j : j + 1], (24, LANES))
-    for copy in copies[1:]:
-        copy.wait()
+
     to_rows(disp0, u)
     to_rows(vel0, v)
     to_rows(force0, fm)
@@ -225,7 +230,7 @@
         for c in range(3):
             rigid[8 + 8 * c + h : 9 + 8 * c + h, 0:n] = pcenter[c : c + 1, at]
             rigid[32 + 8 * c + h : 33 + 8 * c + h, 0:n] = pinertia[c : c + 1, at]
-    slots(slave, owner, master, normal, table)
+    slots(slave, owner, master, normal, table, columns)
     send[:, 0:256] = table[:, 0:256]
     sidx[...] = table[:, 256:384]
     send[:, 256:640] = jnp.zeros((LANES, 384), F32)
@@ -538,7 +543,7 @@
             pltpu.VMEM((LANES, 3 * LANES), F32),
             pltpu.SemaphoreType.DMA((18,)),
         ],
-    )(*inputs)
+    )(*[pltpu.with_memory_space_constraint(x, pltpu.HBM) for x in inputs])
     got = swap(send)
     recv = [got]
     for n in range(CYCLES - 1):

time: 128 us -> 111 us (0.87)
  local copies, waits for them, and re-layouts: 14.1 us -> 0.58 us
  Pallas kernels: 34.6 us -> 31.8 us
    unnamed x38 -> x4, local copies, waits for them, and re-layouts: 13.5 us -> 0.04 us
    pallas_call x1, Pallas kernels: 12.3 us -> 9.52 us  [per_device(): call(first_kernel, [state, state, state, rows, state, ((8, 4096), ints),...]
where the time goes in v3:
time: 111 us
  blocking collectives  56.1 us (51%)
  Pallas kernels  31.8 us (29%)
  starting transfers between devices  14.5 us (13%)
  waiting for transfers between devices  7.44 us (7%)
    all_to_all x3, blocking collectives, swap(): lax.all_to_all(block, 'dom', 0, 0, tiled=True, axis_index_groups=groups)  56.1 us
    ppermute x12, starting transfers between devices, partner(): lax.ppermute(block, 'dom', [(i, i ^ 1 << apart) for i in range(count)])  14.5 us
    pallas_call x2, Pallas kernels, per_device(): call(functools.partial(next_kernel, n == 0), [state, state, state, *own],...  13.5 us
    pallas_call x1, Pallas kernels, per_device(): call(first_kernel, [state, state, state, rows, state, ((8, 4096), ints),...  9.52 us
    ppermute x12, waiting for transfers between devices, partner(): lax.ppermute(block, 'dom', [(i, i ^ 1 << apart) for i in range(count)])  7.44 us
    pallas_call x1, Pallas kernels, per_device(): call(dots_kernel, [state, state, state, trio, ((LANES, LANES), ints), ((3...  4.53 us
    pallas_call x1, Pallas kernels, per_device(): call(contact_kernel, [((3, 4096), F32), half, half], [VMEM] * 9, 'contact...  3.44 us
  transfers between devices with their start and end apart: 12, of which 7 were waited for; matrix products, arithmetic and copies ran while one was open for 0% of the time, Pallas kernels for 0%

profile of v3, /device:TPU:1, one launch (start us, length us, event | category | flops | bytes accessed | tf_op | source)
XLA Modules:
  0.0 111.1 jit_solution(2709923996315128975)
XLA Ops:
  0.6 0.0 copy-start
  0.6 9.5 %first_cycle.1 = (f32[96,128]{1,0:T(8,128)S(1)}, f32[96,128]{1,0:T(8,128)S(1)}, f32[96,128]{1,0:T(8,128)S(1)}, f32[32,128]{1,0:T(8,128)S(1)}, f32[96,128]{1,0:T(...) custom-call(f32[8,24,24]{2,1,0:T(8,128)} %refs_0_.1, ...), custom_call_target="tpu_custom_call" | custom-call | bytes 1048576 | tf_op jit(solution)/shard_map/first_cycle/pallas_call | solution.py:509
  10.2 0.3 copy.20
  10.5 22.9 %all_to_all.33 = f32[128,1,640]{2,1,0:T(1,128)S(1)} all-to-all(f32[128,1,640]{2,1,0:T(1,128)S(1)} %copy.20), channel_id=1, replica_groups=mesh['dom'=128] {'dom'}, dimensions={0} | all-to-all | bytes 655360 | tf_op jit(solution)/shard_map/all_to_all | solution.py:456
  33.5 0.0 copy-done
  33.5 6.7 %next_cycle.2 = (f32[96,128]{1,0:T(8,128)S(1)}, f32[96,128]{1,0:T(8,128)S(1)}, f32[96,128]{1,0:T(8,128)S(1)}, f32[3,128]{1,0:T(4,128)S(1)}, f32[3,128]{1,0:T(4,1...) custom-call(f32[96,128]{1,0:T(8,128)S(1)} %get-tuple-element.41.u, ...), custom_call_target="tpu_custom_call" | custom-call | bytes 1048576 | tf_op jit(solution)/shard_map/next_cycle/pallas_call | solution.py:550
  40.2 1.0 collective-permute-start
  41.1 0.3 collective-permute-start.1
  41.5 1.6 %collective-permute-start.2 = (f32[3,128]{1,0:T(4,128)S(1)}, f32[3,128]{1,0:T(4,128)S(1)}, u32[]{:S(2)}, u32[]{:S(2)}) collective-permute-start(f32[3,128]{1,0:T(4,128)S(1)} %get-tuple-element.56), channel_id=1, source_target_pairs={{0,4},{1,5},{2,6},{3,7},{4,0},{5,1},{6,2},{7,3},{8,12},{9,13},{10,... | collective-permute-start | bytes 4616 | tf_op jit(solution)/shard_map/ppermute | solution.py:452
  43.1 0.6 collective-permute-start.3
  43.6 1.1 collective-permute-start.4
  44.7 0.0 collective-permute-done.rest_0_
  44.7 0.0 collective-permute-done.1.rest_1_
  44.7 0.7 collective-permute-done.2.rest_2_
  45.4 0.4 collective-permute-done.3.rest_3_
  45.8 1.8 %collective-permute-done.4.rest_4_ = f32[3,128]{1,0:T(4,128)S(1)} collective-permute-done((f32[3,128]{1,0:T(4,128)S(1)}, f32[3,128]{1,0:T(4,128)S(1)}, u32[]{:S(2)}, u32[]{:S(2)}) %collective-permute-start.4) | collective-permute-done | bytes 1568 | tf_op jit(solution)/shard_map/ppermute | solution.py:452
  47.6 6.8 %next_cycle.3 = (f32[96,128]{1,0:T(8,128)S(1)}, f32[96,128]{1,0:T(8,128)S(1)}, f32[96,128]{1,0:T(8,128)S(1)}, f32[3,128]{1,0:T(4,128)S(1)}, f32[3,128]{1,0:T(4,1...) custom-call(f32[96,128]{1,0:T(8,128)S(1)} %get-tuple-element.51.u, ...), custom_call_target="tpu_custom_call" | custom-call | bytes 1048576 | tf_op jit(solution)/shard_map/next_cycle/pallas_call | solution.py:550
  54.4 2.2 %collective-permute-start.5 = (f32[3,128]{1,0:T(4,128)S(1)}, f32[3,128]{1,0:T(4,128)S(1)}, u32[]{:S(2)}, u32[]{:S(2)}) collective-permute-start(f32[3,128]{1,0:T(4,128)S(1)} %get-tuple-element.65), channel_id=1, source_target_pairs={{0,1},{1,0},{2,3},{3,2},{4,5},{5,4},{6,7},{7,6},{8,9},{9,8},{10,11... | collective-permute-start | bytes 4616 | tf_op jit(solution)/shard_map/ppermute | solution.py:452
  56.6 0.0 collective-permute-start.6
  56.6 2.8 %collective-permute-start.7 = (f32[3,128]{1,0:T(4,128)S(1)}, f32[3,128]{1,0:T(4,128)S(1)}, u32[]{:S(2)}, u32[]{:S(2)}) collective-permute-start(f32[3,128]{1,0:T(4,128)S(1)} %get-tuple-element.67), channel_id=1, source_target_pairs={{0,4},{1,5},{2,6},{3,7},{4,0},{5,1},{6,2},{7,3},{8,12},{9,13},{10,... | collective-permute-start | bytes 4616 | tf_op jit(solution)/shard_map/ppermute | solution.py:452
  59.4 1.2 %collective-permute-start.8 = (f32[3,128]{1,0:T(4,128)S(1)}, f32[3,128]{1,0:T(4,128)S(1)}, u32[]{:S(2)}, u32[]{:S(2)}) collective-permute-start(f32[3,128]{1,0:T(4,128)S(1)} %get-tuple-element.68), channel_id=1, source_target_pairs={{0,8},{1,9},{2,10},{3,11},{4,12},{5,13},{6,14},{7,15},{8,0},{9,1},... | collective-permute-start | bytes 4616 | tf_op jit(solution)/shard_map/ppermute | solution.py:452
  60.6 1.1 collective-permute-start.9
  61.6 0.0 collective-permute-done.5.rest_0_
  61.6 0.0 collective-permute-done.6.rest_1_
  61.7 0.0 collective-permute-done.7.rest_2_
  61.7 0.1 collective-permute-done.8.rest_3_
  61.8 2.7 %collective-permute-done.9.rest_4_ = f32[3,128]{1,0:T(4,128)S(1)} collective-permute-done((f32[3,128]{1,0:T(4,128)S(1)}, f32[3,128]{1,0:T(4,128)S(1)}, u32[]{:S(2)}, u32[]{:S(2)}) %collective-permute-start.9) | collective-permute-done | bytes 1568 | tf_op jit(solution)/shard_map/ppermute | solution.py:452
  64.5 4.5 %contact_dots.1 = (f32[96,128]{1,0:T(8,128)S(1)}, f32[96,128]{1,0:T(8,128)S(1)}, f32[96,128]{1,0:T(8,128)S(1)}, f32[128,384]{1,0:T(8,128)S(1)}, s32[128,128]{1,0:T(8,128)S(1)}, /*index=5*/f32[3,128,128]{2,1,0:T(8,128)S(1)}) custom-call(f32[96,128]{1,0:T(8,128)S(1)} %get-tuple-element.59.u, f32[96,128]{1,0:T(8,128)S(1)} %get-tuple-element.60.v, ...), custom_call_target="tpu_custom_call" | custom-call | bytes 1048576 | tf_op jit(solution)/shard_map/contact_dots/pallas_call | solution.py:560
  69.1 0.2 copy.21
  69.3 16.0 %all_to_all.34 = f32[128,1,384]{2,1,0:T(1,128)S(1)} all-to-all(f32[128,1,384]{2,1,0:T(1,128)S(1)} %copy.21), channel_id=1, replica_groups=mesh['dom'=128] {'dom'}, dimensions={0} | all-to-all | bytes 393216 | tf_op jit(solution)/shard_map/all_to_all | solution.py:456
  85.3 3.4 %contact_forces.1 = (f32[3,4096]{1,0:T(4,128)}, f32[16,128]{1,0:T(8,128)S(1)}, f32[16,128]{1,0:T(8,128)S(1)}) custom-call(f32[128,384]{1,0:T(8,128)S(1)} %get-tuple-element.70.dots, f32[128,384]{1,0:T(8,128)S(1)} %bitcast.23, s32[128,128]{1,0:T(8,128)S(1)} %get-tuple-element.71.idx, f32[3,128,128]{2,1,0:T(8,128)S(1)} %get-tuple-element.72.nrm, ...), custom_call_target="tpu_custom_call" | custom-call | bytes 1048576 | tf_op jit(solution)/shard_map/contact_forces/pallas_call | solution.py:568
  88.7 0.7 collective-permute-start.10
  89.4 0.8 collective-permute-done.10.given
  90.3 17.2 %all_to_all.35 = f32[64,16,128]{2,1,0:T(8,128)S(1)} all-to-all(f32[64,16,128]{2,1,0:T(8,128)S(1)} %bitcast.19), channel_id=1, replica_groups={{0,2,4,6,8,10,12,14,16,18,20,22,24,26,28,30,32,34,36,38,40,42,44,46,48,..., dimensions={0} | all-to-all | bytes 1048576 | tf_op jit(solution)/shard_map/all_to_all | solution.py:456
  107.5 0.1 part_totals.1.mine
  107.5 2.0 %collective-permute-start.11 = (f32[80,128]{1,0:T(8,128)S(1)}, f32[80,128]{1,0:T(8,128)S(1)}, u32[]{:S(2)}, u32[]{:S(2)}) collective-permute-start(f32[80,128]{1,0:T(8,128)S(1)} %part_totals.1.mine), channel_id=1, source_target_pairs={{0,1},{1,0},{2,3},{3,2},{4,5},{5,4},{6,7},{7,6},{8,9},{9,8},{10,11... | collective-permute-start | bytes 122888 | tf_op jit(solution)/shard_map/ppermute | solution.py:452
  109.5 0.9 collective-permute-done.11.other
  110.4 0.7 part_motion.1
  (3 shorter events, 0.1 us)
Async XLA Ops:
  0.6 32.8 %copy-start = (s32[32]{0:T(128)S(1)}, s32[32]{0:T(128)}, u32[]{:S(2)}) copy-start(s32[32]{0:T(128)} %mat.3) | copy-start | bytes 388
  40.2 4.5 %collective-permute-start = (f32[3,128]{1,0:T(4,128)S(1)}, f32[3,128]{1,0:T(4,128)S(1)}, u32[]{:S(2)}, u32[]{:S(2)}) collective-permute-start(f32[3,128]{1,0:T(4,128)S(1)} %get-tuple-element.54), channel_id=1, source_target_pairs={{0,1},{1,0},{2,3},{3,2},{4,5},{5,4},{6,7},{7,6},{8,9},{9,8},{10,11... | collective-permute-start | bytes 4616 | tf_op jit(solution)/shard_map/ppermute | solution.py:452
  41.1 3.5 %collective-permute-start.1 = (f32[3,128]{1,0:T(4,128)S(1)}, f32[3,128]{1,0:T(4,128)S(1)}, u32[]{:S(2)}, u32[]{:S(2)}) collective-permute-start(f32[3,128]{1,0:T(4,128)S(1)} %get-tuple-element.55), channel_id=1, source_target_pairs={{0,2},{1,3},{2,0},{3,1},{4,6},{5,7},{6,4},{7,5},{8,10},{9,11},{10,... | collective-permute-start | bytes 4616 | tf_op jit(solution)/shard_map/ppermute | solution.py:452
  41.5 3.9 %collective-permute-start.2 = (f32[3,128]{1,0:T(4,128)S(1)}, f32[3,128]{1,0:T(4,128)S(1)}, u32[]{:S(2)}, u32[]{:S(2)}) collective-permute-start(f32[3,128]{1,0:T(4,128)S(1)} %get-tuple-element.56), channel_id=1, source_target_pairs={{0,4},{1,5},{2,6},{3,7},{4,0},{5,1},{6,2},{7,3},{8,12},{9,13},{10,... | collective-permute-start | bytes 4616 | tf_op jit(solution)/shard_map/ppermute | solution.py:452
  43.1 2.7 %collective-permute-start.3 = (f32[3,128]{1,0:T(4,128)S(1)}, f32[3,128]{1,0:T(4,128)S(1)}, u32[]{:S(2)}, u32[]{:S(2)}) collective-permute-start(f32[3,128]{1,0:T(4,128)S(1)} %get-tuple-element.57), channel_id=1, source_target_pairs={{0,8},{1,9},{2,10},{3,11},{4,12},{5,13},{6,14},{7,15},{8,0},{9,1},... | collective-permute-start | bytes 4616 | tf_op jit(solution)/shard_map/ppermute | solution.py:452
  43.6 3.9 %collective-permute-start.4 = (f32[3,128]{1,0:T(4,128)S(1)}, f32[3,128]{1,0:T(4,128)S(1)}, u32[]{:S(2)}, u32[]{:S(2)}) collective-permute-start(f32[3,128]{1,0:T(4,128)S(1)} %get-tuple-element.58), channel_id=1, source_target_pairs={{0,16},{1,17},{2,18},{3,19},{4,20},{5,21},{6,22},{7,23},{8,24},{9,... | collective-permute-start | bytes 4616 | tf_op jit(solution)/shard_map/ppermute | solution.py:452
  54.4 7.3 %collective-permute-start.5 = (f32[3,128]{1,0:T(4,128)S(1)}, f32[3,128]{1,0:T(4,128)S(1)}, u32[]{:S(2)}, u32[]{:S(2)}) collective-permute-start(f32[3,128]{1,0:T(4,128)S(1)} %get-tuple-element.65), channel_id=1, source_target_pairs={{0,1},{1,0},{2,3},{3,2},{4,5},{5,4},{6,7},{7,6},{8,9},{9,8},{10,11... | collective-permute-start | bytes 4616 | tf_op jit(solution)/shard_map/ppermute | solution.py:452
  56.6 5.1 %collective-permute-start.6 = (f32[3,128]{1,0:T(4,128)S(1)}, f32[3,128]{1,0:T(4,128)S(1)}, u32[]{:S(2)}, u32[]{:S(2)}) collective-permute-start(f32[3,128]{1,0:T(4,128)S(1)} %get-tuple-element.66), channel_id=1, source_target_pairs={{0,2},{1,3},{2,0},{3,1},{4,6},{5,7},{6,4},{7,5},{8,10},{9,11},{10,... | collective-permute-start | bytes 4616 | tf_op jit(solution)/shard_map/ppermute | solution.py:452
  56.6 5.1 %collective-permute-start.7 = (f32[3,128]{1,0:T(4,128)S(1)}, f32[3,128]{1,0:T(4,128)S(1)}, u32[]{:S(2)}, u32[]{:S(2)}) collective-permute-start(f32[3,128]{1,0:T(4,128)S(1)} %get-tuple-element.67), channel_id=1, source_target_pairs={{0,4},{1,5},{2,6},{3,7},{4,0},{5,1},{6,2},{7,3},{8,12},{9,13},{10,... | collective-permute-start | bytes 4616 | tf_op jit(solution)/shard_map/ppermute | solution.py:452
  59.4 2.4 %collective-permute-start.8 = (f32[3,128]{1,0:T(4,128)S(1)}, f32[3,128]{1,0:T(4,128)S(1)}, u32[]{:S(2)}, u32[]{:S(2)}) collective-permute-start(f32[3,128]{1,0:T(4,128)S(1)} %get-tuple-element.68), channel_id=1, source_target_pairs={{0,8},{1,9},{2,10},{3,11},{4,12},{5,13},{6,14},{7,15},{8,0},{9,1},... | collective-permute-start | bytes 4616 | tf_op jit(solution)/shard_map/ppermute | solution.py:452
  60.6 3.9 %collective-permute-start.9 = (f32[3,128]{1,0:T(4,128)S(1)}, f32[3,128]{1,0:T(4,128)S(1)}, u32[]{:S(2)}, u32[]{:S(2)}) collective-permute-start(f32[3,128]{1,0:T(4,128)S(1)} %get-tuple-element.69), channel_id=1, source_target_pairs={{0,16},{1,17},{2,18},{3,19},{4,20},{5,21},{6,22},{7,23},{8,24},{9,... | collective-permute-start | bytes 4616 | tf_op jit(solution)/shard_map/ppermute | solution.py:452
  88.7 1.5 %collective-permute-start.10 = (f32[16,128]{1,0:T(8,128)S(1)}, f32[16,128]{1,0:T(8,128)S(1)}, u32[]{:S(2)}, u32[]{:S(2)}) collective-permute-start(f32[16,128]{1,0:T(8,128)S(1)} %get-tuple-element.78), channel_id=1, source_target_pairs={{0,1},{1,0},{2,3},{3,2},{4,5},{5,4},{6,7},{7,6},{8,9},{9,8},{10,11... | collective-permute-start | bytes 24584 | tf_op jit(solution)/shard_map/ppermute | solution.py:452
  107.5 2.9 %collective-permute-start.11 = (f32[80,128]{1,0:T(8,128)S(1)}, f32[80,128]{1,0:T(8,128)S(1)}, u32[]{:S(2)}, u32[]{:S(2)}) collective-permute-start(f32[80,128]{1,0:T(8,128)S(1)} %part_totals.1.mine), channel_id=1, source_target_pairs={{0,1},{1,0},{2,3},{3,2},{4,5},{5,4},{6,7},{7,6},{8,9},{9,8},{10,11... | collective-permute-start | bytes 122888 | tf_op jit(solution)/shard_map/ppermute | solution.py:452

commit v4 on v3

--- a/solution.py
+++ b/solution.py
@@ -46,9 +46,9 @@
     return jnp.take_along_axis(row, idx, axis=1, mode="promise_in_bounds")
 
 
-def gather(tab, bases, lo, hi):
+def gather(tab, bases, lo, hi, rows=ROWS):
     acc = [None] * len(bases)
-    for h in range(ROWS):
+    for h in range(rows):
         here = hi == h
         for c, base in enumerate(bases):
             row = jnp.broadcast_to(tab[base + h : base + h + 1, :], (8, LANES))
@@ -146,7 +146,23 @@
     return gather(internal, (0, ROWS, 2 * ROWS), shared[...] & 127, shared[...] >> 7)
 
 
-def slots(slave, owner, master, normal, acc, between):
+def slotted(hitb, rank, vals):
+    rows = lax.broadcasted_iota(jnp.int32, (64, LANES), 0).astype(F32)
+    mine = jnp.broadcast_to(rank, (64, LANES)) == rows
+    left = [jnp.broadcast_to(x, (64, LANES)) for x in vals]
+    pieces = []
+    for s in range(3):
+        pieces.append(jnp.concatenate([jnp.where(mine, x, 0.0).astype(BF) for x in left], 0))
+        left = [x - x.astype(BF).astype(F32) for x in left]
+    return [hitb] * 3, pieces
+
+
+def hits_of(owner_row):
+    down = lax.broadcasted_iota(jnp.int32, (LANES, LANES), 0)
+    return jnp.where(jnp.broadcast_to(owner_row, (LANES, LANES)) == down, 1.0, 0.0)
+
+
+def slots(owner, master, normal, slot, acc, between):
     acc[...] = jnp.zeros_like(acc)
     down = lax.broadcasted_iota(jnp.int32, (LANES, LANES), 0)
     across = lax.broadcasted_iota(jnp.int32, (LANES, LANES), 1)
@@ -155,21 +171,18 @@
     for pair in range(8):
         hits, pieces = [], []
         for t in (2 * pair, 2 * pair + 1):
-            hit = jnp.where(jnp.broadcast_to(owner[t : t + 1, :], (LANES, LANES)) == down, 1.0, 0.0)
+            hit = hits_of(owner[t : t + 1, :])
             hitb = hit.astype(BF)
             count = jnp.dot(hitb, before, preferred_element_type=F32) + carry
             rank = jnp.sum(hit * count, axis=0, keepdims=True)
             carry = carry + jnp.sum(hit, axis=1, keepdims=True)
-            mine = jnp.broadcast_to(rank, (64, LANES)) == down[:64].astype(F32)
+            slot[t : t + 1, :] = owner[t : t + 1, :] * 64 + rank.astype(jnp.int32)
             vals = [normal[c : c + 1, t * LANES : (t + 1) * LANES] for c in range(3)]
-            vals += [master[t : t + 1, :].astype(F32), slave[t : t + 1, :].astype(F32)]
-            left = [jnp.broadcast_to(x, (64, LANES)) for x in vals]
-            for s in range(3):
-                hits.append(hitb)
-                pieces.append(jnp.concatenate([jnp.where(mine, x, 0.0).astype(BF) for x in left], 0))
-                left = [x - x.astype(BF).astype(F32) for x in left]
+            one, two = slotted(hitb, rank, [*vals, master[t : t + 1, :].astype(F32)])
+            hits += one
+            pieces += two
         between(pair)
-        acc[:, 0:320] += lax.dot_general(
+        acc[...] += lax.dot_general(
             jnp.concatenate(hits, 1), jnp.concatenate(pieces, 1), NT, preferred_element_type=F32
         )
 
@@ -185,11 +198,11 @@
 
 def first_kernel(*refs):
     srcs = refs[:18]
-    (u, v, fm, mass, pos, idx, inv, cols, part, shared, internal, send, sidx, rigid) = refs[18:32]
-    work = refs[32:]
-    (disp0, vel0, force0, pos0, shared0, slave, owner, master, normal, stiff) = work[:10]
-    pmass, pcenter, pinertia, mat, accel, conn = work[10:16]
-    tab, g, acc, small, table, sems = work[16:]
+    (u, v, fm, mass, pos, idx, inv, cols, part, shared, internal, send, slave, slot, nrm, rigid) = refs[18:34]
+    work = refs[34:]
+    (disp0, vel0, force0, pos0, shared0, owner, master, normal, stiff) = work[:9]
+    pmass, pcenter, pinertia, mat, accel, conn = work[9:15]
+    tab, g, acc, small, table, sems = work[15:]
     dsts = (stiff, disp0, vel0, conn, mat, shared0, force0, mass, accel, slave, owner, master, normal)
     dsts = dsts + (pos0, part, pmass, pcenter, pinertia)
     copies = [pltpu.make_async_copy(a, b, sems.at[i]) for i, (a, b) in enumerate(zip(srcs, dsts))]
@@ -230,9 +243,11 @@
         for c in range(3):
             rigid[8 + 8 * c + h : 9 + 8 * c + h, 0:n] = pcenter[c : c + 1, at]
             rigid[32 + 8 * c + h : 33 + 8 * c + h, 0:n] = pinertia[c : c + 1, at]
-    slots(slave, owner, master, normal, table, columns)
-    send[:, 0:256] = table[:, 0:256]
-    sidx[...] = table[:, 256:384]
+    for t in range(16):
+        for c in range(3):
+            nrm[16 * c + t : 16 * c + t + 1, :] = normal[c : c + 1, t * LANES : (t + 1) * LANES]
+    slots(owner, master, normal, slot, table, columns)
+    send[:, 0:256] = table[...]
     send[:, 256:640] = jnp.zeros((LANES, 384), F32)
     elements(idx, mat, tab, cols, g, acc)
     own = finish_internal(acc, internal, shared)
@@ -288,9 +303,9 @@
             own[b][c : c + 1, :] = vals[c][b : b + 1, :]
 
 
-def dots_kernel(u, v, internal, inv, fm, mass, pos, part, send, sidx, got, *rest):
+def dots_kernel(u, v, internal, inv, fm, mass, pos, part, slave, slot, nrm, got, *rest):
     recv = rows_of(rest[:5])
-    x2, v2, net, dots, idx, nrm, tab, acc = rest[5:]
+    x2, v2, net, dots, midx, mnrm, tab, acc, table, ab, dense = rest[5:]
     for c in range(3):
         for r in range(0, ROWS, 8):
             at, disp, speed, total = update(u, v, internal, inv, fm, mass, recv, c, r)
@@ -300,34 +315,53 @@
             net[at, :] = mass[r : r + 8, :] * fm[at, :] - total
             tab[at, :] = place_now
             tab[c * ROWS + 96 + r : c * ROWS + 96 + r + 8, :] = speed
-    left = lax.broadcasted_iota(jnp.int32, (LANES, LANES), 1) < 64
-    own0, own1 = send[:, 0:128], send[:, 128:256]
-    got0, got1 = got[:, 0:128], got[:, 128:256]
-    nrm[0] = jnp.where(left, own0, pltpu.roll(got0, 64, 1))
-    nrm[1] = jnp.where(left, pltpu.roll(own0, 64, 1), got0)
-    nrm[2] = jnp.where(left, own1, pltpu.roll(got1, 64, 1))
-    idx[...] = jnp.where(left, sidx[...], got1).astype(jnp.int32)
+    left = lax.broadcasted_iota(jnp.int32, (64, LANES), 1) < 64
+    for k, out in ((0, mnrm.at[0]), (1, mnrm.at[1]), (2, mnrm.at[2]), (3, midx)):
+        at = slice(LANES * (k // 2), LANES * (k // 2) + LANES)
+        top, low = got[0:64, at], got[64:128, at]
+        if k % 2:
+            out[...] = jnp.where(left, pltpu.roll(top, 64, 1), low).astype(out.dtype)
+        else:
+            out[...] = jnp.where(left, top, pltpu.roll(low, 64, 1))
 
     def vals(r):
         m = mass[r : r + 8, :]
         return [m, *[m * tab[c * ROWS + r : c * ROWS + r + 8, :] for c in range(3)]]
 
+    def both(here, w):
+        y = gather(tab, tuple(range(0, 192, ROWS)), here & 127, here >> 7)
+        return y[0] * w[0] + y[1] * w[1] + y[2] * w[2], y[3] * w[0] + y[4] * w[1] + y[5] * w[2]
+
+    for r in (0, 8):
+        w = [nrm[16 * c + r : 16 * c + r + 8, :] for c in range(3)]
+        ab[r : r + 8, :], ab[16 + r : 24 + r, :] = both(slave[r : r + 8, :], w)
     acc[...] = jnp.zeros_like(acc)
     part_sums(part, vals, acc, True)
     moments = jnp.concatenate([acc[0:32, :] + acc[32:64, :], jnp.zeros((96, LANES), F32)], 0)
     dots[:, 256:384] = moments.T
+    table[...] = jnp.zeros_like(table)
 
     def step(i, carry):
         for q in range(2):
-            off = pl.multiple_of(i * 16 + q * 8, 8)
-            here = idx[pl.ds(off, 8), :]
-            vals = gather(tab, tuple(range(0, 192, ROWS)), here & 127, here >> 7)
-            w = [nrm[c, pl.ds(off, 8), :] for c in range(3)]
-            dots[pl.ds(off, 8), 0:128] = vals[0] * w[0] + vals[1] * w[1] + vals[2] * w[2]
-            dots[pl.ds(off, 8), 128:256] = vals[3] * w[0] + vals[4] * w[1] + vals[5] * w[2]
+            at = pl.ds(pl.multiple_of(i * 16 + q * 8, 8), 8)
+            dense[0, at, :], dense[1, at, :] = both(midx[at, :], [mnrm[c, at, :] for c in range(3)])
+        hits, pieces = [], []
+        for q in range(4):
+            at = pl.ds(i * 4 + q, 1)
+            here = slot[at, :]
+            rows = [ab[at, :], ab[pl.ds(16 + i * 4 + q, 1), :]]
+            one, two = slotted(hits_of(here >> 6).astype(BF), (here & 63).astype(F32), rows)
+            hits += one
+            pieces += two
+        table[...] += lax.dot_general(
+            jnp.concatenate(hits, 1), jnp.concatenate(pieces, 1), NT, preferred_element_type=F32
+        )
         return carry
 
-    lax.fori_loop(0, 8, step, 0)
+    lax.fori_loop(0, 4, step, 0)
+    dots[:, 0:128] = table[...]
+    dots[0:64, 128:256] = jnp.where(left, dense[0], pltpu.roll(dense[1], 64, 1))
+    dots[64:128, 128:256] = jnp.where(left, pltpu.roll(dense[0], 64, 1), dense[1])
 
 
 def part_sums(part, vals, acc, by_device):
@@ -358,30 +392,47 @@
         )
 
 
-def contact_kernel(dots, got, idx, nrm, x, v, net, mass, part, nodal, keep, give, acc, tot, acc2):
+def contact_kernel(
+    dots, got, slave, slot, nrm, midx, mnrm, x, v, net, mass, part, nodal, keep, give, acc, tot, acc2, push, mine
+):
     acc[...] = jnp.zeros_like(acc)
     acc2[...] = jnp.zeros_like(acc2)
-    sign = jnp.where(lax.broadcasted_iota(jnp.int32, (8, LANES), 1) < 64, 1.0, -1.0)
+    left = lax.broadcasted_iota(jnp.int32, (LANES, LANES), 1) < 64
+    as_slave = dots[:, 0:128] - got[:, 128:256]
+    as_master = got[:, 0:128] - dots[:, 128:256]
+    gap = jnp.where(left, as_slave, pltpu.roll(as_master, 64, 1))
+    closing = jnp.where(left, pltpu.roll(as_slave, 64, 1), as_master)
+    z = -gap / GAP_WIDTH
+    soft = jnp.maximum(z, 0.0) + jnp.log1p(jnp.exp(-jnp.abs(z)))
+    size = PENALTY * GAP_WIDTH * soft - CONTACT_DAMP * closing
+    top, low = size[0:64, :], size[64:128, :]
+    mine[...] = jnp.where(left[0:64, :], top, pltpu.roll(low, 64, 1))
+    push[...] = -jnp.where(left[0:64, :], pltpu.roll(top, 64, 1), low)
 
     def step(i, carry):
-        left, right = [], []
+        one, two = [], []
         for q in range(4):
             at = pl.ds(pl.multiple_of(i * 32 + q * 8, 8), 8)
-            gap = sign * (dots[at, 0:128] - pltpu.roll(got[at, 0:128], 64, 1))
-            closing = sign * (dots[at, 128:256] - pltpu.roll(got[at, 128:256], 64, 1))
-            z = -gap / GAP_WIDTH
-            soft = jnp.maximum(z, 0.0) + jnp.log1p(jnp.exp(-jnp.abs(z)))
-            push = sign * (PENALTY * GAP_WIDTH * soft - CONTACT_DAMP * closing)
-            here = idx[at, :]
-            one, two = place(here & 127, here >> 7, [push * nrm[c, at, :] for c in range(3)])
-            left.append(one)
-            right.append(two)
+            here, size = midx[at, :], push[at, :]
+            pair = place(here & 127, here >> 7, [size * mnrm[c, at, :] for c in range(3)])
+            one.append(pair[0])
+            two.append(pair[1])
         acc[...] += lax.dot_general(
-            jnp.concatenate(left, 1), jnp.concatenate(right, 1), NT, preferred_element_type=F32
+            jnp.concatenate(one, 1), jnp.concatenate(two, 1), NT, preferred_element_type=F32
         )
         return carry
 
-    lax.fori_loop(0, 4, step, 0)
+    lax.fori_loop(0, 2, step, 0)
+    one, two = [], []
+    for r in (0, 8):
+        here, at = slave[r : r + 8, :], slot[r : r + 8, :]
+        (size,) = gather(mine, (0,), ((at >> 12) << 6) + (at & 63), (at >> 6) & 63, 64)
+        pair = place(here & 127, here >> 7, [size * nrm[16 * c + r : 16 * c + r + 8, :] for c in range(3)])
+        one.append(pair[0])
+        two.append(pair[1])
+    acc[...] += lax.dot_general(
+        jnp.concatenate(one, 1), jnp.concatenate(two, 1), NT, preferred_element_type=F32
+    )
     contact = acc[0:96, :] + acc[96:192, :]
     tot[...] = net[...] + contact
     for c in range(3):
@@ -401,29 +452,36 @@
 
     part_sums(part, vals, acc2, False)
     acc2[0:48, :] = acc2[0:48, :] + acc2[48:96, :]
+    lane = lax.broadcasted_iota(jnp.int32, (8, LANES), 1)
+    last = jnp.zeros((8, LANES), F32)
+    for k in range(6):
+        piece = jnp.where(lane < 16, acc2[8 * k : 8 * k + 8, :], 0.0)
+        last = last + (pltpu.roll(piece, 16 * k, 1) if k else piece)
     even = lax.axis_index("dom") & 1 == 0
-    for k in range(6):
-        low, high = acc2[8 * k : 8 * k + 2, :], acc2[8 * k + 2 : 8 * k + 4, :]
-        keep[2 * k : 2 * k + 2, :] = jnp.where(even, low, high)
-        give[2 * k : 2 * k + 2, :] = jnp.where(even, high, low)
-    keep[12:16, :] = jnp.zeros((4, LANES), F32)
-    give[12:16, :] = jnp.zeros((4, LANES), F32)
-    keep[12:13, :] = jnp.sum(got[:, 256:384], axis=0, keepdims=True)
+    pairs = [(acc2[8 * k : 8 * k + 1, :], acc2[8 * k + 2 : 8 * k + 3, :]) for k in range(6)]
+    pairs += [(acc2[8 * k + 1 : 8 * k + 2, :], acc2[8 * k + 25 : 8 * k + 26, :]) for k in range(3)]
+    pairs += [(jnp.zeros((1, LANES), F32), last[3:4, :])]
+    for k, (low, high) in enumerate(pairs):
+        keep[k : k + 1, :] = jnp.where(even, low, high)
+        give[k : k + 1, :] = jnp.where(even, high, low)
+    keep[10:16, :] = jnp.zeros((6, LANES), F32)
+    give[10:16, :] = jnp.zeros((6, LANES), F32)
+    moments = jnp.broadcast_to(jnp.sum(got[:, 256:384], axis=0, keepdims=True), (8, LANES))
+    moments = jnp.where(lane < 96, 0.0, pltpu.roll(moments, 96, 1))
+    keep[9:10, :] = keep[9:10, :] + moments[0:1, :]
 
 
 def spread_kernel(keep, given, out):
     tile = keep[...] + given[...]
-    for k in range(64):
-        out[16 * k : 16 * k + 16, :] = tile
+    for k in range(10):
+        out[:, k * LANES : (k + 1) * LANES] = jnp.broadcast_to(tile[k : k + 1, :], (64, LANES))
 
 
 def total_kernel(got, out):
-    total = got[0:16, :]
-    for k in range(1, 64):
-        total = total + got[16 * k : 16 * k + 16, :]
-    out[0:16, :] = total
-    for k in range(64):
-        out[16 + k : 17 + k, :] = got[16 * k + 12 : 16 * k + 13, :]
+    for k in range(10):
+        out[k : k + 1, :] = jnp.sum(got[:, k * LANES : (k + 1) * LANES], axis=0, keepdims=True)
+    out[10:16, :] = jnp.zeros((6, LANES), F32)
+    out[16:80, :] = pltpu.roll(got[:, 9 * LANES : 10 * LANES], 32, 1)
 
 
 def motion_kernel(mine, other, rigid, out):
@@ -432,7 +490,11 @@
     high = jnp.where(even, other[...], mine[...])
     by = jnp.concatenate([low[16:80, :], high[16:80, :]], 0).T
     moments = [by[8 * k : 8 * k + 4, :] for k in range(4)]
-    sums = [jnp.concatenate([low[2 * k : 2 * k + 2, :], high[2 * k : 2 * k + 2, :]], 0) for k in range(6)]
+    sums = []
+    for k in range(6):
+        second = low[6 + k : 7 + k, :] if k < 3 else high[3 + k : 4 + k, :]
+        last = pltpu.roll(high[8:16, :], LANES - 16 * k, 1) if k else high[8:16, :]
+        sums.append(jnp.concatenate([low[k : k + 1, :], second, high[k : k + 1, :], last[1:2, :]], 0))
     own = rigid[0:4, :]
     mass = own + moments[0]
     centre = [(own * rigid[8 + 8 * c : 12 + 8 * c, :] + moments[1 + c]) / mass for c in range(3)]
@@ -477,7 +539,6 @@
     part_inertia,
 ):
     state = ((96, LANES), F32)
-    square = ((LANES, LANES), F32)
     table = ((LANES, 5 * LANES), F32)
     own = [((3, LANES), F32)] * NBR
     work = [
@@ -506,7 +567,7 @@
         part_inertia,
     )
     rows, ints = ((ROWS, LANES), F32), jnp.int32
-    u, v, fm, mass, pos, idx, inv, cols, part, shared, internal, send, sidx, rigid = call(
+    u, v, fm, mass, pos, idx, inv, cols, part, shared, internal, send, slave, slot, nrm, rigid = call(
         first_kernel,
         [
             state,
@@ -521,7 +582,9 @@
             ((8, LANES), ints),
             state,
             table,
-            square,
+            ((16, LANES), ints),
+            ((16, LANES), ints),
+            ((48, LANES), F32),
             ((56, LANES), F32),
         ],
         [HBM] * 18,
@@ -529,7 +592,7 @@
         [
             *[pltpu.VMEM((3, 4096), F32)] * 4,
             pltpu.VMEM((NBR, 1, LANES), ints),
-            *[pltpu.VMEM((16, LANES), ints)] * 3,
+            *[pltpu.VMEM((16, LANES), ints)] * 2,
             pltpu.VMEM((3, 2048), F32),
             pltpu.VMEM((8, 24, 24), F32),
             pltpu.VMEM((1, PARTS_SIZE), F32),
@@ -540,7 +603,7 @@
             pltpu.VMEM((8, 4096), ints),
             *work,
             pltpu.VMEM((LANES, LANES), F32),
-            pltpu.VMEM((LANES, 3 * LANES), F32),
+            pltpu.VMEM((LANES, 2 * LANES), F32),
             pltpu.SemaphoreType.DMA((18,)),
         ],
     )(*[pltpu.with_memory_space_constraint(x, pltpu.HBM) for x in inputs])
@@ -557,22 +620,34 @@
         recv = [partner(mine[b], b) for b in range(NBR)]
 
     trio = ((LANES, 3 * LANES), F32)
-    x, v, net, dots, ends, nrm = call(
+    x, v, net, dots, midx, mnrm = call(
         dots_kernel,
-        [state, state, state, trio, ((LANES, LANES), ints), ((3, LANES, LANES), F32)],
-        [VMEM] * 16,
+        [state, state, state, trio, ((64, LANES), ints), ((3, 64, LANES), F32)],
+        [VMEM] * 17,
         "contact_dots",
-        [pltpu.VMEM((192, LANES), F32), pltpu.VMEM((64, LANES), F32)],
-    )(u, v, internal, inv, fm, mass, pos, part, send, sidx, got, *recv)
+        [
+            pltpu.VMEM((192, LANES), F32),
+            pltpu.VMEM((64, LANES), F32),
+            pltpu.VMEM((LANES, LANES), F32),
+            pltpu.VMEM((32, LANES), F32),
+            pltpu.VMEM((2, 64, LANES), F32),
+        ],
+    )(u, v, internal, inv, fm, mass, pos, part, slave, slot, nrm, got, *recv)
     half = ((16, LANES), F32)
     nodal_velocity, keep, give = call(
         contact_kernel,
         [((3, 4096), F32), half, half],
-        [VMEM] * 9,
+        [VMEM] * 12,
         "contact_forces",
-        [pltpu.VMEM((192, LANES), F32), pltpu.VMEM((96, LANES), F32), pltpu.VMEM((96, LANES), F32)],
-    )(dots, swap(dots), ends, nrm, x, v, net, mass, part)
-    (spread,) = call(spread_kernel, [((1024, LANES), F32)], [VMEM] * 2, "part_spread")(keep, partner(give, 0))
+        [
+            pltpu.VMEM((192, LANES), F32),
+            pltpu.VMEM((96, LANES), F32),
+            pltpu.VMEM((96, LANES), F32),
+            pltpu.VMEM((64, LANES), F32),
+            pltpu.VMEM((64, LANES), F32),
+        ],
+    )(dots, swap(dots), slave, slot, nrm, midx, mnrm, x, v, net, mass, part)
+    (spread,) = call(spread_kernel, [((64, 10 * LANES), F32)], [VMEM] * 2, "part_spread")(keep, partner(give, 0))
     chips = lax.axis_size("dom") // 2
     groups = [[2 * i + core for i in range(chips)] for core in range(2)]
     (total,) = call(total_kernel, [((80, LANES), F32)], [VMEM], "part_totals")(swap(spread, groups))

time: 111 us -> 107 us (0.964)
  Pallas kernels: 31.8 us -> 29.4 us
  blocking collectives: 56.1 us -> 54.2 us
    pallas_call x3, Pallas kernels: 8.01 us -> 5.54 us  [the longest x1 2.81 us: per_device(): call(dots_kernel, [state, state, state, trio, ((64, LANES), ints), ((3, 6...]
    all_to_all x3, blocking collectives: 56.1 us -> 54.2 us  [swap(): lax.all_to_all(block, 'dom', 0, 0, tiled=True, axis_index_groups=groups)]
where the time goes in v4:
time: 107 us
  blocking collectives  54.2 us (51%)
  Pallas kernels  29.4 us (27%)
  starting transfers between devices  14.3 us (13%)
  waiting for transfers between devices  7.44 us (7%)
    all_to_all x3, blocking collectives, swap(): lax.all_to_all(block, 'dom', 0, 0, tiled=True, axis_index_groups=groups)  54.2 us
    ppermute x12, starting transfers between devices, partner(): lax.ppermute(block, 'dom', [(i, i ^ 1 << apart) for i in range(count)])  14.3 us
    pallas_call x2, Pallas kernels, per_device(): call(functools.partial(next_kernel, n == 0), [state, state, state, *own],...  13.5 us
    pallas_call x1, Pallas kernels, per_device(): call(first_kernel, [state, state, state, rows, state, ((8, 4096), ints),...  9.61 us
    ppermute x12, waiting for transfers between devices, partner(): lax.ppermute(block, 'dom', [(i, i ^ 1 << apart) for i in range(count)])  7.44 us
    pallas_call x1, Pallas kernels, per_device(): call(dots_kernel, [state, state, state, trio, ((64, LANES), ints), ((3, 6...  2.81 us
    pallas_call x1, Pallas kernels, per_device(): call(contact_kernel, [((3, 4096), F32), half, half], [VMEM] * 12, 'contac...  2.7 us
  transfers between devices with their start and end apart: 12, of which 7 were waited for; matrix products, arithmetic and copies ran while one was open for 0% of the time, Pallas kernels for 0%

profile of v4, /device:TPU:1, one launch (start us, length us, event | category | flops | bytes accessed | tf_op | source)
XLA Modules:
  0.0 107.0 jit_solution(9825855323984474487)
XLA Ops:
  0.6 0.0 copy-start
  0.6 9.6 %first_cycle.1 = (f32[96,128]{1,0:T(8,128)S(1)}, f32[96,128]{1,0:T(8,128)S(1)}, f32[96,128]{1,0:T(8,128)S(1)}, f32[32,128]{1,0:T(8,128)S(1)}, f32[96,128]{1,0:T(...) custom-call(f32[8,24,24]{2,1,0:T(8,128)} %refs_0_.1, ...), custom_call_target="tpu_custom_call" | custom-call | bytes 1048576 | tf_op jit(solution)/shard_map/first_cycle/pallas_call | solution.py:570
  10.3 0.3 copy.20
  10.6 22.9 %all_to_all.33 = f32[128,1,640]{2,1,0:T(1,128)S(1)} all-to-all(f32[128,1,640]{2,1,0:T(1,128)S(1)} %copy.20), channel_id=1, replica_groups=mesh['dom'=128] {'dom'}, dimensions={0} | all-to-all | bytes 655360 | tf_op jit(solution)/shard_map/all_to_all | solution.py:518
  33.6 0.0 copy-done
  33.6 6.7 %next_cycle.2 = (f32[96,128]{1,0:T(8,128)S(1)}, f32[96,128]{1,0:T(8,128)S(1)}, f32[96,128]{1,0:T(8,128)S(1)}, f32[3,128]{1,0:T(4,128)S(1)}, f32[3,128]{1,0:T(4,1...) custom-call(f32[96,128]{1,0:T(8,128)S(1)} %get-tuple-element.43.u, ...), custom_call_target="tpu_custom_call" | custom-call | bytes 1048576 | tf_op jit(solution)/shard_map/next_cycle/pallas_call | solution.py:613
  40.3 1.0 collective-permute-start
  41.2 0.3 collective-permute-start.1
  41.5 1.6 %collective-permute-start.2 = (f32[3,128]{1,0:T(4,128)S(1)}, f32[3,128]{1,0:T(4,128)S(1)}, u32[]{:S(2)}, u32[]{:S(2)}) collective-permute-start(f32[3,128]{1,0:T(4,128)S(1)} %get-tuple-element.58), channel_id=1, source_target_pairs={{0,4},{1,5},{2,6},{3,7},{4,0},{5,1},{6,2},{7,3},{8,12},{9,13},{10,... | collective-permute-start | bytes 4616 | tf_op jit(solution)/shard_map/ppermute | solution.py:514
  43.2 0.5 collective-permute-start.3
  43.7 1.1 collective-permute-start.4
  44.8 0.0 collective-permute-done.rest_0_
  44.8 0.0 collective-permute-done.1.rest_1_
  44.8 0.7 collective-permute-done.2.rest_2_
  45.5 0.4 collective-permute-done.3.rest_3_
  45.9 1.7 %collective-permute-done.4.rest_4_ = f32[3,128]{1,0:T(4,128)S(1)} collective-permute-done((f32[3,128]{1,0:T(4,128)S(1)}, f32[3,128]{1,0:T(4,128)S(1)}, u32[]{:S(2)}, u32[]{:S(2)}) %collective-permute-start.4) | collective-permute-done | bytes 1568 | tf_op jit(solution)/shard_map/ppermute | solution.py:514
  47.6 6.8 %next_cycle.3 = (f32[96,128]{1,0:T(8,128)S(1)}, f32[96,128]{1,0:T(8,128)S(1)}, f32[96,128]{1,0:T(8,128)S(1)}, f32[3,128]{1,0:T(4,128)S(1)}, f32[3,128]{1,0:T(4,1...) custom-call(f32[96,128]{1,0:T(8,128)S(1)} %get-tuple-element.53.u, ...), custom_call_target="tpu_custom_call" | custom-call | bytes 1048576 | tf_op jit(solution)/shard_map/next_cycle/pallas_call | solution.py:613
  54.4 2.2 %collective-permute-start.5 = (f32[3,128]{1,0:T(4,128)S(1)}, f32[3,128]{1,0:T(4,128)S(1)}, u32[]{:S(2)}, u32[]{:S(2)}) collective-permute-start(f32[3,128]{1,0:T(4,128)S(1)} %get-tuple-element.69), channel_id=1, source_target_pairs={{0,1},{1,0},{2,3},{3,2},{4,5},{5,4},{6,7},{7,6},{8,9},{9,8},{10,11... | collective-permute-start | bytes 4616 | tf_op jit(solution)/shard_map/ppermute | solution.py:514
  56.7 0.0 collective-permute-start.6
  56.7 2.8 %collective-permute-start.7 = (f32[3,128]{1,0:T(4,128)S(1)}, f32[3,128]{1,0:T(4,128)S(1)}, u32[]{:S(2)}, u32[]{:S(2)}) collective-permute-start(f32[3,128]{1,0:T(4,128)S(1)} %get-tuple-element.71), channel_id=1, source_target_pairs={{0,4},{1,5},{2,6},{3,7},{4,0},{5,1},{6,2},{7,3},{8,12},{9,13},{10,... | collective-permute-start | bytes 4616 | tf_op jit(solution)/shard_map/ppermute | solution.py:514
  59.5 1.2 %collective-permute-start.8 = (f32[3,128]{1,0:T(4,128)S(1)}, f32[3,128]{1,0:T(4,128)S(1)}, u32[]{:S(2)}, u32[]{:S(2)}) collective-permute-start(f32[3,128]{1,0:T(4,128)S(1)} %get-tuple-element.72), channel_id=1, source_target_pairs={{0,8},{1,9},{2,10},{3,11},{4,12},{5,13},{6,14},{7,15},{8,0},{9,1},... | collective-permute-start | bytes 4616 | tf_op jit(solution)/shard_map/ppermute | solution.py:514
  60.7 1.1 %collective-permute-start.9 = (f32[3,128]{1,0:T(4,128)S(1)}, f32[3,128]{1,0:T(4,128)S(1)}, u32[]{:S(2)}, u32[]{:S(2)}) collective-permute-start(f32[3,128]{1,0:T(4,128)S(1)} %get-tuple-element.73), channel_id=1, source_target_pairs={{0,16},{1,17},{2,18},{3,19},{4,20},{5,21},{6,22},{7,23},{8,24},{9,... | collective-permute-start | bytes 4616 | tf_op jit(solution)/shard_map/ppermute | solution.py:514
  61.7 0.0 collective-permute-done.5.rest_0_
  61.7 0.0 collective-permute-done.6.rest_1_
  61.7 0.0 collective-permute-done.7.rest_2_
  61.8 0.1 collective-permute-done.8.rest_3_
  61.9 2.7 %collective-permute-done.9.rest_4_ = f32[3,128]{1,0:T(4,128)S(1)} collective-permute-done((f32[3,128]{1,0:T(4,128)S(1)}, f32[3,128]{1,0:T(4,128)S(1)}, u32[]{:S(2)}, u32[]{:S(2)}) %collective-permute-start.9) | collective-permute-done | bytes 1568 | tf_op jit(solution)/shard_map/ppermute | solution.py:514
  64.6 2.8 %contact_dots.1 = (f32[96,128]{1,0:T(8,128)S(1)}, f32[96,128]{1,0:T(8,128)S(1)}, f32[96,128]{1,0:T(8,128)S(1)}, f32[128,384]{1,0:T(8,128)S(1)}, s32[64,128]{1,0:T(8,128)S(1)}, /*index=5*/f32[3,64,128]{2,1,0:T(8,128)S(1)}) custom-call(f32[96,128]{1,0:T(8,128)S(1)} %get-tuple-element.61.u, f32[96,128]{1,0:T(8,128)S(1)} %get-tuple-element.62.v, ...), custom_call_target="tpu_custom_call" | custom-call | bytes 1048576 | tf_op jit(solution)/shard_map/contact_dots/pallas_call | solution.py:623
  67.4 0.2 copy.21
  67.6 16.0 %all_to_all.34 = f32[128,1,384]{2,1,0:T(1,128)S(1)} all-to-all(f32[128,1,384]{2,1,0:T(1,128)S(1)} %copy.21), channel_id=1, replica_groups=mesh['dom'=128] {'dom'}, dimensions={0} | all-to-all | bytes 393216 | tf_op jit(solution)/shard_map/all_to_all | solution.py:518
  83.7 2.7 %contact_forces.1 = (f32[3,4096]{1,0:T(4,128)}, f32[16,128]{1,0:T(8,128)S(1)}, f32[16,128]{1,0:T(8,128)S(1)}) custom-call(f32[128,384]{1,0:T(8,128)S(1)} %get-tuple-element.74.dots, f32[128,384]{1,0:T(8,128)S(1)} %bitcast.24, s32[16,128]{1,0:T(8,128)S(1)} %get-tuple-element.66.slave, s32[16,128]{1,0:T(8,128)S(1)} %get-tuple-element.67.slot, ...), custom_call_target="tpu_custom_call" | custom-call | bytes 1048576 | tf_op jit(solution)/shard_map/contact_forces/pallas_call | solution.py:637
  86.4 0.8 collective-permute-start.10
  87.1 0.8 collective-permute-done.10.given
  88.0 0.3 copy.22
  88.3 15.2 %all_to_all.35 = f32[64,1,1280]{2,1,0:T(1,128)S(1)} all-to-all(f32[64,1,1280]{2,1,0:T(1,128)S(1)} %copy.22), channel_id=1, replica_groups={{0,2,4,6,8,10,12,14,16,18,20,22,24,26,28,30,32,34,36,38,40,42,44,46,48,..., dimensions={0} | all-to-all | bytes 655360 | tf_op jit(solution)/shard_map/all_to_all | solution.py:518
  103.6 0.1 part_totals.1.mine
  103.7 1.8 %collective-permute-start.11 = (f32[80,128]{1,0:T(8,128)S(1)}, f32[80,128]{1,0:T(8,128)S(1)}, u32[]{:S(2)}, u32[]{:S(2)}) collective-permute-start(f32[80,128]{1,0:T(8,128)S(1)} %part_totals.1.mine), channel_id=1, source_target_pairs={{0,1},{1,0},{2,3},{3,2},{4,5},{5,4},{6,7},{7,6},{8,9},{9,8},{10,11... | collective-permute-start | bytes 122888 | tf_op jit(solution)/shard_map/ppermute | solution.py:514
  105.4 0.9 collective-permute-done.11.other
  106.3 0.7 part_motion.1
  (4 shorter events, 0.1 us)
Async XLA Ops:
  0.6 32.9 %copy-start = (s32[32]{0:T(128)S(1)}, s32[32]{0:T(128)}, u32[]{:S(2)}) copy-start(s32[32]{0:T(128)} %mat.3) | copy-start | bytes 388
  40.3 4.5 %collective-permute-start = (f32[3,128]{1,0:T(4,128)S(1)}, f32[3,128]{1,0:T(4,128)S(1)}, u32[]{:S(2)}, u32[]{:S(2)}) collective-permute-start(f32[3,128]{1,0:T(4,128)S(1)} %get-tuple-element.56), channel_id=1, source_target_pairs={{0,1},{1,0},{2,3},{3,2},{4,5},{5,4},{6,7},{7,6},{8,9},{9,8},{10,11... | collective-permute-start | bytes 4616 | tf_op jit(solution)/shard_map/ppermute | solution.py:514
  41.2 3.5 %collective-permute-start.1 = (f32[3,128]{1,0:T(4,128)S(1)}, f32[3,128]{1,0:T(4,128)S(1)}, u32[]{:S(2)}, u32[]{:S(2)}) collective-permute-start(f32[3,128]{1,0:T(4,128)S(1)} %get-tuple-element.57), channel_id=1, source_target_pairs={{0,2},{1,3},{2,0},{3,1},{4,6},{5,7},{6,4},{7,5},{8,10},{9,11},{10,... | collective-permute-start | bytes 4616 | tf_op jit(solution)/shard_map/ppermute | solution.py:514
  41.5 3.9 %collective-permute-start.2 = (f32[3,128]{1,0:T(4,128)S(1)}, f32[3,128]{1,0:T(4,128)S(1)}, u32[]{:S(2)}, u32[]{:S(2)}) collective-permute-start(f32[3,128]{1,0:T(4,128)S(1)} %get-tuple-element.58), channel_id=1, source_target_pairs={{0,4},{1,5},{2,6},{3,7},{4,0},{5,1},{6,2},{7,3},{8,12},{9,13},{10,... | collective-permute-start | bytes 4616 | tf_op jit(solution)/shard_map/ppermute | solution.py:514
  43.2 2.7 %collective-permute-start.3 = (f32[3,128]{1,0:T(4,128)S(1)}, f32[3,128]{1,0:T(4,128)S(1)}, u32[]{:S(2)}, u32[]{:S(2)}) collective-permute-start(f32[3,128]{1,0:T(4,128)S(1)} %get-tuple-element.59), channel_id=1, source_target_pairs={{0,8},{1,9},{2,10},{3,11},{4,12},{5,13},{6,14},{7,15},{8,0},{9,1},... | collective-permute-start | bytes 4616 | tf_op jit(solution)/shard_map/ppermute | solution.py:514
  43.7 3.9 %collective-permute-start.4 = (f32[3,128]{1,0:T(4,128)S(1)}, f32[3,128]{1,0:T(4,128)S(1)}, u32[]{:S(2)}, u32[]{:S(2)}) collective-permute-start(f32[3,128]{1,0:T(4,128)S(1)} %get-tuple-element.60), channel_id=1, source_target_pairs={{0,16},{1,17},{2,18},{3,19},{4,20},{5,21},{6,22},{7,23},{8,24},{9,... | collective-permute-start | bytes 4616 | tf_op jit(solution)/shard_map/ppermute | solution.py:514
  54.4 7.3 %collective-permute-start.5 = (f32[3,128]{1,0:T(4,128)S(1)}, f32[3,128]{1,0:T(4,128)S(1)}, u32[]{:S(2)}, u32[]{:S(2)}) collective-permute-start(f32[3,128]{1,0:T(4,128)S(1)} %get-tuple-element.69), channel_id=1, source_target_pairs={{0,1},{1,0},{2,3},{3,2},{4,5},{5,4},{6,7},{7,6},{8,9},{9,8},{10,11... | collective-permute-start | bytes 4616 | tf_op jit(solution)/shard_map/ppermute | solution.py:514
  56.7 5.1 %collective-permute-start.6 = (f32[3,128]{1,0:T(4,128)S(1)}, f32[3,128]{1,0:T(4,128)S(1)}, u32[]{:S(2)}, u32[]{:S(2)}) collective-permute-start(f32[3,128]{1,0:T(4,128)S(1)} %get-tuple-element.70), channel_id=1, source_target_pairs={{0,2},{1,3},{2,0},{3,1},{4,6},{5,7},{6,4},{7,5},{8,10},{9,11},{10,... | collective-permute-start | bytes 4616 | tf_op jit(solution)/shard_map/ppermute | solution.py:514
  56.7 5.1 %collective-permute-start.7 = (f32[3,128]{1,0:T(4,128)S(1)}, f32[3,128]{1,0:T(4,128)S(1)}, u32[]{:S(2)}, u32[]{:S(2)}) collective-permute-start(f32[3,128]{1,0:T(4,128)S(1)} %get-tuple-element.71), channel_id=1, source_target_pairs={{0,4},{1,5},{2,6},{3,7},{4,0},{5,1},{6,2},{7,3},{8,12},{9,13},{10,... | collective-permute-start | bytes 4616 | tf_op jit(solution)/shard_map/ppermute | solution.py:514
  59.5 2.4 %collective-permute-start.8 = (f32[3,128]{1,0:T(4,128)S(1)}, f32[3,128]{1,0:T(4,128)S(1)}, u32[]{:S(2)}, u32[]{:S(2)}) collective-permute-start(f32[3,128]{1,0:T(4,128)S(1)} %get-tuple-element.72), channel_id=1, source_target_pairs={{0,8},{1,9},{2,10},{3,11},{4,12},{5,13},{6,14},{7,15},{8,0},{9,1},... | collective-permute-start | bytes 4616 | tf_op jit(solution)/shard_map/ppermute | solution.py:514
  60.7 3.9 %collective-permute-start.9 = (f32[3,128]{1,0:T(4,128)S(1)}, f32[3,128]{1,0:T(4,128)S(1)}, u32[]{:S(2)}, u32[]{:S(2)}) collective-permute-start(f32[3,128]{1,0:T(4,128)S(1)} %get-tuple-element.73), channel_id=1, source_target_pairs={{0,16},{1,17},{2,18},{3,19},{4,20},{5,21},{6,22},{7,23},{8,24},{9,... | collective-permute-start | bytes 4616 | tf_op jit(solution)/shard_map/ppermute | solution.py:514
  86.4 1.6 %collective-permute-start.10 = (f32[16,128]{1,0:T(8,128)S(1)}, f32[16,128]{1,0:T(8,128)S(1)}, u32[]{:S(2)}, u32[]{:S(2)}) collective-permute-start(f32[16,128]{1,0:T(8,128)S(1)} %get-tuple-element.82), channel_id=1, source_target_pairs={{0,1},{1,0},{2,3},{3,2},{4,5},{5,4},{6,7},{7,6},{8,9},{9,8},{10,11... | collective-permute-start | bytes 24584 | tf_op jit(solution)/shard_map/ppermute | solution.py:514
  103.7 2.6 %collective-permute-start.11 = (f32[80,128]{1,0:T(8,128)S(1)}, f32[80,128]{1,0:T(8,128)S(1)}, u32[]{:S(2)}, u32[]{:S(2)}) collective-permute-start(f32[80,128]{1,0:T(8,128)S(1)} %part_totals.1.mine), channel_id=1, source_target_pairs={{0,1},{1,0},{2,3},{3,2},{4,5},{5,4},{6,7},{7,6},{8,9},{9,8},{10,11... | collective-permute-start | bytes 122888 | tf_op jit(solution)/shard_map/ppermute | solution.py:514

commit v5 on v4

--- a/solution.py
+++ b/solution.py
@@ -196,30 +196,34 @@
     return pl.ds(pl.multiple_of((row >> 3) << 3, 8), 8), here
 
 
-def first_kernel(*refs):
-    srcs = refs[:18]
-    (u, v, fm, mass, pos, idx, inv, cols, part, shared, internal, send, slave, slot, nrm, rigid) = refs[18:34]
-    work = refs[34:]
-    (disp0, vel0, force0, pos0, shared0, owner, master, normal, stiff) = work[:9]
-    pmass, pcenter, pinertia, mat, accel, conn = work[9:15]
-    tab, g, acc, small, table, sems = work[15:]
-    dsts = (stiff, disp0, vel0, conn, mat, shared0, force0, mass, accel, slave, owner, master, normal)
-    dsts = dsts + (pos0, part, pmass, pcenter, pinertia)
+def copy_all(srcs, dsts, sems):
     copies = [pltpu.make_async_copy(a, b, sems.at[i]) for i, (a, b) in enumerate(zip(srcs, dsts))]
     for copy in copies:
         copy.start()
-    small[...] = jnp.zeros_like(small)
-    for copy in copies:
-        copy.wait()
+    return copies
+
+
+def first_kernel(*refs):
+    srcs = refs[:13]
+    u, v, fm, mass, idx, cols, shared, internal, send, slave, slot, normal = refs[13:25]
+    disp0, vel0, force0, shared0, owner, master, stiff, mat, accel, conn, tab, g, acc, table, sems = refs[25:]
+    dsts = (stiff, owner, master, normal, disp0, vel0, conn, mat, shared0, force0, mass, accel, slave)
+    copies = copy_all(srcs, dsts, sems)
 
     def columns(m):
         for j in range(24):
             cols[m * 24 + j] = jnp.broadcast_to(stiff[m, :, j : j + 1], (24, LANES))
 
+    for copy in copies[:4]:
+        copy.wait()
+    slots(owner, master, normal, slot, table, columns)
+    send[:, 0:256] = table[...]
+    send[:, 256:640] = jnp.zeros((LANES, 384), F32)
+    for copy in copies[4:]:
+        copy.wait()
     to_rows(disp0, u)
     to_rows(vel0, v)
     to_rows(force0, fm)
-    to_rows(pos0, pos)
     tab[...] = u[...] + DAMP_RATIO * v[...]
     for c in range(3):
         at = slice(c * ROWS, (c + 1) * ROWS)
@@ -231,24 +235,6 @@
     shared[...] = jnp.zeros_like(shared)
     for b in range(NBR):
         shared[b : b + 1, :] = shared0[b]
-    row = lax.broadcasted_iota(jnp.int32, (8, LANES), 0).astype(F32)
-    held = row < NBR
-    kept = [jnp.where(held, lane.astype(F32), 0.0), jnp.where(held, row + 1.0, 0.0)]
-    add_placed(small, shared[...] & 127, shared[...] >> 7, kept)
-    inv[...] = (small[0:64, :] + small[64:128, :]).astype(jnp.int32)
-    rigid[...] = jnp.ones_like(rigid)
-    for h, n in spans():
-        at = slice(h * LANES, h * LANES + n)
-        rigid[h : h + 1, 0:n] = pmass[0:1, at]
-        for c in range(3):
-            rigid[8 + 8 * c + h : 9 + 8 * c + h, 0:n] = pcenter[c : c + 1, at]
-            rigid[32 + 8 * c + h : 33 + 8 * c + h, 0:n] = pinertia[c : c + 1, at]
-    for t in range(16):
-        for c in range(3):
-            nrm[16 * c + t : 16 * c + t + 1, :] = normal[c : c + 1, t * LANES : (t + 1) * LANES]
-    slots(owner, master, normal, slot, table, columns)
-    send[:, 0:256] = table[...]
-    send[:, 256:640] = jnp.zeros((LANES, 384), F32)
     elements(idx, mat, tab, cols, g, acc)
     own = finish_internal(acc, internal, shared)
     me = lax.axis_index("dom")
@@ -259,13 +245,49 @@
             send[tile, 256 + c * LANES : 256 + (c + 1) * LANES] += jnp.where(here, row, 0.0)
 
 
+def fixed_kernel(*refs):
+    pos0, part0, pmass0, pcenter0, pinertia0, normal, shared, mass, pos, part, inv, nrm, light, rigid = refs[:14]
+    pos1, pmass, pcenter, pinertia, small, sems = refs[14:]
+    copies = copy_all(
+        (pos0, part0, pmass0, pcenter0, pinertia0), (pos1, part, pmass, pcenter, pinertia), sems
+    )
+    small[...] = jnp.zeros_like(small)
+    lane = lax.broadcasted_iota(jnp.int32, (8, LANES), 1)
+    row = lax.broadcasted_iota(jnp.int32, (8, LANES), 0)
+    held = row < NBR
+    lo, hi = shared[...] & 127, shared[...] >> 7
+    kept = [jnp.where(held, lane, 0).astype(F32), jnp.where(held, row + 1, 0).astype(F32)]
+    add_placed(small, lo, hi, kept)
+    found = (small[0:64, :] + small[64:128, :]).astype(jnp.int32)
+    inv[...] = found[0:ROWS, :] + found[ROWS : 2 * ROWS, :] * LANES
+    (weight,) = gather(mass, (0,), lo, hi)
+    light[...] = -TIME_STEP / weight
+    for t in range(16):
+        for c in range(3):
+            nrm[16 * c + t : 16 * c + t + 1, :] = normal[c : c + 1, t * LANES : (t + 1) * LANES]
+    rigid[...] = jnp.ones_like(rigid)
+    for copy in copies:
+        copy.wait()
+    to_rows(pos1, pos)
+    for h, n in spans():
+        at = slice(h * LANES, h * LANES + n)
+        rigid[h : h + 1, 0:n] = pmass[0:1, at]
+        for c in range(3):
+            rigid[8 + 8 * c + h : 9 + 8 * c + h, 0:n] = pcenter[c : c + 1, at]
+            rigid[32 + 8 * c + h : 33 + 8 * c + h, 0:n] = pinertia[c : c + 1, at]
+
+
+def from_shared(code, rows):
+    total = 0.0
+    for b in range(NBR):
+        row = jnp.broadcast_to(rows[b], (8, LANES))
+        total = total + jnp.where(code >> 7 == b + 1, lanes_of(row, code & 127), 0.0)
+    return total
+
+
 def update(u, v, internal, inv, fm, mass, recv, c, r):
     at = slice(c * ROWS + r, c * ROWS + r + 8)
-    slot, which = inv[r : r + 8, :], inv[ROWS + r : ROWS + r + 8, :]
-    total = internal[at, :]
-    for b in range(NBR):
-        row = jnp.broadcast_to(recv[b][c], (8, LANES))
-        total = total + jnp.where(which == b + 1, lanes_of(row, slot), 0.0)
+    total = internal[at, :] + from_shared(inv[r : r + 8, :], [recv[b][c] for b in range(NBR)])
     speed = v[at, :] + TIME_STEP * (fm[at, :] - total / mass[r : r + 8, :])
     return at, u[at, :] + TIME_STEP * speed, speed, total
 
@@ -303,18 +325,7 @@
             own[b][c : c + 1, :] = vals[c][b : b + 1, :]
 
 
-def dots_kernel(u, v, internal, inv, fm, mass, pos, part, slave, slot, nrm, got, *rest):
-    recv = rows_of(rest[:5])
-    x2, v2, net, dots, midx, mnrm, tab, acc, table, ab, dense = rest[5:]
-    for c in range(3):
-        for r in range(0, ROWS, 8):
-            at, disp, speed, total = update(u, v, internal, inv, fm, mass, recv, c, r)
-            place_now = pos[at, :] + disp
-            x2[at, :] = place_now
-            v2[at, :] = speed
-            net[at, :] = mass[r : r + 8, :] * fm[at, :] - total
-            tab[at, :] = place_now
-            tab[c * ROWS + 96 + r : c * ROWS + 96 + r + 8, :] = speed
+def ends_kernel(got, slave, inv, midx, mnrm, code):
     left = lax.broadcasted_iota(jnp.int32, (64, LANES), 1) < 64
     for k, out in ((0, mnrm.at[0]), (1, mnrm.at[1]), (2, mnrm.at[2]), (3, midx)):
         at = slice(LANES * (k // 2), LANES * (k // 2) + LANES)
@@ -323,10 +334,21 @@
             out[...] = jnp.where(left, pltpu.roll(top, 64, 1), low).astype(out.dtype)
         else:
             out[...] = jnp.where(left, top, pltpu.roll(low, 64, 1))
-
-    def vals(r):
-        m = mass[r : r + 8, :]
-        return [m, *[m * tab[c * ROWS + r : c * ROWS + r + 8, :] for c in range(3)]]
+    for r in range(0, 80, 8):
+        here = slave[r : r + 8, :] if r < 16 else midx[r - 16 : r - 8, :]
+        (code[r : r + 8, :],) = gather(inv, (0,), here & 127, here >> 7)
+
+
+def base_kernel(u, v, internal, fm, mass, pos, slave, nrm, midx, mnrm, x2, v2, ab, tab):
+    for c in range(3):
+        for r in range(0, ROWS, 8):
+            at = slice(c * ROWS + r, c * ROWS + r + 8)
+            speed = v[at, :] + TIME_STEP * (fm[at, :] - internal[at, :] / mass[r : r + 8, :])
+            place_now = pos[at, :] + (u[at, :] + TIME_STEP * speed)
+            x2[at, :] = place_now
+            v2[at, :] = speed
+            tab[at, :] = place_now
+            tab[c * ROWS + 96 + r : c * ROWS + 96 + r + 8, :] = speed
 
     def both(here, w):
         y = gather(tab, tuple(range(0, 192, ROWS)), here & 127, here >> 7)
@@ -334,34 +356,67 @@
 
     for r in (0, 8):
         w = [nrm[16 * c + r : 16 * c + r + 8, :] for c in range(3)]
-        ab[r : r + 8, :], ab[16 + r : 24 + r, :] = both(slave[r : r + 8, :], w)
+        ab[0, r : r + 8, :], ab[1, r : r + 8, :] = both(slave[r : r + 8, :], w)
+
+    def step(i, carry):
+        for q in range(2):
+            at = pl.ds(pl.multiple_of(i * 16 + q * 8, 8), 8)
+            to = pl.ds(pl.multiple_of(i * 16 + q * 8 + 16, 8), 8)
+            ab[0, to, :], ab[1, to, :] = both(midx[at, :], [mnrm[c, at, :] for c in range(3)])
+        return carry
+
+    lax.fori_loop(0, 4, step, 0)
+
+
+def dots_kernel(x1, v1, ab1, internal, inv, light, fm, mass, part, slot, nrm, mnrm, code, *rest):
+    recv = rows_of(rest[:5])
+    x2, v2, net, dots, acc, table, ab = rest[5:]
+    for c in range(3):
+        for r in range(0, ROWS, 8):
+            at = slice(c * ROWS + r, c * ROWS + r + 8)
+            m = mass[r : r + 8, :]
+            more = from_shared(inv[r : r + 8, :], [recv[b][c] for b in range(NBR)])
+            change = -TIME_STEP * (more / m)
+            x2[at, :] = x1[at, :] + TIME_STEP * change
+            v2[at, :] = v1[at, :] + change
+            net[at, :] = m * fm[at, :] - internal[at, :] - more
+    moved = [[recv[b][c] * light[b : b + 1, :] for b in range(NBR)] for c in range(3)]
+    for r in range(0, 80, 8):
+        here = code[r : r + 8, :]
+        if r < 16:
+            w = [nrm[16 * c + r : 16 * c + r + 8, :] for c in range(3)]
+        else:
+            w = [mnrm[c, r - 16 : r - 8, :] for c in range(3)]
+        d = [from_shared(here, moved[c]) for c in range(3)]
+        change = d[0] * w[0] + d[1] * w[1] + d[2] * w[2]
+        ab[0, r : r + 8, :] = ab1[0, r : r + 8, :] + TIME_STEP * change
+        ab[1, r : r + 8, :] = ab1[1, r : r + 8, :] + change
+
+    def vals(r):
+        m = mass[r : r + 8, :]
+        return [m, *[m * x2[c * ROWS + r : c * ROWS + r + 8, :] for c in range(3)]]
+
     acc[...] = jnp.zeros_like(acc)
     part_sums(part, vals, acc, True)
     moments = jnp.concatenate([acc[0:32, :] + acc[32:64, :], jnp.zeros((96, LANES), F32)], 0)
     dots[:, 256:384] = moments.T
     table[...] = jnp.zeros_like(table)
-
-    def step(i, carry):
-        for q in range(2):
-            at = pl.ds(pl.multiple_of(i * 16 + q * 8, 8), 8)
-            dense[0, at, :], dense[1, at, :] = both(midx[at, :], [mnrm[c, at, :] for c in range(3)])
+    for i in range(4):
         hits, pieces = [], []
-        for q in range(4):
-            at = pl.ds(i * 4 + q, 1)
-            here = slot[at, :]
-            rows = [ab[at, :], ab[pl.ds(16 + i * 4 + q, 1), :]]
+        for t in range(4 * i, 4 * i + 4):
+            here = slot[t : t + 1, :]
+            rows = [ab[0, t : t + 1, :], ab[1, t : t + 1, :]]
             one, two = slotted(hits_of(here >> 6).astype(BF), (here & 63).astype(F32), rows)
             hits += one
             pieces += two
         table[...] += lax.dot_general(
             jnp.concatenate(hits, 1), jnp.concatenate(pieces, 1), NT, preferred_element_type=F32
         )
-        return carry
-
-    lax.fori_loop(0, 4, step, 0)
+    left = lax.broadcasted_iota(jnp.int32, (64, LANES), 1) < 64
+    one, two = ab[0, 16:80, :], ab[1, 16:80, :]
     dots[:, 0:128] = table[...]
-    dots[0:64, 128:256] = jnp.where(left, dense[0], pltpu.roll(dense[1], 64, 1))
-    dots[64:128, 128:256] = jnp.where(left, pltpu.roll(dense[0], 64, 1), dense[1])
+    dots[0:64, 128:256] = jnp.where(left, one, pltpu.roll(two, 64, 1))
+    dots[64:128, 128:256] = jnp.where(left, pltpu.roll(one, 64, 1), two)
 
 
 def part_sums(part, vals, acc, by_device):
@@ -393,7 +448,7 @@
 
 
 def contact_kernel(
-    dots, got, slave, slot, nrm, midx, mnrm, x, v, net, mass, part, nodal, keep, give, acc, tot, acc2, push, mine
+    dots, got, slave, slot, nrm, midx, mnrm, x, net, part, contact, keep, give, acc, tot, acc2, push, mine
 ):
     acc[...] = jnp.zeros_like(acc)
     acc2[...] = jnp.zeros_like(acc2)
@@ -433,12 +488,8 @@
     acc[...] += lax.dot_general(
         jnp.concatenate(one, 1), jnp.concatenate(two, 1), NT, preferred_element_type=F32
     )
-    contact = acc[0:96, :] + acc[96:192, :]
-    tot[...] = net[...] + contact
-    for c in range(3):
-        speed = v[c * ROWS : (c + 1) * ROWS, :] + TIME_STEP * contact[c * ROWS : (c + 1) * ROWS, :] / mass[...]
-        for h in range(ROWS):
-            nodal[c : c + 1, h * LANES : (h + 1) * LANES] = speed[h : h + 1, :]
+    contact[...] = acc[0:96, :] + acc[96:192, :]
+    tot[...] = net[...] + contact[...]
 
     def vals(r):
         p = [x[c * ROWS + r : c * ROWS + r + 8, :] for c in range(3)]
@@ -469,6 +520,14 @@
     moments = jnp.broadcast_to(jnp.sum(got[:, 256:384], axis=0, keepdims=True), (8, LANES))
     moments = jnp.where(lane < 96, 0.0, pltpu.roll(moments, 96, 1))
     keep[9:10, :] = keep[9:10, :] + moments[0:1, :]
+
+
+def nodal_kernel(v, contact, mass, nodal):
+    for c in range(3):
+        at = slice(c * ROWS, (c + 1) * ROWS)
+        speed = v[at, :] + TIME_STEP * contact[at, :] / mass[...]
+        for h in range(ROWS):
+            nodal[c : c + 1, h * LANES : (h + 1) * LANES] = speed[h : h + 1, :]
 
 
 def spread_kernel(keep, given, out):
@@ -512,6 +571,14 @@
 def partner(block, apart):
     count = lax.axis_size("dom")
     return lax.ppermute(block, "dom", [(i, i ^ (1 << apart)) for i in range(count)])
+
+
+def in_hbm(*arrays):
+    return [pltpu.with_memory_space_constraint(x, pltpu.HBM) for x in arrays]
+
+
+def later(value, than):
+    return lax.optimization_barrier((value, than))[0]
 
 
 def swap(block, groups=None):
@@ -548,6 +615,9 @@
     ]
     inputs = (
         stiffness,
+        contact_owner.reshape(16, LANES),
+        contact_master.reshape(16, LANES),
+        contact_normal,
         displacement,
         velocity,
         connectivity,
@@ -557,57 +627,70 @@
         node_mass.reshape(ROWS, LANES),
         body_accel,
         contact_slave.reshape(16, LANES),
-        contact_owner.reshape(16, LANES),
-        contact_master.reshape(16, LANES),
-        contact_normal,
-        rest_pos,
-        part_of_node.reshape(ROWS, LANES),
-        part_mass.reshape(1, PARTS_SIZE),
-        part_center,
-        part_inertia,
     )
     rows, ints = ((ROWS, LANES), F32), jnp.int32
-    u, v, fm, mass, pos, idx, inv, cols, part, shared, internal, send, slave, slot, nrm, rigid = call(
+    whole, map_rows = pltpu.VMEM((3, 4096), F32), ((ROWS, LANES), ints)
+    u, v, fm, mass, idx, cols, shared, internal, send, slave, slot, normal = call(
         first_kernel,
         [
             state,
             state,
             state,
             rows,
-            state,
             ((8, 4096), ints),
-            ((64, LANES), ints),
             ((192, 24, LANES), F32),
-            ((ROWS, LANES), ints),
             ((8, LANES), ints),
             state,
             table,
             ((16, LANES), ints),
             ((16, LANES), ints),
-            ((48, LANES), F32),
-            ((56, LANES), F32),
+            ((3, 2048), F32),
         ],
-        [HBM] * 18,
+        [HBM] * 13,
         "first_cycle",
         [
-            *[pltpu.VMEM((3, 4096), F32)] * 4,
+            whole,
+            whole,
+            whole,
             pltpu.VMEM((NBR, 1, LANES), ints),
-            *[pltpu.VMEM((16, LANES), ints)] * 2,
-            pltpu.VMEM((3, 2048), F32),
+            pltpu.VMEM((16, LANES), ints),
+            pltpu.VMEM((16, LANES), ints),
             pltpu.VMEM((8, 24, 24), F32),
-            pltpu.VMEM((1, PARTS_SIZE), F32),
-            pltpu.VMEM((3, PARTS_SIZE), F32),
-            pltpu.VMEM((3, PARTS_SIZE), F32),
             pltpu.SMEM((ROWS,), ints),
             pltpu.SMEM((3,), F32),
             pltpu.VMEM((8, 4096), ints),
             *work,
+            pltpu.VMEM((LANES, 2 * LANES), F32),
+            pltpu.SemaphoreType.DMA((13,)),
+        ],
+    )(*in_hbm(*inputs))
+    got = swap(send)
+    trio = ((3, PARTS_SIZE), F32)
+    pos, part, inv, nrm, light, rigid = call(
+        fixed_kernel,
+        [state, map_rows, map_rows, ((48, LANES), F32), ((8, LANES), F32), ((56, LANES), F32)],
+        [HBM] * 5 + [VMEM] * 3,
+        "fixed_data",
+        [
+            whole,
+            pltpu.VMEM((1, PARTS_SIZE), F32),
+            pltpu.VMEM(*trio),
+            pltpu.VMEM(*trio),
             pltpu.VMEM((LANES, LANES), F32),
-            pltpu.VMEM((LANES, 2 * LANES), F32),
-            pltpu.SemaphoreType.DMA((18,)),
+            pltpu.SemaphoreType.DMA((5,)),
         ],
-    )(*[pltpu.with_memory_space_constraint(x, pltpu.HBM) for x in inputs])
-    got = swap(send)
+    )(
+        *in_hbm(
+            rest_pos,
+            part_of_node.reshape(ROWS, LANES),
+            part_mass.reshape(1, PARTS_SIZE),
+            part_center,
+            part_inertia,
+        ),
+        normal,
+        shared,
+        mass,
+    )
     recv = [got]
     for n in range(CYCLES - 1):
         u, v, internal, *mine = call(
@@ -618,26 +701,34 @@
             work,
         )(u, v, internal, inv, fm, mass, idx, elem_material, cols, shared, *recv)
         recv = [partner(mine[b], b) for b in range(NBR)]
-
-    trio = ((LANES, 3 * LANES), F32)
-    x, v, net, dots, midx, mnrm = call(
+        if n == 0:
+            midx, mnrm, code = call(
+                ends_kernel,
+                [((64, LANES), ints), ((3, 64, LANES), F32), ((80, LANES), ints)],
+                [VMEM] * 3,
+                "contact_ends",
+            )(later(got, mine), slave, inv)
+            recv, code = lax.optimization_barrier((recv, code))
+    both = ((2, 80, LANES), F32)
+    x, v, ab = call(
+        base_kernel,
+        [state, state, both],
+        [VMEM] * 10,
+        "contact_base",
+        [pltpu.VMEM((192, LANES), F32)],
+    )(u, v, internal, fm, mass, pos, slave, nrm, midx, mnrm)
+    x, v, net, dots = call(
         dots_kernel,
-        [state, state, state, trio, ((64, LANES), ints), ((3, 64, LANES), F32)],
-        [VMEM] * 17,
+        [state, state, state, ((LANES, 3 * LANES), F32)],
+        [VMEM] * 18,
         "contact_dots",
-        [
-            pltpu.VMEM((192, LANES), F32),
-            pltpu.VMEM((64, LANES), F32),
-            pltpu.VMEM((LANES, LANES), F32),
-            pltpu.VMEM((32, LANES), F32),
-            pltpu.VMEM((2, 64, LANES), F32),
-        ],
-    )(u, v, internal, inv, fm, mass, pos, part, slave, slot, nrm, got, *recv)
+        [pltpu.VMEM((64, LANES), F32), pltpu.VMEM((LANES, LANES), F32), pltpu.VMEM(*both)],
+    )(x, v, ab, internal, inv, light, fm, mass, part, slot, nrm, mnrm, code, *recv)
     half = ((16, LANES), F32)
-    nodal_velocity, keep, give = call(
+    contact, keep, give = call(
         contact_kernel,
-        [((3, 4096), F32), half, half],
-        [VMEM] * 12,
+        [state, half, half],
+        [VMEM] * 10,
         "contact_forces",
         [
             pltpu.VMEM((192, LANES), F32),
@@ -646,7 +737,8 @@
             pltpu.VMEM((64, LANES), F32),
             pltpu.VMEM((64, LANES), F32),
         ],
-    )(dots, swap(dots), slave, slot, nrm, midx, mnrm, x, v, net, mass, part)
+    )(dots, swap(dots), slave, slot, nrm, midx, mnrm, x, net, part)
+    (nodal_velocity,) = call(nodal_kernel, [((3, 4096), F32)], [VMEM] * 3, "nodal_velocity")(v, contact, mass)
     (spread,) = call(spread_kernel, [((64, 10 * LANES), F32)], [VMEM] * 2, "part_spread")(keep, partner(give, 0))
     chips = lax.axis_size("dom") // 2
     groups = [[2 * i + core for i in range(chips)] for core in range(2)]

time: 107 us -> 106 us (level)
  blocking collectives: 54.2 us -> 31.2 us
  starting transfers between devices: 14.3 us -> 25.7 us
  waiting for transfers between devices: 7.44 us -> 14.4 us
  Pallas kernels: 29.4 us -> 31.8 us
    all_to_all x3 -> x2, blocking collectives: 54.2 us -> 31.2 us  [swap(): lax.all_to_all(block, 'dom', 0, 0, tiled=True, axis_index_groups=groups)]
    all_to_all x0 -> x1, starting transfers between devices: none -> 11.5 us  [swap(): lax.all_to_all(block, 'dom', 0, 0, tiled=True, axis_index_groups=groups)]
    all_to_all x0 -> x1, waiting for transfers between devices: none -> 10.6 us  [swap(): lax.all_to_all(block, 'dom', 0, 0, tiled=True, axis_index_groups=groups)]
    ppermute x12, waiting for transfers between devices: 7.44 us -> 3.86 us  [partner(): lax.ppermute(block, 'dom', [(i, i ^ 1 << apart) for i in range(count)])]
    pallas_call x3 -> x7, Pallas kernels: 15.1 us -> 17.9 us  [the longest x1 9.6 us: per_device(): call(first_kernel, [state, state, state, rows, ((8, 4096), ints), ((192,...]
  transfers between devices with their start and end apart: 12 -> 13, of which waited for: 7 -> 7; matrix products, arithmetic and copies ran while one was open for 0% -> 0% of each run, Pallas kernels for 0% -> 4%
where the time goes in v5:
time: 106 us
  Pallas kernels  31.8 us (30%)
  blocking collectives  31.2 us (29%)
  starting transfers between devices  25.7 us (24%)
  waiting for transfers between devices  14.4 us (14%)
  local copies, waits for them, and re-layouts  1.66 us (2%)
    all_to_all x2, blocking collectives, swap(): lax.all_to_all(block, 'dom', 0, 0, tiled=True, axis_index_groups=groups)  31.2 us
    ppermute x12, starting transfers between devices, partner(): lax.ppermute(block, 'dom', [(i, i ^ 1 << apart) for i in range(count)])  14.2 us
    pallas_call x2, Pallas kernels, per_device(): call(functools.partial(next_kernel, n == 0), [state, state, state, *own],...  13.1 us
    all_to_all x1, starting transfers between devices, swap(): lax.all_to_all(block, 'dom', 0, 0, tiled=True, axis_index_groups=groups)  11.5 us
    all_to_all x1, waiting for transfers between devices, swap(): lax.all_to_all(block, 'dom', 0, 0, tiled=True, axis_index_groups=groups)  10.6 us
    pallas_call x1, Pallas kernels, per_device(): call(first_kernel, [state, state, state, rows, ((8, 4096), ints), ((192,...  9.6 us
    ppermute x12, waiting for transfers between devices, partner(): lax.ppermute(block, 'dom', [(i, i ^ 1 << apart) for i in range(count)])  3.86 us
    pallas_call x1, Pallas kernels, per_device(): call(contact_kernel, [state, half, half], [VMEM] * 10, 'contact_forces',...  2.68 us
  transfers between devices with their start and end apart: 13, of which 7 were waited for; matrix products, arithmetic and copies ran while one was open for 0% of the time, Pallas kernels for 4%

profile of v5, /device:TPU:1, one launch (start us, length us, event | category | flops | bytes accessed | tf_op | source)
XLA Modules:
  0.0 105.7 jit_solution(1006485750606600133)
XLA Ops:
  0.6 0.0 copy-start
  0.6 9.6 %first_cycle.1 = (f32[96,128]{1,0:T(8,128)S(1)}, f32[96,128]{1,0:T(8,128)S(1)}, f32[96,128]{1,0:T(8,128)S(1)}, f32[32,128]{1,0:T(8,128)S(1)}, s32[8,4096]{1,0:T(...) custom-call(f32[8,24,24]{2,1,0:T(8,128)} %refs_0_.2, ...), custom_call_target="tpu_custom_call" | custom-call | bytes 1048576 | tf_op jit(solution)/shard_map/first_cycle/pallas_call | solution.py:633
  10.3 1.1 %copy.20 = f32[128,1,640]{2,1,0:T(1,128)} copy(f32[128,1,640]{2,0,1:T(8,128)S(1)} %bitcast.25) | data formatting | bytes 655360 | tf_op jit(solution)/shard_map/all_to_all | solution.py:585
  11.3 11.5 %all-to-all-start = ((f32[128,1,640]{2,1,0:T(1,128)}), f32[128,1,640]{2,1,0:T(1,128)S(1)}, u32[]{:S(2)}, u32[]{:S(2)}) async-start(f32[128,1,640]{2,1,0:T(1,128)} %copy.20), calls=%async_computation | async-start | bytes 655360 | tf_op jit(solution)/shard_map/all_to_all | solution.py:585
  22.8 1.0 fixed_data.1
  23.9 10.6 %all-to-all-done = f32[128,1,640]{2,1,0:T(1,128)S(1)} async-done(((f32[128,1,640]{2,1,0:T(1,128)}), f32[128,1,640]{2,1,0:T(1,128)S(1)}, u32[]{:S(2)}, u32[]{:S(2)}) %all-to-all-start) | async-done | bytes 327712 | tf_op jit(solution)/shard_map/all_to_all | solution.py:585
  34.5 0.0 copy-done
  34.5 6.5 %next_cycle.2 = (f32[96,128]{1,0:T(8,128)S(1)}, f32[96,128]{1,0:T(8,128)S(1)}, f32[96,128]{1,0:T(8,128)S(1)}, f32[3,128]{1,0:T(4,128)S(1)}, f32[3,128]{1,0:T(4,1...) custom-call(f32[96,128]{1,0:T(8,128)S(1)} %get-tuple-element.56.u, ...), custom_call_target="tpu_custom_call" | custom-call | bytes 1048576 | tf_op jit(solution)/shard_map/next_cycle/pallas_call | solution.py:696
  41.0 0.9 collective-permute-start
  41.9 0.3 collective-permute-start.1
  42.3 1.6 %collective-permute-start.2 = (f32[3,128]{1,0:T(4,128)S(1)}, f32[3,128]{1,0:T(4,128)S(1)}, u32[]{:S(2)}, u32[]{:S(2)}) collective-permute-start(f32[3,128]{1,0:T(4,128)S(1)} %get-tuple-element.72), channel_id=1, source_target_pairs={{0,4},{1,5},{2,6},{3,7},{4,0},{5,1},{6,2},{7,3},{8,12},{9,13},{10,... | collective-permute-start | bytes 4616 | tf_op jit(solution)/shard_map/ppermute | solution.py:573
  43.9 0.5 collective-permute-start.3
  44.5 1.0 collective-permute-start.4
  45.5 0.5 contact_ends.1
  45.9 0.0 collective-permute-done.rest_0_
  46.0 0.0 collective-permute-done.1.rest_1_
  46.0 0.2 collective-permute-done.2.rest_2_
  46.2 0.4 collective-permute-done.3.rest_3_
  46.6 1.8 %collective-permute-done.4.rest_4_ = f32[3,128]{1,0:T(4,128)S(1)} collective-permute-done((f32[3,128]{1,0:T(4,128)S(1)}, f32[3,128]{1,0:T(4,128)S(1)}, u32[]{:S(2)}, u32[]{:S(2)}) %collective-permute-start.4) | collective-permute-done | bytes 1568 | tf_op jit(solution)/shard_map/ppermute | solution.py:573
  48.4 6.6 %next_cycle.3 = (f32[96,128]{1,0:T(8,128)S(1)}, f32[96,128]{1,0:T(8,128)S(1)}, f32[96,128]{1,0:T(8,128)S(1)}, f32[3,128]{1,0:T(4,128)S(1)}, f32[3,128]{1,0:T(4,1...) custom-call(f32[96,128]{1,0:T(8,128)S(1)} %get-tuple-element.67.u, ...), custom_call_target="tpu_custom_call" | custom-call | bytes 1048576 | tf_op jit(solution)/shard_map/next_cycle/pallas_call | solution.py:696
  55.0 2.1 %collective-permute-start.5 = (f32[3,128]{1,0:T(4,128)S(1)}, f32[3,128]{1,0:T(4,128)S(1)}, u32[]{:S(2)}, u32[]{:S(2)}) collective-permute-start(f32[3,128]{1,0:T(4,128)S(1)} %get-tuple-element.97), channel_id=1, source_target_pairs={{0,1},{1,0},{2,3},{3,2},{4,5},{5,4},{6,7},{7,6},{8,9},{9,8},{10,11... | collective-permute-start | bytes 4616 | tf_op jit(solution)/shard_map/ppermute | solution.py:573
  57.1 0.0 collective-permute-start.6
  57.1 2.8 %collective-permute-start.7 = (f32[3,128]{1,0:T(4,128)S(1)}, f32[3,128]{1,0:T(4,128)S(1)}, u32[]{:S(2)}, u32[]{:S(2)}) collective-permute-start(f32[3,128]{1,0:T(4,128)S(1)} %get-tuple-element.99), channel_id=1, source_target_pairs={{0,4},{1,5},{2,6},{3,7},{4,0},{5,1},{6,2},{7,3},{8,12},{9,13},{10,... | collective-permute-start | bytes 4616 | tf_op jit(solution)/shard_map/ppermute | solution.py:573
  59.9 1.2 %collective-permute-start.8 = (f32[3,128]{1,0:T(4,128)S(1)}, f32[3,128]{1,0:T(4,128)S(1)}, u32[]{:S(2)}, u32[]{:S(2)}) collective-permute-start(f32[3,128]{1,0:T(4,128)S(1)} %get-tuple-element.100), channel_id=1, source_target_pairs={{0,8},{1,9},{2,10},{3,11},{4,12},{5,13},{6,14},{7,15},{8,0},{9,1},... | collective-permute-start | bytes 4616 | tf_op jit(solution)/shard_map/ppermute | solution.py:573
  61.1 1.1 %collective-permute-start.9 = (f32[3,128]{1,0:T(4,128)S(1)}, f32[3,128]{1,0:T(4,128)S(1)}, u32[]{:S(2)}, u32[]{:S(2)}) collective-permute-start(f32[3,128]{1,0:T(4,128)S(1)} %get-tuple-element.101), channel_id=1, source_target_pairs={{0,16},{1,17},{2,18},{3,19},{4,20},{5,21},{6,22},{7,23},{8,24},{9,... | collective-permute-start | bytes 4616 | tf_op jit(solution)/shard_map/ppermute | solution.py:573
  62.2 2.4 %contact_base.1 = (f32[96,128]{1,0:T(8,128)S(1)}, f32[96,128]{1,0:T(8,128)S(1)}, f32[2,80,128]{2,1,0:T(8,128)S(1)}) custom-call(f32[96,128]{1,0:T(8,128)S(1)} %get-tuple-element.83.u, f32[96,128]{1,0:T(8,128)S(1)} %get-tuple-element.84.v, f32[96,128]{1,0:T(8,128)S(1)} %get-tuple-element.85.internal, f32[96,128]{1,0:T(8,128)S(1)} %get-tuple-element.63.fm, ...), custom_call_target="tpu_custom_call" | custom-call | bytes 1048576 | tf_op jit(solution)/shard_map/contact_base/pallas_call | solution.py:713
  64.6 0.0 collective-permute-done.5.rest_0_
  64.7 0.0 collective-permute-done.6.rest_1_
  64.7 0.0 collective-permute-done.7.rest_2_
  64.7 0.0 collective-permute-done.8.rest_3_
  64.7 0.4 collective-permute-done.9.rest_4_
  65.1 1.0 contact_dots.1
  66.1 0.2 copy.21
  66.3 16.0 %all_to_all.33 = f32[128,1,384]{2,1,0:T(1,128)S(1)} all-to-all(f32[128,1,384]{2,1,0:T(1,128)S(1)} %copy.21), channel_id=1, replica_groups=mesh['dom'=128] {'dom'}, dimensions={0} | all-to-all | bytes 393216 | tf_op jit(solution)/shard_map/all_to_all | solution.py:585
  82.3 2.7 %contact_forces.1 = (f32[96,128]{1,0:T(8,128)S(1)}, f32[16,128]{1,0:T(8,128)S(1)}, f32[16,128]{1,0:T(8,128)S(1)}) custom-call(f32[128,384]{1,0:T(8,128)S(1)} %get-tuple-element.103.dots, f32[128,384]{1,0:T(8,128)S(1)} %bitcast.24, s32[16,128]{1,0:T(8,128)S(1)} %get-tuple-element.76.slave, s32[16,128]{1,0:T(8,128)S(1)} %get-tuple-element.95.slot, ...), custom_call_target="tpu_custom_call" | custom-call | bytes 1048576 | tf_op jit(solution)/shard_map/contact_forces/pallas_call | solution.py:728
  85.0 0.7 collective-permute-start.10
  85.8 0.8 collective-permute-done.10.given
  86.6 0.3 copy.22
  87.0 15.2 %all_to_all.34 = f32[64,1,1280]{2,1,0:T(1,128)S(1)} all-to-all(f32[64,1,1280]{2,1,0:T(1,128)S(1)} %copy.22), channel_id=1, replica_groups={{0,2,4,6,8,10,12,14,16,18,20,22,24,26,28,30,32,34,36,38,40,42,44,46,48,..., dimensions={0} | all-to-all | bytes 655360 | tf_op jit(solution)/shard_map/all_to_all | solution.py:585
  102.2 0.1 part_totals.1.mine
  102.3 1.8 %collective-permute-start.11 = (f32[80,128]{1,0:T(8,128)S(1)}, f32[80,128]{1,0:T(8,128)S(1)}, u32[]{:S(2)}, u32[]{:S(2)}) collective-permute-start(f32[80,128]{1,0:T(8,128)S(1)} %part_totals.1.mine), channel_id=1, source_target_pairs={{0,1},{1,0},{2,3},{3,2},{4,5},{5,4},{6,7},{7,6},{8,9},{9,8},{10,11... | collective-permute-start | bytes 122888 | tf_op jit(solution)/shard_map/ppermute | solution.py:573
  104.1 0.7 nodal_velocity.1
  104.7 0.2 collective-permute-done.11.other
  104.9 0.7 part_motion.1
  (4 shorter events, 0.1 us)
Async XLA Ops:
  0.6 33.8 %copy-start = (s32[32]{0:T(128)S(1)}, s32[32]{0:T(128)}, u32[]{:S(2)}) copy-start(s32[32]{0:T(128)} %mat.3) | copy-start | bytes 388
  11.3 23.1 %all-to-all-start = ((f32[128,1,640]{2,1,0:T(1,128)}), f32[128,1,640]{2,1,0:T(1,128)S(1)}, u32[]{:S(2)}, u32[]{:S(2)}) async-start(f32[128,1,640]{2,1,0:T(1,128)} %copy.20), calls=%async_computation | async-start | bytes 655360 | tf_op jit(solution)/shard_map/all_to_all | solution.py:585
  41.0 4.9 %collective-permute-start = (f32[3,128]{1,0:T(4,128)S(1)}, f32[3,128]{1,0:T(4,128)S(1)}, u32[]{:S(2)}, u32[]{:S(2)}) collective-permute-start(f32[3,128]{1,0:T(4,128)S(1)} %get-tuple-element.70), channel_id=1, source_target_pairs={{0,1},{1,0},{2,3},{3,2},{4,5},{5,4},{6,7},{7,6},{8,9},{9,8},{10,11... | collective-permute-start | bytes 4616 | tf_op jit(solution)/shard_map/ppermute | solution.py:573
  41.9 4.0 %collective-permute-start.1 = (f32[3,128]{1,0:T(4,128)S(1)}, f32[3,128]{1,0:T(4,128)S(1)}, u32[]{:S(2)}, u32[]{:S(2)}) collective-permute-start(f32[3,128]{1,0:T(4,128)S(1)} %get-tuple-element.71), channel_id=1, source_target_pairs={{0,2},{1,3},{2,0},{3,1},{4,6},{5,7},{6,4},{7,5},{8,10},{9,11},{10,... | collective-permute-start | bytes 4616 | tf_op jit(solution)/shard_map/ppermute | solution.py:573
  42.3 3.9 %collective-permute-start.2 = (f32[3,128]{1,0:T(4,128)S(1)}, f32[3,128]{1,0:T(4,128)S(1)}, u32[]{:S(2)}, u32[]{:S(2)}) collective-permute-start(f32[3,128]{1,0:T(4,128)S(1)} %get-tuple-element.72), channel_id=1, source_target_pairs={{0,4},{1,5},{2,6},{3,7},{4,0},{5,1},{6,2},{7,3},{8,12},{9,13},{10,... | collective-permute-start | bytes 4616 | tf_op jit(solution)/shard_map/ppermute | solution.py:573
  43.9 2.7 %collective-permute-start.3 = (f32[3,128]{1,0:T(4,128)S(1)}, f32[3,128]{1,0:T(4,128)S(1)}, u32[]{:S(2)}, u32[]{:S(2)}) collective-permute-start(f32[3,128]{1,0:T(4,128)S(1)} %get-tuple-element.73), channel_id=1, source_target_pairs={{0,8},{1,9},{2,10},{3,11},{4,12},{5,13},{6,14},{7,15},{8,0},{9,1},... | collective-permute-start | bytes 4616 | tf_op jit(solution)/shard_map/ppermute | solution.py:573
  44.5 3.9 %collective-permute-start.4 = (f32[3,128]{1,0:T(4,128)S(1)}, f32[3,128]{1,0:T(4,128)S(1)}, u32[]{:S(2)}, u32[]{:S(2)}) collective-permute-start(f32[3,128]{1,0:T(4,128)S(1)} %get-tuple-element.74), channel_id=1, source_target_pairs={{0,16},{1,17},{2,18},{3,19},{4,20},{5,21},{6,22},{7,23},{8,24},{9,... | collective-permute-start | bytes 4616 | tf_op jit(solution)/shard_map/ppermute | solution.py:573
  55.0 9.7 %collective-permute-start.5 = (f32[3,128]{1,0:T(4,128)S(1)}, f32[3,128]{1,0:T(4,128)S(1)}, u32[]{:S(2)}, u32[]{:S(2)}) collective-permute-start(f32[3,128]{1,0:T(4,128)S(1)} %get-tuple-element.97), channel_id=1, source_target_pairs={{0,1},{1,0},{2,3},{3,2},{4,5},{5,4},{6,7},{7,6},{8,9},{9,8},{10,11... | collective-permute-start | bytes 4616 | tf_op jit(solution)/shard_map/ppermute | solution.py:573
  57.1 7.6 %collective-permute-start.6 = (f32[3,128]{1,0:T(4,128)S(1)}, f32[3,128]{1,0:T(4,128)S(1)}, u32[]{:S(2)}, u32[]{:S(2)}) collective-permute-start(f32[3,128]{1,0:T(4,128)S(1)} %get-tuple-element.98), channel_id=1, source_target_pairs={{0,2},{1,3},{2,0},{3,1},{4,6},{5,7},{6,4},{7,5},{8,10},{9,11},{10,... | collective-permute-start | bytes 4616 | tf_op jit(solution)/shard_map/ppermute | solution.py:573
  57.1 7.6 %collective-permute-start.7 = (f32[3,128]{1,0:T(4,128)S(1)}, f32[3,128]{1,0:T(4,128)S(1)}, u32[]{:S(2)}, u32[]{:S(2)}) collective-permute-start(f32[3,128]{1,0:T(4,128)S(1)} %get-tuple-element.99), channel_id=1, source_target_pairs={{0,4},{1,5},{2,6},{3,7},{4,0},{5,1},{6,2},{7,3},{8,12},{9,13},{10,... | collective-permute-start | bytes 4616 | tf_op jit(solution)/shard_map/ppermute | solution.py:573
  59.9 4.8 %collective-permute-start.8 = (f32[3,128]{1,0:T(4,128)S(1)}, f32[3,128]{1,0:T(4,128)S(1)}, u32[]{:S(2)}, u32[]{:S(2)}) collective-permute-start(f32[3,128]{1,0:T(4,128)S(1)} %get-tuple-element.100), channel_id=1, source_target_pairs={{0,8},{1,9},{2,10},{3,11},{4,12},{5,13},{6,14},{7,15},{8,0},{9,1},... | collective-permute-start | bytes 4616 | tf_op jit(solution)/shard_map/ppermute | solution.py:573
  61.1 3.9 %collective-permute-start.9 = (f32[3,128]{1,0:T(4,128)S(1)}, f32[3,128]{1,0:T(4,128)S(1)}, u32[]{:S(2)}, u32[]{:S(2)}) collective-permute-start(f32[3,128]{1,0:T(4,128)S(1)} %get-tuple-element.101), channel_id=1, source_target_pairs={{0,16},{1,17},{2,18},{3,19},{4,20},{5,21},{6,22},{7,23},{8,24},{9,... | collective-permute-start | bytes 4616 | tf_op jit(solution)/shard_map/ppermute | solution.py:573
  85.0 1.6 %collective-permute-start.10 = (f32[16,128]{1,0:T(8,128)S(1)}, f32[16,128]{1,0:T(8,128)S(1)}, u32[]{:S(2)}, u32[]{:S(2)}) collective-permute-start(f32[16,128]{1,0:T(8,128)S(1)} %get-tuple-element.108), channel_id=1, source_target_pairs={{0,1},{1,0},{2,3},{3,2},{4,5},{5,4},{6,7},{7,6},{8,9},{9,8},{10,11... | collective-permute-start | bytes 24584 | tf_op jit(solution)/shard_map/ppermute | solution.py:573
  102.3 2.6 %collective-permute-start.11 = (f32[80,128]{1,0:T(8,128)S(1)}, f32[80,128]{1,0:T(8,128)S(1)}, u32[]{:S(2)}, u32[]{:S(2)}) collective-permute-start(f32[80,128]{1,0:T(8,128)S(1)} %part_totals.1.mine), channel_id=1, source_target_pairs={{0,1},{1,0},{2,3},{3,2},{4,5},{5,4},{6,7},{7,6},{8,9},{9,8},{10,11... | collective-permute-start | bytes 122888 | tf_op jit(solution)/shard_map/ppermute | solution.py:573

commit v6 on v5

--- a/solution.py
+++ b/solution.py
@@ -29,12 +29,12 @@
 HBM = pl.BlockSpec(memory_space=pltpu.HBM)
 
 
-def call(body, outs, in_specs, name, scratch=(), flops=0):
+def call(body, outs, in_specs, name, scratch=(), flops=0, last=()):
     return pl.pallas_call(
         body,
         out_shape=[jax.ShapeDtypeStruct(s, d) for s, d in outs],
         in_specs=in_specs,
-        out_specs=[VMEM] * len(outs),
+        out_specs=[VMEM] * (len(outs) - len(last)) + list(last),
         scratch_shapes=list(scratch),
         compiler_params=pltpu.CompilerParams(vmem_limit_bytes=40 << 20),
         cost_estimate=pl.CostEstimate(flops=flops, bytes_accessed=1 << 20, transcendentals=0),
@@ -167,21 +167,26 @@
     down = lax.broadcasted_iota(jnp.int32, (LANES, LANES), 0)
     across = lax.broadcasted_iota(jnp.int32, (LANES, LANES), 1)
     before = jnp.where(down < across, 1.0, 0.0).astype(BF)
+    hits = [hits_of(owner[t : t + 1, :]) for t in range(16)]
+    counts = jnp.dot(jnp.concatenate([hit.astype(BF) for hit in hits], 0), before, preferred_element_type=F32)
     carry = jnp.zeros((LANES, 1), F32)
-    for pair in range(8):
+    for t, hit in enumerate(hits):
+        count = counts[t * LANES : (t + 1) * LANES, :] + carry
+        rank = jnp.sum(hit * count, axis=0, keepdims=True)
+        carry = carry + jnp.sum(hit, axis=1, keepdims=True)
+        slot[t : t + 1, :] = owner[t : t + 1, :] * 64 + rank.astype(jnp.int32)
+    for four in range(4):
         hits, pieces = [], []
-        for t in (2 * pair, 2 * pair + 1):
-            hit = hits_of(owner[t : t + 1, :])
-            hitb = hit.astype(BF)
-            count = jnp.dot(hitb, before, preferred_element_type=F32) + carry
-            rank = jnp.sum(hit * count, axis=0, keepdims=True)
-            carry = carry + jnp.sum(hit, axis=1, keepdims=True)
-            slot[t : t + 1, :] = owner[t : t + 1, :] * 64 + rank.astype(jnp.int32)
+        for t in range(4 * four, 4 * four + 4):
             vals = [normal[c : c + 1, t * LANES : (t + 1) * LANES] for c in range(3)]
-            one, two = slotted(hitb, rank, [*vals, master[t : t + 1, :].astype(F32)])
+            rank = (slot[t : t + 1, :] & 63).astype(F32)
+            one, two = slotted(
+                hits_of(owner[t : t + 1, :]).astype(BF), rank, [*vals, master[t : t + 1, :].astype(F32)]
+            )
             hits += one
             pieces += two
-        between(pair)
+        between(2 * four)
+        between(2 * four + 1)
         acc[...] += lax.dot_general(
             jnp.concatenate(hits, 1), jnp.concatenate(pieces, 1), NT, preferred_element_type=F32
         )
@@ -191,9 +196,8 @@
     return [(h, min(LANES, PARTS_SIZE - h * LANES)) for h in range(4)]
 
 
-def row_of_tile(row):
-    here = lax.broadcasted_iota(jnp.int32, (8, LANES), 0) == (row & 7)
-    return pl.ds(pl.multiple_of((row >> 3) << 3, 8), 8), here
+def every(first, stride, count=LANES):
+    return pl.ds(first, count, stride=stride)
 
 
 def copy_all(srcs, dsts, sems):
@@ -205,8 +209,8 @@
 
 def first_kernel(*refs):
     srcs = refs[:13]
-    u, v, fm, mass, idx, cols, shared, internal, send, slave, slot, normal = refs[13:25]
-    disp0, vel0, force0, shared0, owner, master, stiff, mat, accel, conn, tab, g, acc, table, sems = refs[25:]
+    u, v, fm, mass, idx, inv, cols, shared, internal, send, slave, slot, normal, mat = refs[13:27]
+    disp0, vel0, force0, shared0, owner, master, stiff, accel, conn, tab, g, acc, small, table, sems = refs[27:]
     dsts = (stiff, owner, master, normal, disp0, vel0, conn, mat, shared0, force0, mass, accel, slave)
     copies = copy_all(srcs, dsts, sems)
 
@@ -217,8 +221,9 @@
     for copy in copies[:4]:
         copy.wait()
     slots(owner, master, normal, slot, table, columns)
-    send[:, 0:256] = table[...]
-    send[:, 256:640] = jnp.zeros((LANES, 384), F32)
+    send[...] = jnp.zeros_like(send)
+    send[every(0, 5), :] = table[:, 0:128]
+    send[every(1, 5), :] = table[:, 128:256]
     for copy in copies[4:]:
         copy.wait()
     to_rows(disp0, u)
@@ -235,24 +240,7 @@
     shared[...] = jnp.zeros_like(shared)
     for b in range(NBR):
         shared[b : b + 1, :] = shared0[b]
-    elements(idx, mat, tab, cols, g, acc)
-    own = finish_internal(acc, internal, shared)
-    me = lax.axis_index("dom")
-    for b in range(NBR):
-        tile, here = row_of_tile(me ^ (1 << b))
-        for c in range(3):
-            row = jnp.broadcast_to(own[c][b : b + 1, :], (8, LANES))
-            send[tile, 256 + c * LANES : 256 + (c + 1) * LANES] += jnp.where(here, row, 0.0)
-
-
-def fixed_kernel(*refs):
-    pos0, part0, pmass0, pcenter0, pinertia0, normal, shared, mass, pos, part, inv, nrm, light, rigid = refs[:14]
-    pos1, pmass, pcenter, pinertia, small, sems = refs[14:]
-    copies = copy_all(
-        (pos0, part0, pmass0, pcenter0, pinertia0), (pos1, part, pmass, pcenter, pinertia), sems
-    )
     small[...] = jnp.zeros_like(small)
-    lane = lax.broadcasted_iota(jnp.int32, (8, LANES), 1)
     row = lax.broadcasted_iota(jnp.int32, (8, LANES), 0)
     held = row < NBR
     lo, hi = shared[...] & 127, shared[...] >> 7
@@ -260,7 +248,21 @@
     add_placed(small, lo, hi, kept)
     found = (small[0:64, :] + small[64:128, :]).astype(jnp.int32)
     inv[...] = found[0:ROWS, :] + found[ROWS : 2 * ROWS, :] * LANES
-    (weight,) = gather(mass, (0,), lo, hi)
+    elements(idx, mat, tab, cols, g, acc)
+    own = finish_internal(acc, internal, shared)
+    me = lax.axis_index("dom")
+    for b in range(NBR):
+        for c in range(3):
+            send[pl.ds(5 * (me ^ (1 << b)) + 2 + c, 1), :] = own[c][b : b + 1, :]
+
+
+def fixed_kernel(*refs):
+    pos0, part0, pmass0, pcenter0, pinertia0, normal, shared, mass, pos, part, nrm, light, rigid = refs[:13]
+    pos1, pmass, pcenter, pinertia, sems = refs[13:]
+    copies = copy_all(
+        (pos0, part0, pmass0, pcenter0, pinertia0), (pos1, part, pmass, pcenter, pinertia), sems
+    )
+    (weight,) = gather(mass, (0,), shared[...] & 127, shared[...] >> 7)
     light[...] = -TIME_STEP / weight
     for t in range(16):
         for c in range(3):
@@ -300,13 +302,7 @@
     if from_table:
         got, rest = rest[0], rest[1:]
         me = lax.axis_index("dom")
-        recv = []
-        for b in range(NBR):
-            tile, here = row_of_tile(me ^ (1 << b))
-            picked = [
-                jnp.where(here, got[tile, 256 + c * LANES : 256 + (c + 1) * LANES], 0.0) for c in range(3)
-            ]
-            recv.append([jnp.sum(x, axis=0, keepdims=True) for x in picked])
+        recv = [[got[pl.ds(5 * (me ^ (1 << b)) + 2 + c, 1), :] for c in range(3)] for b in range(NBR)]
     else:
         recv, rest = rows_of(rest[:NBR]), rest[NBR:]
     u2, v2, internal2 = rest[:3]
@@ -328,8 +324,7 @@
 def ends_kernel(got, slave, inv, midx, mnrm, code):
     left = lax.broadcasted_iota(jnp.int32, (64, LANES), 1) < 64
     for k, out in ((0, mnrm.at[0]), (1, mnrm.at[1]), (2, mnrm.at[2]), (3, midx)):
-        at = slice(LANES * (k // 2), LANES * (k // 2) + LANES)
-        top, low = got[0:64, at], got[64:128, at]
+        top, low = got[every(k // 2, 5, 64), :], got[every(320 + k // 2, 5, 64), :]
         if k % 2:
             out[...] = jnp.where(left, pltpu.roll(top, 64, 1), low).astype(out.dtype)
         else:
@@ -399,7 +394,7 @@
     acc[...] = jnp.zeros_like(acc)
     part_sums(part, vals, acc, True)
     moments = jnp.concatenate([acc[0:32, :] + acc[32:64, :], jnp.zeros((96, LANES), F32)], 0)
-    dots[:, 256:384] = moments.T
+    dots[every(2, 3), :] = moments.T
     table[...] = jnp.zeros_like(table)
     for i in range(4):
         hits, pieces = [], []
@@ -414,9 +409,9 @@
         )
     left = lax.broadcasted_iota(jnp.int32, (64, LANES), 1) < 64
     one, two = ab[0, 16:80, :], ab[1, 16:80, :]
-    dots[:, 0:128] = table[...]
-    dots[0:64, 128:256] = jnp.where(left, one, pltpu.roll(two, 64, 1))
-    dots[64:128, 128:256] = jnp.where(left, pltpu.roll(one, 64, 1), two)
+    dots[every(0, 3), :] = table[...]
+    dots[every(1, 3, 64), :] = jnp.where(left, one, pltpu.roll(two, 64, 1))
+    dots[every(193, 3, 64), :] = jnp.where(left, pltpu.roll(one, 64, 1), two)
 
 
 def part_sums(part, vals, acc, by_device):
@@ -453,8 +448,8 @@
     acc[...] = jnp.zeros_like(acc)
     acc2[...] = jnp.zeros_like(acc2)
     left = lax.broadcasted_iota(jnp.int32, (LANES, LANES), 1) < 64
-    as_slave = dots[:, 0:128] - got[:, 128:256]
-    as_master = got[:, 0:128] - dots[:, 128:256]
+    as_slave = dots[every(0, 3), :] - got[every(1, 3), :]
+    as_master = got[every(0, 3), :] - dots[every(1, 3), :]
     gap = jnp.where(left, as_slave, pltpu.roll(as_master, 64, 1))
     closing = jnp.where(left, pltpu.roll(as_slave, 64, 1), as_master)
     z = -gap / GAP_WIDTH
@@ -517,7 +512,7 @@
         give[k : k + 1, :] = jnp.where(even, high, low)
     keep[10:16, :] = jnp.zeros((6, LANES), F32)
     give[10:16, :] = jnp.zeros((6, LANES), F32)
-    moments = jnp.broadcast_to(jnp.sum(got[:, 256:384], axis=0, keepdims=True), (8, LANES))
+    moments = jnp.broadcast_to(jnp.sum(got[every(2, 3), :], axis=0, keepdims=True), (8, LANES))
     moments = jnp.where(lane < 96, 0.0, pltpu.roll(moments, 96, 1))
     keep[9:10, :] = keep[9:10, :] + moments[0:1, :]
 
@@ -531,16 +526,19 @@
 
 
 def spread_kernel(keep, given, out):
-    tile = keep[...] + given[...]
-    for k in range(10):
-        out[:, k * LANES : (k + 1) * LANES] = jnp.broadcast_to(tile[k : k + 1, :], (64, LANES))
+    tile = (keep[...] + given[...])[0:10, :]
+    four = jnp.concatenate([tile] * 4, 0)
+    for k in range(16):
+        out[40 * k : 40 * k + 40, :] = four
 
 
 def total_kernel(got, out):
-    for k in range(10):
-        out[k : k + 1, :] = jnp.sum(got[:, k * LANES : (k + 1) * LANES], axis=0, keepdims=True)
+    four = got[0:40, :]
+    for k in range(1, 16):
+        four = four + got[40 * k : 40 * k + 40, :]
+    out[0:10, :] = four[0:10, :] + four[10:20, :] + four[20:30, :] + four[30:40, :]
     out[10:16, :] = jnp.zeros((6, LANES), F32)
-    out[16:80, :] = pltpu.roll(got[:, 9 * LANES : 10 * LANES], 32, 1)
+    out[16:80, :] = pltpu.roll(got[every(9, 10, 64), :], 32, 1)
 
 
 def motion_kernel(mine, other, rigid, out):
@@ -582,7 +580,9 @@
 
 
 def swap(block, groups=None):
-    return lax.all_to_all(block, "dom", 0, 0, tiled=True, axis_index_groups=groups)
+    peers = len(groups[0]) if groups else lax.axis_size("dom")
+    flat = block.reshape(peers, 1, -1)
+    return lax.all_to_all(flat, "dom", 0, 0, tiled=True, axis_index_groups=groups).reshape(block.shape)
 
 
 def per_device(
@@ -606,7 +606,7 @@
     part_inertia,
 ):
     state = ((96, LANES), F32)
-    table = ((LANES, 5 * LANES), F32)
+    table = ((5 * LANES, LANES), F32)
     own = [((3, LANES), F32)] * NBR
     work = [
         pltpu.VMEM((96, LANES), F32),
@@ -630,7 +630,7 @@
     )
     rows, ints = ((ROWS, LANES), F32), jnp.int32
     whole, map_rows = pltpu.VMEM((3, 4096), F32), ((ROWS, LANES), ints)
-    u, v, fm, mass, idx, cols, shared, internal, send, slave, slot, normal = call(
+    u, v, fm, mass, idx, inv, cols, shared, internal, send, slave, slot, normal, mat = call(
         first_kernel,
         [
             state,
@@ -638,6 +638,7 @@
             state,
             rows,
             ((8, 4096), ints),
+            map_rows,
             ((192, 24, LANES), F32),
             ((8, LANES), ints),
             state,
@@ -645,6 +646,7 @@
             ((16, LANES), ints),
             ((16, LANES), ints),
             ((3, 2048), F32),
+            ((ROWS,), ints),
         ],
         [HBM] * 13,
         "first_cycle",
@@ -656,41 +658,17 @@
             pltpu.VMEM((16, LANES), ints),
             pltpu.VMEM((16, LANES), ints),
             pltpu.VMEM((8, 24, 24), F32),
-            pltpu.SMEM((ROWS,), ints),
             pltpu.SMEM((3,), F32),
             pltpu.VMEM((8, 4096), ints),
             *work,
+            pltpu.VMEM((LANES, LANES), F32),
             pltpu.VMEM((LANES, 2 * LANES), F32),
             pltpu.SemaphoreType.DMA((13,)),
         ],
+        last=[SMEM],
     )(*in_hbm(*inputs))
     got = swap(send)
     trio = ((3, PARTS_SIZE), F32)
-    pos, part, inv, nrm, light, rigid = call(
-        fixed_kernel,
-        [state, map_rows, map_rows, ((48, LANES), F32), ((8, LANES), F32), ((56, LANES), F32)],
-        [HBM] * 5 + [VMEM] * 3,
-        "fixed_data",
-        [
-            whole,
-            pltpu.VMEM((1, PARTS_SIZE), F32),
-            pltpu.VMEM(*trio),
-            pltpu.VMEM(*trio),
-            pltpu.VMEM((LANES, LANES), F32),
-            pltpu.SemaphoreType.DMA((5,)),
-        ],
-    )(
-        *in_hbm(
-            rest_pos,
-            part_of_node.reshape(ROWS, LANES),
-            part_mass.reshape(1, PARTS_SIZE),
-            part_center,
-            part_inertia,
-        ),
-        normal,
-        shared,
-        mass,
-    )
     recv = [got]
     for n in range(CYCLES - 1):
         u, v, internal, *mine = call(
@@ -699,7 +677,7 @@
             [VMEM] * 7 + [SMEM] + [VMEM] * (2 + len(recv)),
             "next_cycle",
             work,
-        )(u, v, internal, inv, fm, mass, idx, elem_material, cols, shared, *recv)
+        )(u, v, internal, inv, fm, mass, idx, mat, cols, shared, *recv)
         recv = [partner(mine[b], b) for b in range(NBR)]
         if n == 0:
             midx, mnrm, code = call(
@@ -708,7 +686,31 @@
                 [VMEM] * 3,
                 "contact_ends",
             )(later(got, mine), slave, inv)
-            recv, code = lax.optimization_barrier((recv, code))
+            pos, part, nrm, light, rigid = call(
+                fixed_kernel,
+                [state, map_rows, ((48, LANES), F32), ((8, LANES), F32), ((56, LANES), F32)],
+                [HBM] * 5 + [VMEM] * 3,
+                "fixed_data",
+                [
+                    whole,
+                    pltpu.VMEM((1, PARTS_SIZE), F32),
+                    pltpu.VMEM(*trio),
+                    pltpu.VMEM(*trio),
+                    pltpu.SemaphoreType.DMA((5,)),
+                ],
+            )(
+                *in_hbm(
+                    rest_pos,
+                    part_of_node.reshape(ROWS, LANES),
+                    part_mass.reshape(1, PARTS_SIZE),
+                    part_center,
+                    part_inertia,
+                ),
+                later(normal, mine),
+                shared,
+                mass,
+            )
+            recv, code, nrm = lax.optimization_barrier((recv, code, nrm))
     both = ((2, 80, LANES), F32)
     x, v, ab = call(
         base_kernel,
@@ -719,7 +721,7 @@
     )(u, v, internal, fm, mass, pos, slave, nrm, midx, mnrm)
     x, v, net, dots = call(
         dots_kernel,
-        [state, state, state, ((LANES, 3 * LANES), F32)],
+        [state, state, state, ((3 * LANES, LANES), F32)],
         [VMEM] * 18,
         "contact_dots",
         [pltpu.VMEM((64, LANES), F32), pltpu.VMEM((LANES, LANES), F32), pltpu.VMEM(*both)],
@@ -739,7 +741,7 @@
         ],
     )(dots, swap(dots), slave, slot, nrm, midx, mnrm, x, net, part)
     (nodal_velocity,) = call(nodal_kernel, [((3, 4096), F32)], [VMEM] * 3, "nodal_velocity")(v, contact, mass)
-    (spread,) = call(spread_kernel, [((64, 10 * LANES), F32)], [VMEM] * 2, "part_spread")(keep, partner(give, 0))
+    (spread,) = call(spread_kernel, [((640, LANES), F32)], [VMEM] * 2, "part_spread")(keep, partner(give, 0))
     chips = lax.axis_size("dom") // 2
     groups = [[2 * i + core for i in range(chips)] for core in range(2)]
     (total,) = call(total_kernel, [((80, LANES), F32)], [VMEM], "part_totals")(swap(spread, groups))

time: 106 us -> 104 us (0.981)
  blocking collectives: 31.2 us -> 54.2 us
  waiting for transfers between devices: 14.4 us -> 2.89 us
  starting transfers between devices: 25.7 us -> 14.2 us
  local copies, waits for them, and re-layouts: 1.66 us -> 0 us
    all_to_all x2 -> x3, blocking collectives: 31.2 us -> 54.2 us  [swap(): lax.all_to_all(flat, 'dom', 0, 0, tiled=True, axis_index_groups=groups)]
    all_to_all x1 -> x0, starting transfers between devices: 11.5 us -> none  [swap(): lax.all_to_all(block, 'dom', 0, 0, tiled=True, axis_index_groups=groups)]
    all_to_all x1 -> x0, waiting for transfers between devices: 10.6 us -> none  [swap(): lax.all_to_all(block, 'dom', 0, 0, tiled=True, axis_index_groups=groups)]
    all_to_all x3 -> x0, local copies, waits for them, and re-layouts: 1.6 us -> none  [swap(): lax.all_to_all(block, 'dom', 0, 0, tiled=True, axis_index_groups=groups)]
  transfers between devices with their start and end apart: 13 -> 12, of which waited for: 7 -> 4; matrix products, arithmetic and copies ran while one was open for 0% -> 0% of each run, Pallas kernels for 4% -> 4%
where the time goes in v6:
time: 104 us; the launch traced here: 103 us
  blocking collectives  54.2 us (52%)
  Pallas kernels  31.4 us (30%)
  starting transfers between devices  14.2 us (14%)
  waiting for transfers between devices  2.89 us (3%)
    all_to_all x3, blocking collectives, swap(): lax.all_to_all(flat, 'dom', 0, 0, tiled=True, axis_index_groups=groups)  54.2 us
    ppermute x12, starting transfers between devices, partner(): lax.ppermute(block, 'dom', [(i, i ^ 1 << apart) for i in range(count)])  14.2 us
    pallas_call x2, Pallas kernels, per_device(): call(functools.partial(next_kernel, n == 0), [state, state, state, *own],...  13.6 us
    pallas_call x1, Pallas kernels, per_device(): call(first_kernel, [state, state, state, rows, ((8, 4096), ints), map_row...  8.81 us
    ppermute x12, waiting for transfers between devices, partner(): lax.ppermute(block, 'dom', [(i, i ^ 1 << apart) for i in range(count)])  2.89 us
    pallas_call x1, Pallas kernels, per_device(): call(contact_kernel, [state, half, half], [VMEM] * 10, 'contact_forces',...  2.68 us
    pallas_call x1, Pallas kernels, per_device(): call(base_kernel, [state, state, both], [VMEM] * 10, 'contact_base', [plt...  2.42 us
  transfers between devices with their start and end apart: 12, of which 4 were waited for; matrix products, arithmetic and copies ran while one was open for 0% of the time, Pallas kernels for 4%

profile of v6, /device:TPU:1, one launch (start us, length us, event | category | flops | bytes accessed | tf_op | source)
XLA Modules:
  0.0 103.5 jit_solution(2341219078082315810)
XLA Ops:
  0.6 8.8 %first_cycle.1 = (f32[96,128]{1,0:T(8,128)S(1)}, f32[96,128]{1,0:T(8,128)S(1)}, f32[96,128]{1,0:T(8,128)S(1)}, f32[32,128]{1,0:T(8,128)S(1)}, s32[8,4096]{1,0:T(...) custom-call(f32[8,24,24]{2,1,0:T(8,128)} %refs_0_.2, ...), custom_call_target="tpu_custom_call" | custom-call | bytes 1048576 | tf_op jit(solution)/shard_map/first_cycle/pallas_call | solution.py:633
  9.5 22.9 %all_to_all.15 = f32[128,1,640]{2,1,0:T(1,128)S(1)} all-to-all(f32[128,1,640]{2,1,0:T(1,128)S(1)} %bitcast.19), channel_id=1, replica_groups=mesh['dom'=128] {'dom'}, dimensions={0} | all-to-all | bytes 655360 | tf_op jit(solution)/shard_map/all_to_all | solution.py:585
  32.4 6.8 %next_cycle.2 = (f32[96,128]{1,0:T(8,128)S(1)}, f32[96,128]{1,0:T(8,128)S(1)}, f32[96,128]{1,0:T(8,128)S(1)}, f32[3,128]{1,0:T(4,128)S(1)}, f32[3,128]{1,0:T(4,1...) custom-call(f32[96,128]{1,0:T(8,128)S(1)} %get-tuple-element.59.u, ...), custom_call_target="tpu_custom_call" | custom-call | bytes 1048576 | tf_op jit(solution)/shard_map/next_cycle/pallas_call | solution.py:674
  39.2 1.0 collective-permute-start
  40.1 0.3 collective-permute-start.1
  40.4 1.6 %collective-permute-start.2 = (f32[3,128]{1,0:T(4,128)S(1)}, f32[3,128]{1,0:T(4,128)S(1)}, u32[]{:S(2)}, u32[]{:S(2)}) collective-permute-start(f32[3,128]{1,0:T(4,128)S(1)} %get-tuple-element.75), channel_id=1, source_target_pairs={{0,4},{1,5},{2,6},{3,7},{4,0},{5,1},{6,2},{7,3},{8,12},{9,13},{10,... | collective-permute-start | bytes 4616 | tf_op jit(solution)/shard_map/ppermute | solution.py:571
  42.1 0.5 collective-permute-start.3
  42.6 1.1 %collective-permute-start.4 = (f32[3,128]{1,0:T(4,128)S(1)}, f32[3,128]{1,0:T(4,128)S(1)}, u32[]{:S(2)}, u32[]{:S(2)}) collective-permute-start(f32[3,128]{1,0:T(4,128)S(1)} %get-tuple-element.77), channel_id=1, source_target_pairs={{0,16},{1,17},{2,18},{3,19},{4,20},{5,21},{6,22},{7,23},{8,24},{9,... | collective-permute-start | bytes 4616 | tf_op jit(solution)/shard_map/ppermute | solution.py:571
  43.7 0.5 contact_ends.1
  44.1 0.9 fixed_data.1
  45.1 0.0 collective-permute-done.rest_0_
  45.1 0.0 collective-permute-done.1.rest_1_
  45.1 0.0 collective-permute-done.2.rest_2_
  45.1 0.0 collective-permute-done.3.rest_3_
  45.1 1.4 %collective-permute-done.4.rest_4_ = f32[3,128]{1,0:T(4,128)S(1)} collective-permute-done((f32[3,128]{1,0:T(4,128)S(1)}, f32[3,128]{1,0:T(4,128)S(1)}, u32[]{:S(2)}, u32[]{:S(2)}) %collective-permute-start.4) | collective-permute-done | bytes 1568 | tf_op jit(solution)/shard_map/ppermute | solution.py:571
  46.5 6.8 %next_cycle.3 = (f32[96,128]{1,0:T(8,128)S(1)}, f32[96,128]{1,0:T(8,128)S(1)}, f32[96,128]{1,0:T(8,128)S(1)}, f32[3,128]{1,0:T(4,128)S(1)}, f32[3,128]{1,0:T(4,1...) custom-call(f32[96,128]{1,0:T(8,128)S(1)} %get-tuple-element.70.u, ...), custom_call_target="tpu_custom_call" | custom-call | bytes 1048576 | tf_op jit(solution)/shard_map/next_cycle/pallas_call | solution.py:674
  53.4 2.2 %collective-permute-start.5 = (f32[3,128]{1,0:T(4,128)S(1)}, f32[3,128]{1,0:T(4,128)S(1)}, u32[]{:S(2)}, u32[]{:S(2)}) collective-permute-start(f32[3,128]{1,0:T(4,128)S(1)} %get-tuple-element.103), channel_id=1, source_target_pairs={{0,1},{1,0},{2,3},{3,2},{4,5},{5,4},{6,7},{7,6},{8,9},{9,8},{10,11... | collective-permute-start | bytes 4616 | tf_op jit(solution)/shard_map/ppermute | solution.py:571
  55.6 0.0 collective-permute-start.6
  55.6 2.8 %collective-permute-start.7 = (f32[3,128]{1,0:T(4,128)S(1)}, f32[3,128]{1,0:T(4,128)S(1)}, u32[]{:S(2)}, u32[]{:S(2)}) collective-permute-start(f32[3,128]{1,0:T(4,128)S(1)} %get-tuple-element.105), channel_id=1, source_target_pairs={{0,4},{1,5},{2,6},{3,7},{4,0},{5,1},{6,2},{7,3},{8,12},{9,13},{10,... | collective-permute-start | bytes 4616 | tf_op jit(solution)/shard_map/ppermute | solution.py:571
  58.4 1.2 %collective-permute-start.8 = (f32[3,128]{1,0:T(4,128)S(1)}, f32[3,128]{1,0:T(4,128)S(1)}, u32[]{:S(2)}, u32[]{:S(2)}) collective-permute-start(f32[3,128]{1,0:T(4,128)S(1)} %get-tuple-element.106), channel_id=1, source_target_pairs={{0,8},{1,9},{2,10},{3,11},{4,12},{5,13},{6,14},{7,15},{8,0},{9,1},... | collective-permute-start | bytes 4616 | tf_op jit(solution)/shard_map/ppermute | solution.py:571
  59.6 1.0 %collective-permute-start.9 = (f32[3,128]{1,0:T(4,128)S(1)}, f32[3,128]{1,0:T(4,128)S(1)}, u32[]{:S(2)}, u32[]{:S(2)}) collective-permute-start(f32[3,128]{1,0:T(4,128)S(1)} %get-tuple-element.107), channel_id=1, source_target_pairs={{0,16},{1,17},{2,18},{3,19},{4,20},{5,21},{6,22},{7,23},{8,24},{9,... | collective-permute-start | bytes 4616 | tf_op jit(solution)/shard_map/ppermute | solution.py:571
  60.6 2.4 %contact_base.1 = (f32[96,128]{1,0:T(8,128)S(1)}, f32[96,128]{1,0:T(8,128)S(1)}, f32[2,80,128]{2,1,0:T(8,128)S(1)}) custom-call(f32[96,128]{1,0:T(8,128)S(1)} %get-tuple-element.89.u, f32[96,128]{1,0:T(8,128)S(1)} %get-tuple-element.90.v, f32[96,128]{1,0:T(8,128)S(1)} %get-tuple-element.91.internal, f32[96,128]{1,0:T(8,128)S(1)} %get-tuple-element.63.fm, ...), custom_call_target="tpu_custom_call" | custom-call | bytes 1048576 | tf_op jit(solution)/shard_map/contact_base/pallas_call | solution.py:715
  63.0 0.0 collective-permute-done.5.rest_0_
  63.1 0.0 collective-permute-done.6.rest_1_
  63.1 0.0 collective-permute-done.7.rest_2_
  63.1 0.0 collective-permute-done.8.rest_3_
  63.1 0.4 collective-permute-done.9.rest_4_
  63.5 1.0 contact_dots.1
  64.5 16.0 %all_to_all.16 = f32[128,1,384]{2,1,0:T(1,128)S(1)} all-to-all(f32[128,1,384]{2,1,0:T(1,128)S(1)} %bitcast.17), channel_id=1, replica_groups=mesh['dom'=128] {'dom'}, dimensions={0} | all-to-all | bytes 393216 | tf_op jit(solution)/shard_map/all_to_all | solution.py:585
  80.5 2.7 %contact_forces.1 = (f32[96,128]{1,0:T(8,128)S(1)}, f32[16,128]{1,0:T(8,128)S(1)}, f32[16,128]{1,0:T(8,128)S(1)}) custom-call(f32[384,128]{1,0:T(8,128)S(1)} %get-tuple-element.109.dots, f32[384,128]{1,0:T(8,128)S(1)} %bitcast.18, s32[16,128]{1,0:T(8,128)S(1)} %get-tuple-element.79.slave, s32[16,128]{1,0:T(8,128)S(1)} %get-tuple-element.101.slot, ...), custom_call_target="tpu_custom_call" | custom-call | bytes 1048576 | tf_op jit(solution)/shard_map/contact_forces/pallas_call | solution.py:730
  83.2 0.7 collective-permute-start.10
  84.0 0.8 collective-permute-done.10.given
  84.8 15.2 %all_to_all.17 = f32[64,1,1280]{2,1,0:T(1,128)S(1)} all-to-all(f32[64,1,1280]{2,1,0:T(1,128)S(1)} %bitcast.15), channel_id=1, replica_groups={{0,2,4,6,8,10,12,14,16,18,20,22,24,26,28,30,32,34,36,38,40,42,44,46,48,..., dimensions={0} | all-to-all | bytes 655360 | tf_op jit(solution)/shard_map/all_to_all | solution.py:585
  100.0 0.1 part_totals.1.mine
  100.1 1.8 %collective-permute-start.11 = (f32[80,128]{1,0:T(8,128)S(1)}, f32[80,128]{1,0:T(8,128)S(1)}, u32[]{:S(2)}, u32[]{:S(2)}) collective-permute-start(f32[80,128]{1,0:T(8,128)S(1)} %part_totals.1.mine), channel_id=1, source_target_pairs={{0,1},{1,0},{2,3},{3,2},{4,5},{5,4},{6,7},{7,6},{8,9},{9,8},{10,11... | collective-permute-start | bytes 122888 | tf_op jit(solution)/shard_map/ppermute | solution.py:571
  101.9 0.7 nodal_velocity.1
  102.6 0.2 collective-permute-done.11.other
  102.8 0.7 part_motion.1
  (1 shorter events, 0.0 us)
Async XLA Ops:
  39.2 5.9 %collective-permute-start = (f32[3,128]{1,0:T(4,128)S(1)}, f32[3,128]{1,0:T(4,128)S(1)}, u32[]{:S(2)}, u32[]{:S(2)}) collective-permute-start(f32[3,128]{1,0:T(4,128)S(1)} %get-tuple-element.73), channel_id=1, source_target_pairs={{0,1},{1,0},{2,3},{3,2},{4,5},{5,4},{6,7},{7,6},{8,9},{9,8},{10,11... | collective-permute-start | bytes 4616 | tf_op jit(solution)/shard_map/ppermute | solution.py:571
  40.1 5.0 %collective-permute-start.1 = (f32[3,128]{1,0:T(4,128)S(1)}, f32[3,128]{1,0:T(4,128)S(1)}, u32[]{:S(2)}, u32[]{:S(2)}) collective-permute-start(f32[3,128]{1,0:T(4,128)S(1)} %get-tuple-element.74), channel_id=1, source_target_pairs={{0,2},{1,3},{2,0},{3,1},{4,6},{5,7},{6,4},{7,5},{8,10},{9,11},{10,... | collective-permute-start | bytes 4616 | tf_op jit(solution)/shard_map/ppermute | solution.py:571
  40.4 4.7 %collective-permute-start.2 = (f32[3,128]{1,0:T(4,128)S(1)}, f32[3,128]{1,0:T(4,128)S(1)}, u32[]{:S(2)}, u32[]{:S(2)}) collective-permute-start(f32[3,128]{1,0:T(4,128)S(1)} %get-tuple-element.75), channel_id=1, source_target_pairs={{0,4},{1,5},{2,6},{3,7},{4,0},{5,1},{6,2},{7,3},{8,12},{9,13},{10,... | collective-permute-start | bytes 4616 | tf_op jit(solution)/shard_map/ppermute | solution.py:571
  42.1 3.0 %collective-permute-start.3 = (f32[3,128]{1,0:T(4,128)S(1)}, f32[3,128]{1,0:T(4,128)S(1)}, u32[]{:S(2)}, u32[]{:S(2)}) collective-permute-start(f32[3,128]{1,0:T(4,128)S(1)} %get-tuple-element.76), channel_id=1, source_target_pairs={{0,8},{1,9},{2,10},{3,11},{4,12},{5,13},{6,14},{7,15},{8,0},{9,1},... | collective-permute-start | bytes 4616 | tf_op jit(solution)/shard_map/ppermute | solution.py:571
  42.6 3.9 %collective-permute-start.4 = (f32[3,128]{1,0:T(4,128)S(1)}, f32[3,128]{1,0:T(4,128)S(1)}, u32[]{:S(2)}, u32[]{:S(2)}) collective-permute-start(f32[3,128]{1,0:T(4,128)S(1)} %get-tuple-element.77), channel_id=1, source_target_pairs={{0,16},{1,17},{2,18},{3,19},{4,20},{5,21},{6,22},{7,23},{8,24},{9,... | collective-permute-start | bytes 4616 | tf_op jit(solution)/shard_map/ppermute | solution.py:571
  53.4 9.7 %collective-permute-start.5 = (f32[3,128]{1,0:T(4,128)S(1)}, f32[3,128]{1,0:T(4,128)S(1)}, u32[]{:S(2)}, u32[]{:S(2)}) collective-permute-start(f32[3,128]{1,0:T(4,128)S(1)} %get-tuple-element.103), channel_id=1, source_target_pairs={{0,1},{1,0},{2,3},{3,2},{4,5},{5,4},{6,7},{7,6},{8,9},{9,8},{10,11... | collective-permute-start | bytes 4616 | tf_op jit(solution)/shard_map/ppermute | solution.py:571
  55.6 7.5 %collective-permute-start.6 = (f32[3,128]{1,0:T(4,128)S(1)}, f32[3,128]{1,0:T(4,128)S(1)}, u32[]{:S(2)}, u32[]{:S(2)}) collective-permute-start(f32[3,128]{1,0:T(4,128)S(1)} %get-tuple-element.104), channel_id=1, source_target_pairs={{0,2},{1,3},{2,0},{3,1},{4,6},{5,7},{6,4},{7,5},{8,10},{9,11},{10,... | collective-permute-start | bytes 4616 | tf_op jit(solution)/shard_map/ppermute | solution.py:571
  55.6 7.5 %collective-permute-start.7 = (f32[3,128]{1,0:T(4,128)S(1)}, f32[3,128]{1,0:T(4,128)S(1)}, u32[]{:S(2)}, u32[]{:S(2)}) collective-permute-start(f32[3,128]{1,0:T(4,128)S(1)} %get-tuple-element.105), channel_id=1, source_target_pairs={{0,4},{1,5},{2,6},{3,7},{4,0},{5,1},{6,2},{7,3},{8,12},{9,13},{10,... | collective-permute-start | bytes 4616 | tf_op jit(solution)/shard_map/ppermute | solution.py:571
  58.4 4.7 %collective-permute-start.8 = (f32[3,128]{1,0:T(4,128)S(1)}, f32[3,128]{1,0:T(4,128)S(1)}, u32[]{:S(2)}, u32[]{:S(2)}) collective-permute-start(f32[3,128]{1,0:T(4,128)S(1)} %get-tuple-element.106), channel_id=1, source_target_pairs={{0,8},{1,9},{2,10},{3,11},{4,12},{5,13},{6,14},{7,15},{8,0},{9,1},... | collective-permute-start | bytes 4616 | tf_op jit(solution)/shard_map/ppermute | solution.py:571
  59.6 3.9 %collective-permute-start.9 = (f32[3,128]{1,0:T(4,128)S(1)}, f32[3,128]{1,0:T(4,128)S(1)}, u32[]{:S(2)}, u32[]{:S(2)}) collective-permute-start(f32[3,128]{1,0:T(4,128)S(1)} %get-tuple-element.107), channel_id=1, source_target_pairs={{0,16},{1,17},{2,18},{3,19},{4,20},{5,21},{6,22},{7,23},{8,24},{9,... | collective-permute-start | bytes 4616 | tf_op jit(solution)/shard_map/ppermute | solution.py:571
  83.2 1.6 %collective-permute-start.10 = (f32[16,128]{1,0:T(8,128)S(1)}, f32[16,128]{1,0:T(8,128)S(1)}, u32[]{:S(2)}, u32[]{:S(2)}) collective-permute-start(f32[16,128]{1,0:T(8,128)S(1)} %get-tuple-element.114), channel_id=1, source_target_pairs={{0,1},{1,0},{2,3},{3,2},{4,5},{5,4},{6,7},{7,6},{8,9},{9,8},{10,11... | collective-permute-start | bytes 24584 | tf_op jit(solution)/shard_map/ppermute | solution.py:571
  100.1 2.6 %collective-permute-start.11 = (f32[80,128]{1,0:T(8,128)S(1)}, f32[80,128]{1,0:T(8,128)S(1)}, u32[]{:S(2)}, u32[]{:S(2)}) collective-permute-start(f32[80,128]{1,0:T(8,128)S(1)} %part_totals.1.mine), channel_id=1, source_target_pairs={{0,1},{1,0},{2,3},{3,2},{4,5},{5,4},{6,7},{7,6},{8,9},{9,8},{10,11... | collective-permute-start | bytes 122888 | tf_op jit(solution)/shard_map/ppermute | solution.py:571

commit v7 on v6

--- a/solution.py
+++ b/solution.py
@@ -22,19 +22,19 @@
 LANES = 128
 ROWS = 32
 NBR = 5
-TOGETHER = 4
+TOGETHER = 8
 
 VMEM = pl.BlockSpec(memory_space=pltpu.VMEM)
 SMEM = pl.BlockSpec(memory_space=pltpu.SMEM)
 HBM = pl.BlockSpec(memory_space=pltpu.HBM)
 
 
-def call(body, outs, in_specs, name, scratch=(), flops=0, last=()):
+def call(body, outs, in_specs, name, scratch=(), flops=0):
     return pl.pallas_call(
         body,
         out_shape=[jax.ShapeDtypeStruct(s, d) for s, d in outs],
         in_specs=in_specs,
-        out_specs=[VMEM] * (len(outs) - len(last)) + list(last),
+        out_specs=[VMEM] * len(outs),
         scratch_shapes=list(scratch),
         compiler_params=pltpu.CompilerParams(vmem_limit_bytes=40 << 20),
         cost_estimate=pl.CostEstimate(flops=flops, bytes_accessed=1 << 20, transcendentals=0),
@@ -57,11 +57,6 @@
     return acc
 
 
-def halves(x):
-    first = x.astype(BF)
-    return first, (x - first.astype(F32)).astype(BF)
-
-
 def wide(x, a, n):
     row = jnp.broadcast_to(x[a : a + 1, :].astype(F32), (16, LANES)).astype(BF)
     return jnp.concatenate([row] * (n // 16), 0)
@@ -71,30 +66,30 @@
     return lax.broadcasted_iota(jnp.int32, (n, LANES), 0).astype(F32).astype(BF)
 
 
-def place(lo, hi, vals):
-    lof, hif = lo.astype(F32), hi.astype(F32)
+def place(lo, hi, vals, held, base):
     it = iota_rows(LANES)
-    split = [halves(v) for v in vals]
     one, zero = jnp.ones((LANES, LANES), BF), jnp.zeros((LANES, LANES), BF)
+    first = [v.astype(BF).astype(F32) for v in vals]
+    items = first + [v - x for v, x in zip(vals, first)] + [lo.astype(F32), hi.astype(F32)]
+    for k, x in enumerate(items):
+        held[base + 8 * k : base + 8 * k + 8, :] = x
+
+    def spread(k, a, n):
+        at = base + 8 * k + a
+        row = jnp.broadcast_to(held[at : at + 1, :], (16, LANES)).astype(BF)
+        return jnp.concatenate([row] * (n // 16), 0)
+
     left, right = [], []
+    count = 2 * len(vals)
     for a in range(8):
-        right.append(jnp.where(wide(lof, a, LANES) == it, one, zero))
-        mask = wide(hif, a, ROWS) == it[:ROWS]
-        left.append(
-            jnp.concatenate(
-                [
-                    jnp.where(mask, wide(split[c][s], a, ROWS), zero[:ROWS])
-                    for s in range(2)
-                    for c in range(len(vals))
-                ],
-                0,
-            )
-        )
+        right.append(jnp.where(spread(count, a, LANES) == it, one, zero))
+        mask = spread(count + 1, a, ROWS) == it[:ROWS]
+        left.append(jnp.concatenate([jnp.where(mask, spread(k, a, ROWS), zero[:ROWS]) for k in range(count)], 0))
     return jnp.concatenate(left, 1), jnp.concatenate(right, 1)
 
 
-def add_placed(acc, lo, hi, vals):
-    left, right = place(lo, hi, vals)
+def add_placed(acc, lo, hi, vals, held):
+    left, right = place(lo, hi, vals, held, 0)
     acc[...] += lax.dot_general(left, right, NT, preferred_element_type=F32)
 
 
@@ -104,7 +99,7 @@
             dst[c * ROWS + h : c * ROWS + h + 1, :] = src[c : c + 1, h * LANES : (h + 1) * LANES]
 
 
-def elements(idx, mat, tab, cols, g, acc):
+def elements(idx, mat, tab, cols, g, acc, held):
     acc[...] = jnp.zeros_like(acc)
     steps = ROWS // TOGETHER
 
@@ -130,7 +125,7 @@
                 col = cols.at[first + j]
                 row = jnp.broadcast_to(g[q * 24 + j : q * 24 + j + 1, :], (8, LANES))
                 force = [force[c] + col[8 * c : 8 * c + 8, :] * row for c in range(3)]
-            one, two = place(*corners(i, q), force)
+            one, two = place(*corners(i, q), force, held, 64 * q)
             left.append(one)
             right.append(two)
         acc[...] += lax.dot_general(
@@ -208,10 +203,10 @@
 
 
 def first_kernel(*refs):
-    srcs = refs[:13]
-    u, v, fm, mass, idx, inv, cols, shared, internal, send, slave, slot, normal, mat = refs[13:27]
-    disp0, vel0, force0, shared0, owner, master, stiff, accel, conn, tab, g, acc, small, table, sems = refs[27:]
-    dsts = (stiff, owner, master, normal, disp0, vel0, conn, mat, shared0, force0, mass, accel, slave)
+    srcs = [*refs[:13], refs[7]]
+    u, v, fm, mass, idx, inv, cols, shared, internal, send, slave, slot, normal, matv = refs[13:27]
+    disp0, vel0, force0, shared0, owner, master, stiff, accel, conn, mat, tab, g, acc, held, small, table, sems = refs[27:]
+    dsts = (stiff, owner, master, normal, disp0, vel0, conn, mat, shared0, force0, mass, accel, slave, matv)
     copies = copy_all(srcs, dsts, sems)
 
     def columns(m):
@@ -242,13 +237,13 @@
         shared[b : b + 1, :] = shared0[b]
     small[...] = jnp.zeros_like(small)
     row = lax.broadcasted_iota(jnp.int32, (8, LANES), 0)
-    held = row < NBR
+    listed = row < NBR
     lo, hi = shared[...] & 127, shared[...] >> 7
-    kept = [jnp.where(held, lane, 0).astype(F32), jnp.where(held, row + 1, 0).astype(F32)]
-    add_placed(small, lo, hi, kept)
+    kept = [jnp.where(listed, lane, 0).astype(F32), jnp.where(listed, row + 1, 0).astype(F32)]
+    add_placed(small, lo, hi, kept, held)
     found = (small[0:64, :] + small[64:128, :]).astype(jnp.int32)
     inv[...] = found[0:ROWS, :] + found[ROWS : 2 * ROWS, :] * LANES
-    elements(idx, mat, tab, cols, g, acc)
+    elements(idx, mat, tab, cols, g, acc, held)
     own = finish_internal(acc, internal, shared)
     me = lax.axis_index("dom")
     for b in range(NBR):
@@ -298,7 +293,7 @@
     return [[ref[c : c + 1, :] for c in range(3)] for ref in refs]
 
 
-def next_kernel(from_table, u, v, internal, inv, fm, mass, idx, mat, cols, shared, *rest):
+def next_kernel(from_table, u, v, internal, inv, fm, mass, idx, matv, cols, shared, *rest):
     if from_table:
         got, rest = rest[0], rest[1:]
         me = lax.axis_index("dom")
@@ -307,14 +302,17 @@
         recv, rest = rows_of(rest[:NBR]), rest[NBR:]
     u2, v2, internal2 = rest[:3]
     own = rest[3:8]
-    tab, g, acc = rest[8:]
+    tab, g, acc, held, mat, sem = rest[8:]
+    numbers = pltpu.make_async_copy(matv, mat, sem)
+    numbers.start()
     for c in range(3):
         for r in range(0, ROWS, 8):
             at, disp, speed, _ = update(u, v, internal, inv, fm, mass, recv, c, r)
             u2[at, :] = disp
             v2[at, :] = speed
             tab[at, :] = disp + DAMP_RATIO * speed
-    elements(idx, mat, tab, cols, g, acc)
+    numbers.wait()
+    elements(idx, mat, tab, cols, g, acc, held)
     vals = finish_internal(acc, internal2, shared)
     for b in range(NBR):
         for c in range(3):
@@ -443,7 +441,7 @@
 
 
 def contact_kernel(
-    dots, got, slave, slot, nrm, midx, mnrm, x, net, part, contact, keep, give, acc, tot, acc2, push, mine
+    dots, got, slave, slot, nrm, midx, mnrm, x, net, part, contact, keep, give, acc, tot, acc2, push, mine, held
 ):
     acc[...] = jnp.zeros_like(acc)
     acc2[...] = jnp.zeros_like(acc2)
@@ -464,7 +462,7 @@
         for q in range(4):
             at = pl.ds(pl.multiple_of(i * 32 + q * 8, 8), 8)
             here, size = midx[at, :], push[at, :]
-            pair = place(here & 127, here >> 7, [size * mnrm[c, at, :] for c in range(3)])
+            pair = place(here & 127, here >> 7, [size * mnrm[c, at, :] for c in range(3)], held, 64 * q)
             one.append(pair[0])
             two.append(pair[1])
         acc[...] += lax.dot_general(
@@ -477,7 +475,8 @@
     for r in (0, 8):
         here, at = slave[r : r + 8, :], slot[r : r + 8, :]
         (size,) = gather(mine, (0,), ((at >> 12) << 6) + (at & 63), (at >> 6) & 63, 64)
-        pair = place(here & 127, here >> 7, [size * nrm[16 * c + r : 16 * c + r + 8, :] for c in range(3)])
+        w = [size * nrm[16 * c + r : 16 * c + r + 8, :] for c in range(3)]
+        pair = place(here & 127, here >> 7, w, held, 256 + 8 * r)
         one.append(pair[0])
         two.append(pair[1])
     acc[...] += lax.dot_general(
@@ -612,6 +611,7 @@
         pltpu.VMEM((96, LANES), F32),
         pltpu.VMEM((24 * TOGETHER, LANES), F32),
         pltpu.VMEM((192, LANES), F32),
+        pltpu.VMEM((64 * TOGETHER, LANES), F32),
     ]
     inputs = (
         stiffness,
@@ -660,12 +660,12 @@
             pltpu.VMEM((8, 24, 24), F32),
             pltpu.SMEM((3,), F32),
             pltpu.VMEM((8, 4096), ints),
+            pltpu.SMEM((ROWS,), ints),
             *work,
             pltpu.VMEM((LANES, LANES), F32),
             pltpu.VMEM((LANES, 2 * LANES), F32),
-            pltpu.SemaphoreType.DMA((13,)),
+            pltpu.SemaphoreType.DMA((14,)),
         ],
-        last=[SMEM],
     )(*in_hbm(*inputs))
     got = swap(send)
     trio = ((3, PARTS_SIZE), F32)
@@ -674,9 +674,9 @@
         u, v, internal, *mine = call(
             functools.partial(next_kernel, n == 0),
             [state, state, state, *own],
-            [VMEM] * 7 + [SMEM] + [VMEM] * (2 + len(recv)),
+            [VMEM] * (10 + len(recv)),
             "next_cycle",
-            work,
+            [*work, pltpu.SMEM((ROWS,), ints), pltpu.SemaphoreType.DMA],
         )(u, v, internal, inv, fm, mass, idx, mat, cols, shared, *recv)
         recv = [partner(mine[b], b) for b in range(NBR)]
         if n == 0:
@@ -738,6 +738,7 @@
             pltpu.VMEM((96, LANES), F32),
             pltpu.VMEM((64, LANES), F32),
             pltpu.VMEM((64, LANES), F32),
+            pltpu.VMEM((384, LANES), F32),
         ],
     )(dots, swap(dots), slave, slot, nrm, midx, mnrm, x, net, part)
     (nodal_velocity,) = call(nodal_kernel, [((3, 4096), F32)], [VMEM] * 3, "nodal_velocity")(v, contact, mass)

time: 104 us -> 102 us (0.981)
  Pallas kernels: 31.4 us -> 30 us
where the time goes in v7:
time: 102 us
  blocking collectives  54.2 us (53%)
  Pallas kernels  30 us (29%)
  starting transfers between devices  14.3 us (14%)
  waiting for transfers between devices  2.87 us (3%)
    all_to_all x3, blocking collectives, swap(): lax.all_to_all(flat, 'dom', 0, 0, tiled=True, axis_index_groups=groups)  54.2 us
    ppermute x12, starting transfers between devices, partner(): lax.ppermute(block, 'dom', [(i, i ^ 1 << apart) for i in range(count)])  14.3 us
    pallas_call x2, Pallas kernels, per_device(): call(functools.partial(next_kernel, n == 0), [state, state, state, *own],...  12.6 us
    pallas_call x1, Pallas kernels, per_device(): call(first_kernel, [state, state, state, rows, ((8, 4096), ints), map_row...  8.39 us
    ppermute x12, waiting for transfers between devices, partner(): lax.ppermute(block, 'dom', [(i, i ^ 1 << apart) for i in range(count)])  2.87 us
    pallas_call x1, Pallas kernels, per_device(): call(contact_kernel, [state, half, half], [VMEM] * 10, 'contact_forces',...  2.7 us
    pallas_call x1, Pallas kernels, per_device(): call(base_kernel, [state, state, both], [VMEM] * 10, 'contact_base', [plt...  2.42 us
  transfers between devices with their start and end apart: 12, of which 4 were waited for; matrix products, arithmetic and copies ran while one was open for 0% of the time, Pallas kernels for 4%

profile of v7, /device:TPU:1, one launch (start us, length us, event | category | flops | bytes accessed | tf_op | source)
XLA Modules:
  0.0 102.1 jit_solution(14938040086051420454)
XLA Ops:
  0.6 8.4 %first_cycle.1 = (f32[96,128]{1,0:T(8,128)S(1)}, f32[96,128]{1,0:T(8,128)S(1)}, f32[96,128]{1,0:T(8,128)S(1)}, f32[32,128]{1,0:T(8,128)S(1)}, s32[8,4096]{1,0:T(...) custom-call(f32[8,24,24]{2,1,0:T(8,128)} %refs_0_.2, ...), custom_call_target="tpu_custom_call" | custom-call | bytes 1048576 | tf_op jit(solution)/shard_map/first_cycle/pallas_call | solution.py:633
  9.0 22.9 %all_to_all.15 = f32[128,1,640]{2,1,0:T(1,128)S(1)} all-to-all(f32[128,1,640]{2,1,0:T(1,128)S(1)} %bitcast.19), channel_id=1, replica_groups=mesh['dom'=128] {'dom'}, dimensions={0} | all-to-all | bytes 655360 | tf_op jit(solution)/shard_map/all_to_all | solution.py:584
  32.0 6.3 %next_cycle.2 = (f32[96,128]{1,0:T(8,128)S(1)}, f32[96,128]{1,0:T(8,128)S(1)}, f32[96,128]{1,0:T(8,128)S(1)}, f32[3,128]{1,0:T(4,128)S(1)}, f32[3,128]{1,0:T(4,1...) custom-call(f32[96,128]{1,0:T(8,128)S(1)} %get-tuple-element.59.u, ...), custom_call_target="tpu_custom_call" | custom-call | bytes 1048576 | tf_op jit(solution)/shard_map/next_cycle/pallas_call | solution.py:674
  38.3 1.0 collective-permute-start
  39.3 0.3 collective-permute-start.1
  39.6 1.6 %collective-permute-start.2 = (f32[3,128]{1,0:T(4,128)S(1)}, f32[3,128]{1,0:T(4,128)S(1)}, u32[]{:S(2)}, u32[]{:S(2)}) collective-permute-start(f32[3,128]{1,0:T(4,128)S(1)} %get-tuple-element.75), channel_id=1, source_target_pairs={{0,4},{1,5},{2,6},{3,7},{4,0},{5,1},{6,2},{7,3},{8,12},{9,13},{10,... | collective-permute-start | bytes 4616 | tf_op jit(solution)/shard_map/ppermute | solution.py:570
  41.2 0.5 collective-permute-start.3
  41.7 1.1 %collective-permute-start.4 = (f32[3,128]{1,0:T(4,128)S(1)}, f32[3,128]{1,0:T(4,128)S(1)}, u32[]{:S(2)}, u32[]{:S(2)}) collective-permute-start(f32[3,128]{1,0:T(4,128)S(1)} %get-tuple-element.77), channel_id=1, source_target_pairs={{0,16},{1,17},{2,18},{3,19},{4,20},{5,21},{6,22},{7,23},{8,24},{9,... | collective-permute-start | bytes 4616 | tf_op jit(solution)/shard_map/ppermute | solution.py:570
  42.8 0.5 contact_ends.1
  43.2 0.9 fixed_data.1
  44.2 0.0 collective-permute-done.rest_0_
  44.2 0.0 collective-permute-done.1.rest_1_
  44.2 0.0 collective-permute-done.2.rest_2_
  44.2 0.0 collective-permute-done.3.rest_3_
  44.2 1.4 %collective-permute-done.4.rest_4_ = f32[3,128]{1,0:T(4,128)S(1)} collective-permute-done((f32[3,128]{1,0:T(4,128)S(1)}, f32[3,128]{1,0:T(4,128)S(1)}, u32[]{:S(2)}, u32[]{:S(2)}) %collective-permute-start.4) | collective-permute-done | bytes 1568 | tf_op jit(solution)/shard_map/ppermute | solution.py:570
  45.7 6.2 %next_cycle.3 = (f32[96,128]{1,0:T(8,128)S(1)}, f32[96,128]{1,0:T(8,128)S(1)}, f32[96,128]{1,0:T(8,128)S(1)}, f32[3,128]{1,0:T(4,128)S(1)}, f32[3,128]{1,0:T(4,1...) custom-call(f32[96,128]{1,0:T(8,128)S(1)} %get-tuple-element.70.u, ...), custom_call_target="tpu_custom_call" | custom-call | bytes 1048576 | tf_op jit(solution)/shard_map/next_cycle/pallas_call | solution.py:674
  51.9 2.2 %collective-permute-start.5 = (f32[3,128]{1,0:T(4,128)S(1)}, f32[3,128]{1,0:T(4,128)S(1)}, u32[]{:S(2)}, u32[]{:S(2)}) collective-permute-start(f32[3,128]{1,0:T(4,128)S(1)} %get-tuple-element.103), channel_id=1, source_target_pairs={{0,1},{1,0},{2,3},{3,2},{4,5},{5,4},{6,7},{7,6},{8,9},{9,8},{10,11... | collective-permute-start | bytes 4616 | tf_op jit(solution)/shard_map/ppermute | solution.py:570
  54.1 0.0 collective-permute-start.6
  54.1 2.8 %collective-permute-start.7 = (f32[3,128]{1,0:T(4,128)S(1)}, f32[3,128]{1,0:T(4,128)S(1)}, u32[]{:S(2)}, u32[]{:S(2)}) collective-permute-start(f32[3,128]{1,0:T(4,128)S(1)} %get-tuple-element.105), channel_id=1, source_target_pairs={{0,4},{1,5},{2,6},{3,7},{4,0},{5,1},{6,2},{7,3},{8,12},{9,13},{10,... | collective-permute-start | bytes 4616 | tf_op jit(solution)/shard_map/ppermute | solution.py:570
  56.9 1.2 %collective-permute-start.8 = (f32[3,128]{1,0:T(4,128)S(1)}, f32[3,128]{1,0:T(4,128)S(1)}, u32[]{:S(2)}, u32[]{:S(2)}) collective-permute-start(f32[3,128]{1,0:T(4,128)S(1)} %get-tuple-element.106), channel_id=1, source_target_pairs={{0,8},{1,9},{2,10},{3,11},{4,12},{5,13},{6,14},{7,15},{8,0},{9,1},... | collective-permute-start | bytes 4616 | tf_op jit(solution)/shard_map/ppermute | solution.py:570
  58.1 1.1 %collective-permute-start.9 = (f32[3,128]{1,0:T(4,128)S(1)}, f32[3,128]{1,0:T(4,128)S(1)}, u32[]{:S(2)}, u32[]{:S(2)}) collective-permute-start(f32[3,128]{1,0:T(4,128)S(1)} %get-tuple-element.107), channel_id=1, source_target_pairs={{0,16},{1,17},{2,18},{3,19},{4,20},{5,21},{6,22},{7,23},{8,24},{9,... | collective-permute-start | bytes 4616 | tf_op jit(solution)/shard_map/ppermute | solution.py:570
  59.2 2.4 %contact_base.1 = (f32[96,128]{1,0:T(8,128)S(1)}, f32[96,128]{1,0:T(8,128)S(1)}, f32[2,80,128]{2,1,0:T(8,128)S(1)}) custom-call(f32[96,128]{1,0:T(8,128)S(1)} %get-tuple-element.89.u, f32[96,128]{1,0:T(8,128)S(1)} %get-tuple-element.90.v, f32[96,128]{1,0:T(8,128)S(1)} %get-tuple-element.91.internal, f32[96,128]{1,0:T(8,128)S(1)} %get-tuple-element.63.fm, ...), custom_call_target="tpu_custom_call" | custom-call | bytes 1048576 | tf_op jit(solution)/shard_map/contact_base/pallas_call | solution.py:715
  61.6 0.0 collective-permute-done.5.rest_0_
  61.7 0.0 collective-permute-done.6.rest_1_
  61.7 0.0 collective-permute-done.7.rest_2_
  61.7 0.0 collective-permute-done.8.rest_3_
  61.7 0.4 collective-permute-done.9.rest_4_
  62.1 1.0 %contact_dots.1 = (f32[96,128]{1,0:T(8,128)S(1)}, f32[96,128]{1,0:T(8,128)S(1)}, f32[96,128]{1,0:T(8,128)S(1)}, f32[384,128]{1,0:T(8,128)S(1)}) custom-call(f32[96,128]{1,0:T(8,128)S(1)} %get-tuple-element.96.x1, f32[96,128]{1,0:T(8,128)S(1)} %get-tuple-element.97.v1, f32[2,80,128]{2,1,0:T(8,128)S(1)} %get-tuple-element.98.ab1, ...), custom_call_target="tpu_custom_call" | custom-call | bytes 1048576 | tf_op jit(solution)/shard_map/contact_dots/pallas_call | solution.py:722
  63.1 16.0 %all_to_all.16 = f32[128,1,384]{2,1,0:T(1,128)S(1)} all-to-all(f32[128,1,384]{2,1,0:T(1,128)S(1)} %bitcast.17), channel_id=1, replica_groups=mesh['dom'=128] {'dom'}, dimensions={0} | all-to-all | bytes 393216 | tf_op jit(solution)/shard_map/all_to_all | solution.py:584
  79.1 2.7 %contact_forces.1 = (f32[96,128]{1,0:T(8,128)S(1)}, f32[16,128]{1,0:T(8,128)S(1)}, f32[16,128]{1,0:T(8,128)S(1)}) custom-call(f32[384,128]{1,0:T(8,128)S(1)} %get-tuple-element.109.dots, f32[384,128]{1,0:T(8,128)S(1)} %bitcast.18, s32[16,128]{1,0:T(8,128)S(1)} %get-tuple-element.79.slave, s32[16,128]{1,0:T(8,128)S(1)} %get-tuple-element.101.slot, ...), custom_call_target="tpu_custom_call" | custom-call | bytes 1048576 | tf_op jit(solution)/shard_map/contact_forces/pallas_call | solution.py:730
  81.8 0.7 collective-permute-start.10
  82.5 0.8 collective-permute-done.10.given
  83.4 15.2 %all_to_all.17 = f32[64,1,1280]{2,1,0:T(1,128)S(1)} all-to-all(f32[64,1,1280]{2,1,0:T(1,128)S(1)} %bitcast.15), channel_id=1, replica_groups={{0,2,4,6,8,10,12,14,16,18,20,22,24,26,28,30,32,34,36,38,40,42,44,46,48,..., dimensions={0} | all-to-all | bytes 655360 | tf_op jit(solution)/shard_map/all_to_all | solution.py:584
  98.6 0.1 part_totals.1.mine
  98.7 1.8 %collective-permute-start.11 = (f32[80,128]{1,0:T(8,128)S(1)}, f32[80,128]{1,0:T(8,128)S(1)}, u32[]{:S(2)}, u32[]{:S(2)}) collective-permute-start(f32[80,128]{1,0:T(8,128)S(1)} %part_totals.1.mine), channel_id=1, source_target_pairs={{0,1},{1,0},{2,3},{3,2},{4,5},{5,4},{6,7},{7,6},{8,9},{9,8},{10,11... | collective-permute-start | bytes 122888 | tf_op jit(solution)/shard_map/ppermute | solution.py:570
  100.5 0.7 nodal_velocity.1
  101.2 0.2 collective-permute-done.11.other
  101.4 0.7 part_motion.1
  (1 shorter events, 0.0 us)
Async XLA Ops:
  38.3 5.9 %collective-permute-start = (f32[3,128]{1,0:T(4,128)S(1)}, f32[3,128]{1,0:T(4,128)S(1)}, u32[]{:S(2)}, u32[]{:S(2)}) collective-permute-start(f32[3,128]{1,0:T(4,128)S(1)} %get-tuple-element.73), channel_id=1, source_target_pairs={{0,1},{1,0},{2,3},{3,2},{4,5},{5,4},{6,7},{7,6},{8,9},{9,8},{10,11... | collective-permute-start | bytes 4616 | tf_op jit(solution)/shard_map/ppermute | solution.py:570
  39.3 5.0 %collective-permute-start.1 = (f32[3,128]{1,0:T(4,128)S(1)}, f32[3,128]{1,0:T(4,128)S(1)}, u32[]{:S(2)}, u32[]{:S(2)}) collective-permute-start(f32[3,128]{1,0:T(4,128)S(1)} %get-tuple-element.74), channel_id=1, source_target_pairs={{0,2},{1,3},{2,0},{3,1},{4,6},{5,7},{6,4},{7,5},{8,10},{9,11},{10,... | collective-permute-start | bytes 4616 | tf_op jit(solution)/shard_map/ppermute | solution.py:570
  39.6 4.7 %collective-permute-start.2 = (f32[3,128]{1,0:T(4,128)S(1)}, f32[3,128]{1,0:T(4,128)S(1)}, u32[]{:S(2)}, u32[]{:S(2)}) collective-permute-start(f32[3,128]{1,0:T(4,128)S(1)} %get-tuple-element.75), channel_id=1, source_target_pairs={{0,4},{1,5},{2,6},{3,7},{4,0},{5,1},{6,2},{7,3},{8,12},{9,13},{10,... | collective-permute-start | bytes 4616 | tf_op jit(solution)/shard_map/ppermute | solution.py:570
  41.2 3.0 %collective-permute-start.3 = (f32[3,128]{1,0:T(4,128)S(1)}, f32[3,128]{1,0:T(4,128)S(1)}, u32[]{:S(2)}, u32[]{:S(2)}) collective-permute-start(f32[3,128]{1,0:T(4,128)S(1)} %get-tuple-element.76), channel_id=1, source_target_pairs={{0,8},{1,9},{2,10},{3,11},{4,12},{5,13},{6,14},{7,15},{8,0},{9,1},... | collective-permute-start | bytes 4616 | tf_op jit(solution)/shard_map/ppermute | solution.py:570
  41.7 3.9 %collective-permute-start.4 = (f32[3,128]{1,0:T(4,128)S(1)}, f32[3,128]{1,0:T(4,128)S(1)}, u32[]{:S(2)}, u32[]{:S(2)}) collective-permute-start(f32[3,128]{1,0:T(4,128)S(1)} %get-tuple-element.77), channel_id=1, source_target_pairs={{0,16},{1,17},{2,18},{3,19},{4,20},{5,21},{6,22},{7,23},{8,24},{9,... | collective-permute-start | bytes 4616 | tf_op jit(solution)/shard_map/ppermute | solution.py:570
  51.9 9.7 %collective-permute-start.5 = (f32[3,128]{1,0:T(4,128)S(1)}, f32[3,128]{1,0:T(4,128)S(1)}, u32[]{:S(2)}, u32[]{:S(2)}) collective-permute-start(f32[3,128]{1,0:T(4,128)S(1)} %get-tuple-element.103), channel_id=1, source_target_pairs={{0,1},{1,0},{2,3},{3,2},{4,5},{5,4},{6,7},{7,6},{8,9},{9,8},{10,11... | collective-permute-start | bytes 4616 | tf_op jit(solution)/shard_map/ppermute | solution.py:570
  54.1 7.5 %collective-permute-start.6 = (f32[3,128]{1,0:T(4,128)S(1)}, f32[3,128]{1,0:T(4,128)S(1)}, u32[]{:S(2)}, u32[]{:S(2)}) collective-permute-start(f32[3,128]{1,0:T(4,128)S(1)} %get-tuple-element.104), channel_id=1, source_target_pairs={{0,2},{1,3},{2,0},{3,1},{4,6},{5,7},{6,4},{7,5},{8,10},{9,11},{10,... | collective-permute-start | bytes 4616 | tf_op jit(solution)/shard_map/ppermute | solution.py:570
  54.1 7.5 %collective-permute-start.7 = (f32[3,128]{1,0:T(4,128)S(1)}, f32[3,128]{1,0:T(4,128)S(1)}, u32[]{:S(2)}, u32[]{:S(2)}) collective-permute-start(f32[3,128]{1,0:T(4,128)S(1)} %get-tuple-element.105), channel_id=1, source_target_pairs={{0,4},{1,5},{2,6},{3,7},{4,0},{5,1},{6,2},{7,3},{8,12},{9,13},{10,... | collective-permute-start | bytes 4616 | tf_op jit(solution)/shard_map/ppermute | solution.py:570
  56.9 4.7 %collective-permute-start.8 = (f32[3,128]{1,0:T(4,128)S(1)}, f32[3,128]{1,0:T(4,128)S(1)}, u32[]{:S(2)}, u32[]{:S(2)}) collective-permute-start(f32[3,128]{1,0:T(4,128)S(1)} %get-tuple-element.106), channel_id=1, source_target_pairs={{0,8},{1,9},{2,10},{3,11},{4,12},{5,13},{6,14},{7,15},{8,0},{9,1},... | collective-permute-start | bytes 4616 | tf_op jit(solution)/shard_map/ppermute | solution.py:570
  58.1 3.9 %collective-permute-start.9 = (f32[3,128]{1,0:T(4,128)S(1)}, f32[3,128]{1,0:T(4,128)S(1)}, u32[]{:S(2)}, u32[]{:S(2)}) collective-permute-start(f32[3,128]{1,0:T(4,128)S(1)} %get-tuple-element.107), channel_id=1, source_target_pairs={{0,16},{1,17},{2,18},{3,19},{4,20},{5,21},{6,22},{7,23},{8,24},{9,... | collective-permute-start | bytes 4616 | tf_op jit(solution)/shard_map/ppermute | solution.py:570
  81.8 1.6 %collective-permute-start.10 = (f32[16,128]{1,0:T(8,128)S(1)}, f32[16,128]{1,0:T(8,128)S(1)}, u32[]{:S(2)}, u32[]{:S(2)}) collective-permute-start(f32[16,128]{1,0:T(8,128)S(1)} %get-tuple-element.114), channel_id=1, source_target_pairs={{0,1},{1,0},{2,3},{3,2},{4,5},{5,4},{6,7},{7,6},{8,9},{9,8},{10,11... | collective-permute-start | bytes 24584 | tf_op jit(solution)/shard_map/ppermute | solution.py:570
  98.7 2.6 %collective-permute-start.11 = (f32[80,128]{1,0:T(8,128)S(1)}, f32[80,128]{1,0:T(8,128)S(1)}, u32[]{:S(2)}, u32[]{:S(2)}) collective-permute-start(f32[80,128]{1,0:T(8,128)S(1)} %part_totals.1.mine), channel_id=1, source_target_pairs={{0,1},{1,0},{2,3},{3,2},{4,5},{5,4},{6,7},{7,6},{8,9},{9,8},{10,11... | collective-permute-start | bytes 122888 | tf_op jit(solution)/shard_map/ppermute | solution.py:570

commit v8 on v7

--- a/solution.py
+++ b/solution.py
@@ -23,6 +23,7 @@
 ROWS = 32
 NBR = 5
 TOGETHER = 8
+AHEAD = 2
 
 VMEM = pl.BlockSpec(memory_space=pltpu.VMEM)
 SMEM = pl.BlockSpec(memory_space=pltpu.SMEM)
@@ -101,39 +102,38 @@
 
 def elements(idx, mat, tab, cols, g, acc, held):
     acc[...] = jnp.zeros_like(acc)
-    steps = ROWS // TOGETHER
-
-    def corners(i, q):
-        here = idx[:, pl.ds(pl.multiple_of((i * TOGETHER + q) * LANES, LANES), LANES)]
+
+    def corners(b):
+        here = idx[:, pl.ds(pl.multiple_of(b * LANES, LANES), LANES)]
         return here & 127, here >> 7
 
-    def fetch(i):
-        vals = []
-        for q in range(TOGETHER):
-            vals += gather(tab, (0, ROWS, 2 * ROWS), *corners(i, q))
-        return tuple(vals)
+    def fetch(b):
+        return gather(tab, (0, ROWS, 2 * ROWS), *corners(b & (ROWS - 1)))
 
     def step(i, vals):
-        upcoming = fetch((i + 1) & (steps - 1))
+        vals = list(vals)
         left, right = [], []
         for q in range(TOGETHER):
+            b = i * TOGETHER + q
+            vals += fetch(b + AHEAD)
             for c in range(3):
-                g[q * 24 + 8 * c : q * 24 + 8 * c + 8, :] = vals[q * 3 + c]
-            first = mat[i * TOGETHER + q] * 24
+                g[q * 24 + 8 * c : q * 24 + 8 * c + 8, :] = vals[c]
+            vals = vals[3:]
+            first = mat[b] * 24
             force = [jnp.zeros((8, LANES), F32)] * 3
             for j in range(24):
                 col = cols.at[first + j]
                 row = jnp.broadcast_to(g[q * 24 + j : q * 24 + j + 1, :], (8, LANES))
                 force = [force[c] + col[8 * c : 8 * c + 8, :] * row for c in range(3)]
-            one, two = place(*corners(i, q), force, held, 64 * q)
+            one, two = place(*corners(b), force, held, 64 * q)
             left.append(one)
             right.append(two)
         acc[...] += lax.dot_general(
             jnp.concatenate(left, 1), jnp.concatenate(right, 1), NT, preferred_element_type=F32
         )
-        return upcoming
-
-    lax.fori_loop(0, steps, step, fetch(0))
+        return tuple(vals)
+
+    lax.fori_loop(0, ROWS // TOGETHER, step, tuple(x for b in range(AHEAD) for x in fetch(b)))
 
 
 def finish_internal(acc, internal, shared):

time: 102 us -> 101 us (level)
  Pallas kernels: 30 us -> 28.2 us
    pallas_call x2, Pallas kernels: 12.6 us -> 11.3 us  [per_device(): call(functools.partial(next_kernel, n == 0), [state, state, state, *own],...]
where the time goes in v8:
time: 101 us; the launch traced here: 100 us
  blocking collectives  54.2 us (54%)
  Pallas kernels  28.2 us (28%)
  starting transfers between devices  14.2 us (14%)
  waiting for transfers between devices  2.9 us (3%)
    all_to_all x3, blocking collectives, swap(): lax.all_to_all(flat, 'dom', 0, 0, tiled=True, axis_index_groups=groups)  54.2 us
    ppermute x12, starting transfers between devices, partner(): lax.ppermute(block, 'dom', [(i, i ^ 1 << apart) for i in range(count)])  14.2 us
    pallas_call x2, Pallas kernels, per_device(): call(functools.partial(next_kernel, n == 0), [state, state, state, *own],...  11.3 us
    pallas_call x1, Pallas kernels, per_device(): call(first_kernel, [state, state, state, rows, ((8, 4096), ints), map_row...  7.85 us
    ppermute x12, waiting for transfers between devices, partner(): lax.ppermute(block, 'dom', [(i, i ^ 1 << apart) for i in range(count)])  2.9 us
    pallas_call x1, Pallas kernels, per_device(): call(contact_kernel, [state, half, half], [VMEM] * 10, 'contact_forces',...  2.71 us
    pallas_call x1, Pallas kernels, per_device(): call(base_kernel, [state, state, both], [VMEM] * 10, 'contact_base', [plt...  2.42 us
  transfers between devices with their start and end apart: 12, of which 4 were waited for; matrix products, arithmetic and copies ran while one was open for 0% of the time, Pallas kernels for 4%

profile of v8, /device:TPU:1, one launch (start us, length us, event | category | flops | bytes accessed | tf_op | source)
XLA Modules:
  0.0 100.3 jit_solution(8669880322006171493)
XLA Ops:
  0.6 7.8 %first_cycle.1 = (f32[96,128]{1,0:T(8,128)S(1)}, f32[96,128]{1,0:T(8,128)S(1)}, f32[96,128]{1,0:T(8,128)S(1)}, f32[32,128]{1,0:T(8,128)S(1)}, s32[8,4096]{1,0:T(...) custom-call(f32[8,24,24]{2,1,0:T(8,128)} %refs_0_.2, ...), custom_call_target="tpu_custom_call" | custom-call | bytes 1048576 | tf_op jit(solution)/shard_map/first_cycle/pallas_call | solution.py:633
  8.5 22.9 %all_to_all.15 = f32[128,1,640]{2,1,0:T(1,128)S(1)} all-to-all(f32[128,1,640]{2,1,0:T(1,128)S(1)} %bitcast.19), channel_id=1, replica_groups=mesh['dom'=128] {'dom'}, dimensions={0} | all-to-all | bytes 655360 | tf_op jit(solution)/shard_map/all_to_all | solution.py:584
  31.4 5.7 %next_cycle.2 = (f32[96,128]{1,0:T(8,128)S(1)}, f32[96,128]{1,0:T(8,128)S(1)}, f32[96,128]{1,0:T(8,128)S(1)}, f32[3,128]{1,0:T(4,128)S(1)}, f32[3,128]{1,0:T(4,1...) custom-call(f32[96,128]{1,0:T(8,128)S(1)} %get-tuple-element.59.u, ...), custom_call_target="tpu_custom_call" | custom-call | bytes 1048576 | tf_op jit(solution)/shard_map/next_cycle/pallas_call | solution.py:674
  37.1 1.0 collective-permute-start
  38.1 0.3 collective-permute-start.1
  38.4 1.6 %collective-permute-start.2 = (f32[3,128]{1,0:T(4,128)S(1)}, f32[3,128]{1,0:T(4,128)S(1)}, u32[]{:S(2)}, u32[]{:S(2)}) collective-permute-start(f32[3,128]{1,0:T(4,128)S(1)} %get-tuple-element.75), channel_id=1, source_target_pairs={{0,4},{1,5},{2,6},{3,7},{4,0},{5,1},{6,2},{7,3},{8,12},{9,13},{10,... | collective-permute-start | bytes 4616 | tf_op jit(solution)/shard_map/ppermute | solution.py:570
  40.0 0.6 collective-permute-start.3
  40.6 1.0 %collective-permute-start.4 = (f32[3,128]{1,0:T(4,128)S(1)}, f32[3,128]{1,0:T(4,128)S(1)}, u32[]{:S(2)}, u32[]{:S(2)}) collective-permute-start(f32[3,128]{1,0:T(4,128)S(1)} %get-tuple-element.77), channel_id=1, source_target_pairs={{0,16},{1,17},{2,18},{3,19},{4,20},{5,21},{6,22},{7,23},{8,24},{9,... | collective-permute-start | bytes 4616 | tf_op jit(solution)/shard_map/ppermute | solution.py:570
  41.6 0.5 contact_ends.1
  42.1 0.9 fixed_data.1
  43.0 0.0 collective-permute-done.rest_0_
  43.0 0.0 collective-permute-done.1.rest_1_
  43.1 0.0 collective-permute-done.2.rest_2_
  43.1 0.0 collective-permute-done.3.rest_3_
  43.1 1.5 %collective-permute-done.4.rest_4_ = f32[3,128]{1,0:T(4,128)S(1)} collective-permute-done((f32[3,128]{1,0:T(4,128)S(1)}, f32[3,128]{1,0:T(4,128)S(1)}, u32[]{:S(2)}, u32[]{:S(2)}) %collective-permute-start.4) | collective-permute-done | bytes 1568 | tf_op jit(solution)/shard_map/ppermute | solution.py:570
  44.5 5.6 %next_cycle.3 = (f32[96,128]{1,0:T(8,128)S(1)}, f32[96,128]{1,0:T(8,128)S(1)}, f32[96,128]{1,0:T(8,128)S(1)}, f32[3,128]{1,0:T(4,128)S(1)}, f32[3,128]{1,0:T(4,1...) custom-call(f32[96,128]{1,0:T(8,128)S(1)} %get-tuple-element.70.u, ...), custom_call_target="tpu_custom_call" | custom-call | bytes 1048576 | tf_op jit(solution)/shard_map/next_cycle/pallas_call | solution.py:674
  50.2 2.2 %collective-permute-start.5 = (f32[3,128]{1,0:T(4,128)S(1)}, f32[3,128]{1,0:T(4,128)S(1)}, u32[]{:S(2)}, u32[]{:S(2)}) collective-permute-start(f32[3,128]{1,0:T(4,128)S(1)} %get-tuple-element.103), channel_id=1, source_target_pairs={{0,1},{1,0},{2,3},{3,2},{4,5},{5,4},{6,7},{7,6},{8,9},{9,8},{10,11... | collective-permute-start | bytes 4616 | tf_op jit(solution)/shard_map/ppermute | solution.py:570
  52.3 0.0 collective-permute-start.6
  52.3 2.8 %collective-permute-start.7 = (f32[3,128]{1,0:T(4,128)S(1)}, f32[3,128]{1,0:T(4,128)S(1)}, u32[]{:S(2)}, u32[]{:S(2)}) collective-permute-start(f32[3,128]{1,0:T(4,128)S(1)} %get-tuple-element.105), channel_id=1, source_target_pairs={{0,4},{1,5},{2,6},{3,7},{4,0},{5,1},{6,2},{7,3},{8,12},{9,13},{10,... | collective-permute-start | bytes 4616 | tf_op jit(solution)/shard_map/ppermute | solution.py:570
  55.1 1.2 %collective-permute-start.8 = (f32[3,128]{1,0:T(4,128)S(1)}, f32[3,128]{1,0:T(4,128)S(1)}, u32[]{:S(2)}, u32[]{:S(2)}) collective-permute-start(f32[3,128]{1,0:T(4,128)S(1)} %get-tuple-element.106), channel_id=1, source_target_pairs={{0,8},{1,9},{2,10},{3,11},{4,12},{5,13},{6,14},{7,15},{8,0},{9,1},... | collective-permute-start | bytes 4616 | tf_op jit(solution)/shard_map/ppermute | solution.py:570
  56.4 1.1 %collective-permute-start.9 = (f32[3,128]{1,0:T(4,128)S(1)}, f32[3,128]{1,0:T(4,128)S(1)}, u32[]{:S(2)}, u32[]{:S(2)}) collective-permute-start(f32[3,128]{1,0:T(4,128)S(1)} %get-tuple-element.107), channel_id=1, source_target_pairs={{0,16},{1,17},{2,18},{3,19},{4,20},{5,21},{6,22},{7,23},{8,24},{9,... | collective-permute-start | bytes 4616 | tf_op jit(solution)/shard_map/ppermute | solution.py:570
  57.4 2.4 %contact_base.1 = (f32[96,128]{1,0:T(8,128)S(1)}, f32[96,128]{1,0:T(8,128)S(1)}, f32[2,80,128]{2,1,0:T(8,128)S(1)}) custom-call(f32[96,128]{1,0:T(8,128)S(1)} %get-tuple-element.89.u, f32[96,128]{1,0:T(8,128)S(1)} %get-tuple-element.90.v, f32[96,128]{1,0:T(8,128)S(1)} %get-tuple-element.91.internal, f32[96,128]{1,0:T(8,128)S(1)} %get-tuple-element.63.fm, ...), custom_call_target="tpu_custom_call" | custom-call | bytes 1048576 | tf_op jit(solution)/shard_map/contact_base/pallas_call | solution.py:715
  59.9 0.0 collective-permute-done.5.rest_0_
  59.9 0.0 collective-permute-done.6.rest_1_
  59.9 0.0 collective-permute-done.7.rest_2_
  59.9 0.0 collective-permute-done.8.rest_3_
  59.9 0.4 collective-permute-done.9.rest_4_
  60.3 1.0 %contact_dots.1 = (f32[96,128]{1,0:T(8,128)S(1)}, f32[96,128]{1,0:T(8,128)S(1)}, f32[96,128]{1,0:T(8,128)S(1)}, f32[384,128]{1,0:T(8,128)S(1)}) custom-call(f32[96,128]{1,0:T(8,128)S(1)} %get-tuple-element.96.x1, f32[96,128]{1,0:T(8,128)S(1)} %get-tuple-element.97.v1, f32[2,80,128]{2,1,0:T(8,128)S(1)} %get-tuple-element.98.ab1, ...), custom_call_target="tpu_custom_call" | custom-call | bytes 1048576 | tf_op jit(solution)/shard_map/contact_dots/pallas_call | solution.py:722
  61.3 16.0 %all_to_all.16 = f32[128,1,384]{2,1,0:T(1,128)S(1)} all-to-all(f32[128,1,384]{2,1,0:T(1,128)S(1)} %bitcast.17), channel_id=1, replica_groups=mesh['dom'=128] {'dom'}, dimensions={0} | all-to-all | bytes 393216 | tf_op jit(solution)/shard_map/all_to_all | solution.py:584
  77.3 2.7 %contact_forces.1 = (f32[96,128]{1,0:T(8,128)S(1)}, f32[16,128]{1,0:T(8,128)S(1)}, f32[16,128]{1,0:T(8,128)S(1)}) custom-call(f32[384,128]{1,0:T(8,128)S(1)} %get-tuple-element.109.dots, f32[384,128]{1,0:T(8,128)S(1)} %bitcast.18, s32[16,128]{1,0:T(8,128)S(1)} %get-tuple-element.79.slave, s32[16,128]{1,0:T(8,128)S(1)} %get-tuple-element.101.slot, ...), custom_call_target="tpu_custom_call" | custom-call | bytes 1048576 | tf_op jit(solution)/shard_map/contact_forces/pallas_call | solution.py:730
  80.0 0.7 collective-permute-start.10
  80.8 0.8 collective-permute-done.10.given
  81.6 15.3 %all_to_all.17 = f32[64,1,1280]{2,1,0:T(1,128)S(1)} all-to-all(f32[64,1,1280]{2,1,0:T(1,128)S(1)} %bitcast.15), channel_id=1, replica_groups={{0,2,4,6,8,10,12,14,16,18,20,22,24,26,28,30,32,34,36,38,40,42,44,46,48,..., dimensions={0} | all-to-all | bytes 655360 | tf_op jit(solution)/shard_map/all_to_all | solution.py:584
  96.9 0.1 part_totals.1.mine
  97.0 1.8 %collective-permute-start.11 = (f32[80,128]{1,0:T(8,128)S(1)}, f32[80,128]{1,0:T(8,128)S(1)}, u32[]{:S(2)}, u32[]{:S(2)}) collective-permute-start(f32[80,128]{1,0:T(8,128)S(1)} %part_totals.1.mine), channel_id=1, source_target_pairs={{0,1},{1,0},{2,3},{3,2},{4,5},{5,4},{6,7},{7,6},{8,9},{9,8},{10,11... | collective-permute-start | bytes 122888 | tf_op jit(solution)/shard_map/ppermute | solution.py:570
  98.7 0.7 nodal_velocity.1
  99.4 0.2 collective-permute-done.11.other
  99.6 0.7 part_motion.1
  (1 shorter events, 0.0 us)
Async XLA Ops:
  37.1 5.9 %collective-permute-start = (f32[3,128]{1,0:T(4,128)S(1)}, f32[3,128]{1,0:T(4,128)S(1)}, u32[]{:S(2)}, u32[]{:S(2)}) collective-permute-start(f32[3,128]{1,0:T(4,128)S(1)} %get-tuple-element.73), channel_id=1, source_target_pairs={{0,1},{1,0},{2,3},{3,2},{4,5},{5,4},{6,7},{7,6},{8,9},{9,8},{10,11... | collective-permute-start | bytes 4616 | tf_op jit(solution)/shard_map/ppermute | solution.py:570
  38.1 5.0 %collective-permute-start.1 = (f32[3,128]{1,0:T(4,128)S(1)}, f32[3,128]{1,0:T(4,128)S(1)}, u32[]{:S(2)}, u32[]{:S(2)}) collective-permute-start(f32[3,128]{1,0:T(4,128)S(1)} %get-tuple-element.74), channel_id=1, source_target_pairs={{0,2},{1,3},{2,0},{3,1},{4,6},{5,7},{6,4},{7,5},{8,10},{9,11},{10,... | collective-permute-start | bytes 4616 | tf_op jit(solution)/shard_map/ppermute | solution.py:570
  38.4 4.7 %collective-permute-start.2 = (f32[3,128]{1,0:T(4,128)S(1)}, f32[3,128]{1,0:T(4,128)S(1)}, u32[]{:S(2)}, u32[]{:S(2)}) collective-permute-start(f32[3,128]{1,0:T(4,128)S(1)} %get-tuple-element.75), channel_id=1, source_target_pairs={{0,4},{1,5},{2,6},{3,7},{4,0},{5,1},{6,2},{7,3},{8,12},{9,13},{10,... | collective-permute-start | bytes 4616 | tf_op jit(solution)/shard_map/ppermute | solution.py:570
  40.0 3.1 %collective-permute-start.3 = (f32[3,128]{1,0:T(4,128)S(1)}, f32[3,128]{1,0:T(4,128)S(1)}, u32[]{:S(2)}, u32[]{:S(2)}) collective-permute-start(f32[3,128]{1,0:T(4,128)S(1)} %get-tuple-element.76), channel_id=1, source_target_pairs={{0,8},{1,9},{2,10},{3,11},{4,12},{5,13},{6,14},{7,15},{8,0},{9,1},... | collective-permute-start | bytes 4616 | tf_op jit(solution)/shard_map/ppermute | solution.py:570
  40.6 3.9 %collective-permute-start.4 = (f32[3,128]{1,0:T(4,128)S(1)}, f32[3,128]{1,0:T(4,128)S(1)}, u32[]{:S(2)}, u32[]{:S(2)}) collective-permute-start(f32[3,128]{1,0:T(4,128)S(1)} %get-tuple-element.77), channel_id=1, source_target_pairs={{0,16},{1,17},{2,18},{3,19},{4,20},{5,21},{6,22},{7,23},{8,24},{9,... | collective-permute-start | bytes 4616 | tf_op jit(solution)/shard_map/ppermute | solution.py:570
  50.2 9.7 %collective-permute-start.5 = (f32[3,128]{1,0:T(4,128)S(1)}, f32[3,128]{1,0:T(4,128)S(1)}, u32[]{:S(2)}, u32[]{:S(2)}) collective-permute-start(f32[3,128]{1,0:T(4,128)S(1)} %get-tuple-element.103), channel_id=1, source_target_pairs={{0,1},{1,0},{2,3},{3,2},{4,5},{5,4},{6,7},{7,6},{8,9},{9,8},{10,11... | collective-permute-start | bytes 4616 | tf_op jit(solution)/shard_map/ppermute | solution.py:570
  52.3 7.6 %collective-permute-start.6 = (f32[3,128]{1,0:T(4,128)S(1)}, f32[3,128]{1,0:T(4,128)S(1)}, u32[]{:S(2)}, u32[]{:S(2)}) collective-permute-start(f32[3,128]{1,0:T(4,128)S(1)} %get-tuple-element.104), channel_id=1, source_target_pairs={{0,2},{1,3},{2,0},{3,1},{4,6},{5,7},{6,4},{7,5},{8,10},{9,11},{10,... | collective-permute-start | bytes 4616 | tf_op jit(solution)/shard_map/ppermute | solution.py:570
  52.3 7.6 %collective-permute-start.7 = (f32[3,128]{1,0:T(4,128)S(1)}, f32[3,128]{1,0:T(4,128)S(1)}, u32[]{:S(2)}, u32[]{:S(2)}) collective-permute-start(f32[3,128]{1,0:T(4,128)S(1)} %get-tuple-element.105), channel_id=1, source_target_pairs={{0,4},{1,5},{2,6},{3,7},{4,0},{5,1},{6,2},{7,3},{8,12},{9,13},{10,... | collective-permute-start | bytes 4616 | tf_op jit(solution)/shard_map/ppermute | solution.py:570
  55.1 4.8 %collective-permute-start.8 = (f32[3,128]{1,0:T(4,128)S(1)}, f32[3,128]{1,0:T(4,128)S(1)}, u32[]{:S(2)}, u32[]{:S(2)}) collective-permute-start(f32[3,128]{1,0:T(4,128)S(1)} %get-tuple-element.106), channel_id=1, source_target_pairs={{0,8},{1,9},{2,10},{3,11},{4,12},{5,13},{6,14},{7,15},{8,0},{9,1},... | collective-permute-start | bytes 4616 | tf_op jit(solution)/shard_map/ppermute | solution.py:570
  56.4 3.9 %collective-permute-start.9 = (f32[3,128]{1,0:T(4,128)S(1)}, f32[3,128]{1,0:T(4,128)S(1)}, u32[]{:S(2)}, u32[]{:S(2)}) collective-permute-start(f32[3,128]{1,0:T(4,128)S(1)} %get-tuple-element.107), channel_id=1, source_target_pairs={{0,16},{1,17},{2,18},{3,19},{4,20},{5,21},{6,22},{7,23},{8,24},{9,... | collective-permute-start | bytes 4616 | tf_op jit(solution)/shard_map/ppermute | solution.py:570
  80.0 1.6 %collective-permute-start.10 = (f32[16,128]{1,0:T(8,128)S(1)}, f32[16,128]{1,0:T(8,128)S(1)}, u32[]{:S(2)}, u32[]{:S(2)}) collective-permute-start(f32[16,128]{1,0:T(8,128)S(1)} %get-tuple-element.114), channel_id=1, source_target_pairs={{0,1},{1,0},{2,3},{3,2},{4,5},{5,4},{6,7},{7,6},{8,9},{9,8},{10,11... | collective-permute-start | bytes 24584 | tf_op jit(solution)/shard_map/ppermute | solution.py:570
  97.0 2.6 %collective-permute-start.11 = (f32[80,128]{1,0:T(8,128)S(1)}, f32[80,128]{1,0:T(8,128)S(1)}, u32[]{:S(2)}, u32[]{:S(2)}) collective-permute-start(f32[80,128]{1,0:T(8,128)S(1)} %part_totals.1.mine), channel_id=1, source_target_pairs={{0,1},{1,0},{2,3},{3,2},{4,5},{5,4},{6,7},{7,6},{8,9},{9,8},{10,11... | collective-permute-start | bytes 122888 | tf_op jit(solution)/shard_map/ppermute | solution.py:570

commit v9 on v8

--- a/solution.py
+++ b/solution.py
@@ -22,7 +22,7 @@
 LANES = 128
 ROWS = 32
 NBR = 5
-TOGETHER = 8
+TOGETHER = 16
 AHEAD = 2
 
 VMEM = pl.BlockSpec(memory_space=pltpu.VMEM)
@@ -443,7 +443,6 @@
 def contact_kernel(
     dots, got, slave, slot, nrm, midx, mnrm, x, net, part, contact, keep, give, acc, tot, acc2, push, mine, held
 ):
-    acc[...] = jnp.zeros_like(acc)
     acc2[...] = jnp.zeros_like(acc2)
     left = lax.broadcasted_iota(jnp.int32, (LANES, LANES), 1) < 64
     as_slave = dots[every(0, 3), :] - got[every(1, 3), :]
@@ -457,30 +456,20 @@
     mine[...] = jnp.where(left[0:64, :], top, pltpu.roll(low, 64, 1))
     push[...] = -jnp.where(left[0:64, :], pltpu.roll(top, 64, 1), low)
 
-    def step(i, carry):
-        one, two = [], []
-        for q in range(4):
-            at = pl.ds(pl.multiple_of(i * 32 + q * 8, 8), 8)
-            here, size = midx[at, :], push[at, :]
-            pair = place(here & 127, here >> 7, [size * mnrm[c, at, :] for c in range(3)], held, 64 * q)
-            one.append(pair[0])
-            two.append(pair[1])
-        acc[...] += lax.dot_general(
-            jnp.concatenate(one, 1), jnp.concatenate(two, 1), NT, preferred_element_type=F32
-        )
-        return carry
-
-    lax.fori_loop(0, 2, step, 0)
-    one, two = [], []
+    blocks = []
+    for r in range(0, 64, 8):
+        here, at = midx[r : r + 8, :], push[r : r + 8, :]
+        blocks.append((here, [at * mnrm[c, r : r + 8, :] for c in range(3)]))
     for r in (0, 8):
-        here, at = slave[r : r + 8, :], slot[r : r + 8, :]
+        at = slot[r : r + 8, :]
         (size,) = gather(mine, (0,), ((at >> 12) << 6) + (at & 63), (at >> 6) & 63, 64)
-        w = [size * nrm[16 * c + r : 16 * c + r + 8, :] for c in range(3)]
-        pair = place(here & 127, here >> 7, w, held, 256 + 8 * r)
-        one.append(pair[0])
-        two.append(pair[1])
-    acc[...] += lax.dot_general(
-        jnp.concatenate(one, 1), jnp.concatenate(two, 1), NT, preferred_element_type=F32
+        blocks.append((slave[r : r + 8, :], [size * nrm[16 * c + r : 16 * c + r + 8, :] for c in range(3)]))
+    pairs = [place(here & 127, here >> 7, w, held, 64 * k) for k, (here, w) in enumerate(blocks)]
+    acc[...] = lax.dot_general(
+        jnp.concatenate([pair[0] for pair in pairs], 1),
+        jnp.concatenate([pair[1] for pair in pairs], 1),
+        NT,
+        preferred_element_type=F32,
     )
     contact[...] = acc[0:96, :] + acc[96:192, :]
     tot[...] = net[...] + contact[...]
@@ -738,7 +727,7 @@
             pltpu.VMEM((96, LANES), F32),
             pltpu.VMEM((64, LANES), F32),
             pltpu.VMEM((64, LANES), F32),
-            pltpu.VMEM((384, LANES), F32),
+            pltpu.VMEM((640, LANES), F32),
         ],
     )(dots, swap(dots), slave, slot, nrm, midx, mnrm, x, net, part)
     (nodal_velocity,) = call(nodal_kernel, [((3, 4096), F32)], [VMEM] * 3, "nodal_velocity")(v, contact, mass)

time: 101 us -> 99.3 us (0.983)
  Pallas kernels: 28.2 us -> 26.9 us
  transfers between devices with their start and end apart: 12 -> 12, of which waited for: 4 -> 4; matrix products, arithmetic and copies ran while one was open for 0% -> 0% of each run, Pallas kernels for 4% -> 5%
where the time goes in v9:
time: 99.3 us; the launch traced here: 99.1 us
  blocking collectives  54.3 us (55%)
  Pallas kernels  26.9 us (27%)
  starting transfers between devices  14.2 us (14%)
  waiting for transfers between devices  2.95 us (3%)
    all_to_all x3, blocking collectives, swap(): lax.all_to_all(flat, 'dom', 0, 0, tiled=True, axis_index_groups=groups)  54.3 us
    ppermute x12, starting transfers between devices, partner(): lax.ppermute(block, 'dom', [(i, i ^ 1 << apart) for i in range(count)])  14.2 us
    pallas_call x2, Pallas kernels, per_device(): call(functools.partial(next_kernel, n == 0), [state, state, state, *own],...  10.7 us
    pallas_call x1, Pallas kernels, per_device(): call(first_kernel, [state, state, state, rows, ((8, 4096), ints), map_row...  7.49 us
    ppermute x12, waiting for transfers between devices, partner(): lax.ppermute(block, 'dom', [(i, i ^ 1 << apart) for i in range(count)])  2.95 us
    pallas_call x1, Pallas kernels, per_device(): call(base_kernel, [state, state, both], [VMEM] * 10, 'contact_base', [plt...  2.42 us
    pallas_call x1, Pallas kernels, per_device(): call(contact_kernel, [state, half, half], [VMEM] * 10, 'contact_forces',...  2.3 us
  transfers between devices with their start and end apart: 12, of which 4 were waited for; matrix products, arithmetic and copies ran while one was open for 0% of the time, Pallas kernels for 5%

profile of v9, /device:TPU:1, one launch (start us, length us, event | category | flops | bytes accessed | tf_op | source)
XLA Modules:
  0.0 99.1 jit_solution(7454872742395802209)
XLA Ops:
  0.6 7.5 %first_cycle.1 = (f32[96,128]{1,0:T(8,128)S(1)}, f32[96,128]{1,0:T(8,128)S(1)}, f32[96,128]{1,0:T(8,128)S(1)}, f32[32,128]{1,0:T(8,128)S(1)}, s32[8,4096]{1,0:T(...) custom-call(f32[8,24,24]{2,1,0:T(8,128)} %refs_0_.2, ...), custom_call_target="tpu_custom_call" | custom-call | bytes 1048576 | tf_op jit(solution)/shard_map/first_cycle/pallas_call | solution.py:622
  8.1 22.9 %all_to_all.15 = f32[128,1,640]{2,1,0:T(1,128)S(1)} all-to-all(f32[128,1,640]{2,1,0:T(1,128)S(1)} %bitcast.19), channel_id=1, replica_groups=mesh['dom'=128] {'dom'}, dimensions={0} | all-to-all | bytes 655360 | tf_op jit(solution)/shard_map/all_to_all | solution.py:573
  31.1 5.4 %next_cycle.2 = (f32[96,128]{1,0:T(8,128)S(1)}, f32[96,128]{1,0:T(8,128)S(1)}, f32[96,128]{1,0:T(8,128)S(1)}, f32[3,128]{1,0:T(4,128)S(1)}, f32[3,128]{1,0:T(4,1...) custom-call(f32[96,128]{1,0:T(8,128)S(1)} %get-tuple-element.59.u, ...), custom_call_target="tpu_custom_call" | custom-call | bytes 1048576 | tf_op jit(solution)/shard_map/next_cycle/pallas_call | solution.py:663
  36.5 1.0 collective-permute-start
  37.4 0.3 collective-permute-start.1
  37.7 1.6 %collective-permute-start.2 = (f32[3,128]{1,0:T(4,128)S(1)}, f32[3,128]{1,0:T(4,128)S(1)}, u32[]{:S(2)}, u32[]{:S(2)}) collective-permute-start(f32[3,128]{1,0:T(4,128)S(1)} %get-tuple-element.75), channel_id=1, source_target_pairs={{0,4},{1,5},{2,6},{3,7},{4,0},{5,1},{6,2},{7,3},{8,12},{9,13},{10,... | collective-permute-start | bytes 4616 | tf_op jit(solution)/shard_map/ppermute | solution.py:559
  39.4 0.6 collective-permute-start.3
  39.9 1.0 %collective-permute-start.4 = (f32[3,128]{1,0:T(4,128)S(1)}, f32[3,128]{1,0:T(4,128)S(1)}, u32[]{:S(2)}, u32[]{:S(2)}) collective-permute-start(f32[3,128]{1,0:T(4,128)S(1)} %get-tuple-element.77), channel_id=1, source_target_pairs={{0,16},{1,17},{2,18},{3,19},{4,20},{5,21},{6,22},{7,23},{8,24},{9,... | collective-permute-start | bytes 4616 | tf_op jit(solution)/shard_map/ppermute | solution.py:559
  40.9 0.5 contact_ends.1
  41.4 0.9 fixed_data.1
  42.4 0.0 collective-permute-done.rest_0_
  42.4 0.0 collective-permute-done.1.rest_1_
  42.4 0.0 collective-permute-done.2.rest_2_
  42.4 0.0 collective-permute-done.3.rest_3_
  42.4 1.5 %collective-permute-done.4.rest_4_ = f32[3,128]{1,0:T(4,128)S(1)} collective-permute-done((f32[3,128]{1,0:T(4,128)S(1)}, f32[3,128]{1,0:T(4,128)S(1)}, u32[]{:S(2)}, u32[]{:S(2)}) %collective-permute-start.4) | collective-permute-done | bytes 1568 | tf_op jit(solution)/shard_map/ppermute | solution.py:559
  43.9 5.3 %next_cycle.3 = (f32[96,128]{1,0:T(8,128)S(1)}, f32[96,128]{1,0:T(8,128)S(1)}, f32[96,128]{1,0:T(8,128)S(1)}, f32[3,128]{1,0:T(4,128)S(1)}, f32[3,128]{1,0:T(4,1...) custom-call(f32[96,128]{1,0:T(8,128)S(1)} %get-tuple-element.70.u, ...), custom_call_target="tpu_custom_call" | custom-call | bytes 1048576 | tf_op jit(solution)/shard_map/next_cycle/pallas_call | solution.py:663
  49.2 2.2 %collective-permute-start.5 = (f32[3,128]{1,0:T(4,128)S(1)}, f32[3,128]{1,0:T(4,128)S(1)}, u32[]{:S(2)}, u32[]{:S(2)}) collective-permute-start(f32[3,128]{1,0:T(4,128)S(1)} %get-tuple-element.103), channel_id=1, source_target_pairs={{0,1},{1,0},{2,3},{3,2},{4,5},{5,4},{6,7},{7,6},{8,9},{9,8},{10,11... | collective-permute-start | bytes 4616 | tf_op jit(solution)/shard_map/ppermute | solution.py:559
  51.4 0.0 collective-permute-start.6
  51.4 2.8 %collective-permute-start.7 = (f32[3,128]{1,0:T(4,128)S(1)}, f32[3,128]{1,0:T(4,128)S(1)}, u32[]{:S(2)}, u32[]{:S(2)}) collective-permute-start(f32[3,128]{1,0:T(4,128)S(1)} %get-tuple-element.105), channel_id=1, source_target_pairs={{0,4},{1,5},{2,6},{3,7},{4,0},{5,1},{6,2},{7,3},{8,12},{9,13},{10,... | collective-permute-start | bytes 4616 | tf_op jit(solution)/shard_map/ppermute | solution.py:559
  54.2 1.2 %collective-permute-start.8 = (f32[3,128]{1,0:T(4,128)S(1)}, f32[3,128]{1,0:T(4,128)S(1)}, u32[]{:S(2)}, u32[]{:S(2)}) collective-permute-start(f32[3,128]{1,0:T(4,128)S(1)} %get-tuple-element.106), channel_id=1, source_target_pairs={{0,8},{1,9},{2,10},{3,11},{4,12},{5,13},{6,14},{7,15},{8,0},{9,1},... | collective-permute-start | bytes 4616 | tf_op jit(solution)/shard_map/ppermute | solution.py:559
  55.4 1.0 %collective-permute-start.9 = (f32[3,128]{1,0:T(4,128)S(1)}, f32[3,128]{1,0:T(4,128)S(1)}, u32[]{:S(2)}, u32[]{:S(2)}) collective-permute-start(f32[3,128]{1,0:T(4,128)S(1)} %get-tuple-element.107), channel_id=1, source_target_pairs={{0,16},{1,17},{2,18},{3,19},{4,20},{5,21},{6,22},{7,23},{8,24},{9,... | collective-permute-start | bytes 4616 | tf_op jit(solution)/shard_map/ppermute | solution.py:559
  56.4 2.4 %contact_base.1 = (f32[96,128]{1,0:T(8,128)S(1)}, f32[96,128]{1,0:T(8,128)S(1)}, f32[2,80,128]{2,1,0:T(8,128)S(1)}) custom-call(f32[96,128]{1,0:T(8,128)S(1)} %get-tuple-element.89.u, f32[96,128]{1,0:T(8,128)S(1)} %get-tuple-element.90.v, f32[96,128]{1,0:T(8,128)S(1)} %get-tuple-element.91.internal, f32[96,128]{1,0:T(8,128)S(1)} %get-tuple-element.63.fm, ...), custom_call_target="tpu_custom_call" | custom-call | bytes 1048576 | tf_op jit(solution)/shard_map/contact_base/pallas_call | solution.py:704
  58.8 0.0 collective-permute-done.5.rest_0_
  58.8 0.0 collective-permute-done.6.rest_1_
  58.9 0.0 collective-permute-done.7.rest_2_
  58.9 0.0 collective-permute-done.8.rest_3_
  58.9 0.4 collective-permute-done.9.rest_4_
  59.3 1.0 %contact_dots.1 = (f32[96,128]{1,0:T(8,128)S(1)}, f32[96,128]{1,0:T(8,128)S(1)}, f32[96,128]{1,0:T(8,128)S(1)}, f32[384,128]{1,0:T(8,128)S(1)}) custom-call(f32[96,128]{1,0:T(8,128)S(1)} %get-tuple-element.96.x1, f32[96,128]{1,0:T(8,128)S(1)} %get-tuple-element.97.v1, f32[2,80,128]{2,1,0:T(8,128)S(1)} %get-tuple-element.98.ab1, ...), custom_call_target="tpu_custom_call" | custom-call | bytes 1048576 | tf_op jit(solution)/shard_map/contact_dots/pallas_call | solution.py:711
  60.3 16.2 %all_to_all.16 = f32[128,1,384]{2,1,0:T(1,128)S(1)} all-to-all(f32[128,1,384]{2,1,0:T(1,128)S(1)} %bitcast.17), channel_id=1, replica_groups=mesh['dom'=128] {'dom'}, dimensions={0} | all-to-all | bytes 393216 | tf_op jit(solution)/shard_map/all_to_all | solution.py:573
  76.5 2.3 %contact_forces.1 = (f32[96,128]{1,0:T(8,128)S(1)}, f32[16,128]{1,0:T(8,128)S(1)}, f32[16,128]{1,0:T(8,128)S(1)}) custom-call(f32[384,128]{1,0:T(8,128)S(1)} %get-tuple-element.109.dots, f32[384,128]{1,0:T(8,128)S(1)} %bitcast.18, s32[16,128]{1,0:T(8,128)S(1)} %get-tuple-element.79.slave, s32[16,128]{1,0:T(8,128)S(1)} %get-tuple-element.101.slot, ...), custom_call_target="tpu_custom_call" | custom-call | bytes 1048576 | tf_op jit(solution)/shard_map/contact_forces/pallas_call | solution.py:719
  78.8 0.7 collective-permute-start.10
  79.6 0.8 collective-permute-done.10.given
  80.4 15.2 %all_to_all.17 = f32[64,1,1280]{2,1,0:T(1,128)S(1)} all-to-all(f32[64,1,1280]{2,1,0:T(1,128)S(1)} %bitcast.15), channel_id=1, replica_groups={{0,2,4,6,8,10,12,14,16,18,20,22,24,26,28,30,32,34,36,38,40,42,44,46,48,..., dimensions={0} | all-to-all | bytes 655360 | tf_op jit(solution)/shard_map/all_to_all | solution.py:573
  95.7 0.1 part_totals.1.mine
  95.7 1.8 %collective-permute-start.11 = (f32[80,128]{1,0:T(8,128)S(1)}, f32[80,128]{1,0:T(8,128)S(1)}, u32[]{:S(2)}, u32[]{:S(2)}) collective-permute-start(f32[80,128]{1,0:T(8,128)S(1)} %part_totals.1.mine), channel_id=1, source_target_pairs={{0,1},{1,0},{2,3},{3,2},{4,5},{5,4},{6,7},{7,6},{8,9},{9,8},{10,11... | collective-permute-start | bytes 122888 | tf_op jit(solution)/shard_map/ppermute | solution.py:559
  97.5 0.7 nodal_velocity.1
  98.2 0.2 collective-permute-done.11.other
  98.4 0.7 part_motion.1
  (1 shorter events, 0.0 us)
Async XLA Ops:
  36.5 5.9 %collective-permute-start = (f32[3,128]{1,0:T(4,128)S(1)}, f32[3,128]{1,0:T(4,128)S(1)}, u32[]{:S(2)}, u32[]{:S(2)}) collective-permute-start(f32[3,128]{1,0:T(4,128)S(1)} %get-tuple-element.73), channel_id=1, source_target_pairs={{0,1},{1,0},{2,3},{3,2},{4,5},{5,4},{6,7},{7,6},{8,9},{9,8},{10,11... | collective-permute-start | bytes 4616 | tf_op jit(solution)/shard_map/ppermute | solution.py:559
  37.4 5.0 %collective-permute-start.1 = (f32[3,128]{1,0:T(4,128)S(1)}, f32[3,128]{1,0:T(4,128)S(1)}, u32[]{:S(2)}, u32[]{:S(2)}) collective-permute-start(f32[3,128]{1,0:T(4,128)S(1)} %get-tuple-element.74), channel_id=1, source_target_pairs={{0,2},{1,3},{2,0},{3,1},{4,6},{5,7},{6,4},{7,5},{8,10},{9,11},{10,... | collective-permute-start | bytes 4616 | tf_op jit(solution)/shard_map/ppermute | solution.py:559
  37.7 4.7 %collective-permute-start.2 = (f32[3,128]{1,0:T(4,128)S(1)}, f32[3,128]{1,0:T(4,128)S(1)}, u32[]{:S(2)}, u32[]{:S(2)}) collective-permute-start(f32[3,128]{1,0:T(4,128)S(1)} %get-tuple-element.75), channel_id=1, source_target_pairs={{0,4},{1,5},{2,6},{3,7},{4,0},{5,1},{6,2},{7,3},{8,12},{9,13},{10,... | collective-permute-start | bytes 4616 | tf_op jit(solution)/shard_map/ppermute | solution.py:559
  39.4 3.0 %collective-permute-start.3 = (f32[3,128]{1,0:T(4,128)S(1)}, f32[3,128]{1,0:T(4,128)S(1)}, u32[]{:S(2)}, u32[]{:S(2)}) collective-permute-start(f32[3,128]{1,0:T(4,128)S(1)} %get-tuple-element.76), channel_id=1, source_target_pairs={{0,8},{1,9},{2,10},{3,11},{4,12},{5,13},{6,14},{7,15},{8,0},{9,1},... | collective-permute-start | bytes 4616 | tf_op jit(solution)/shard_map/ppermute | solution.py:559
  39.9 3.9 %collective-permute-start.4 = (f32[3,128]{1,0:T(4,128)S(1)}, f32[3,128]{1,0:T(4,128)S(1)}, u32[]{:S(2)}, u32[]{:S(2)}) collective-permute-start(f32[3,128]{1,0:T(4,128)S(1)} %get-tuple-element.77), channel_id=1, source_target_pairs={{0,16},{1,17},{2,18},{3,19},{4,20},{5,21},{6,22},{7,23},{8,24},{9,... | collective-permute-start | bytes 4616 | tf_op jit(solution)/shard_map/ppermute | solution.py:559
  49.2 9.6 %collective-permute-start.5 = (f32[3,128]{1,0:T(4,128)S(1)}, f32[3,128]{1,0:T(4,128)S(1)}, u32[]{:S(2)}, u32[]{:S(2)}) collective-permute-start(f32[3,128]{1,0:T(4,128)S(1)} %get-tuple-element.103), channel_id=1, source_target_pairs={{0,1},{1,0},{2,3},{3,2},{4,5},{5,4},{6,7},{7,6},{8,9},{9,8},{10,11... | collective-permute-start | bytes 4616 | tf_op jit(solution)/shard_map/ppermute | solution.py:559
  51.4 7.5 %collective-permute-start.6 = (f32[3,128]{1,0:T(4,128)S(1)}, f32[3,128]{1,0:T(4,128)S(1)}, u32[]{:S(2)}, u32[]{:S(2)}) collective-permute-start(f32[3,128]{1,0:T(4,128)S(1)} %get-tuple-element.104), channel_id=1, source_target_pairs={{0,2},{1,3},{2,0},{3,1},{4,6},{5,7},{6,4},{7,5},{8,10},{9,11},{10,... | collective-permute-start | bytes 4616 | tf_op jit(solution)/shard_map/ppermute | solution.py:559
  51.4 7.5 %collective-permute-start.7 = (f32[3,128]{1,0:T(4,128)S(1)}, f32[3,128]{1,0:T(4,128)S(1)}, u32[]{:S(2)}, u32[]{:S(2)}) collective-permute-start(f32[3,128]{1,0:T(4,128)S(1)} %get-tuple-element.105), channel_id=1, source_target_pairs={{0,4},{1,5},{2,6},{3,7},{4,0},{5,1},{6,2},{7,3},{8,12},{9,13},{10,... | collective-permute-start | bytes 4616 | tf_op jit(solution)/shard_map/ppermute | solution.py:559
  54.2 4.7 %collective-permute-start.8 = (f32[3,128]{1,0:T(4,128)S(1)}, f32[3,128]{1,0:T(4,128)S(1)}, u32[]{:S(2)}, u32[]{:S(2)}) collective-permute-start(f32[3,128]{1,0:T(4,128)S(1)} %get-tuple-element.106), channel_id=1, source_target_pairs={{0,8},{1,9},{2,10},{3,11},{4,12},{5,13},{6,14},{7,15},{8,0},{9,1},... | collective-permute-start | bytes 4616 | tf_op jit(solution)/shard_map/ppermute | solution.py:559
  55.4 3.9 %collective-permute-start.9 = (f32[3,128]{1,0:T(4,128)S(1)}, f32[3,128]{1,0:T(4,128)S(1)}, u32[]{:S(2)}, u32[]{:S(2)}) collective-permute-start(f32[3,128]{1,0:T(4,128)S(1)} %get-tuple-element.107), channel_id=1, source_target_pairs={{0,16},{1,17},{2,18},{3,19},{4,20},{5,21},{6,22},{7,23},{8,24},{9,... | collective-permute-start | bytes 4616 | tf_op jit(solution)/shard_map/ppermute | solution.py:559
  78.8 1.6 %collective-permute-start.10 = (f32[16,128]{1,0:T(8,128)S(1)}, f32[16,128]{1,0:T(8,128)S(1)}, u32[]{:S(2)}, u32[]{:S(2)}) collective-permute-start(f32[16,128]{1,0:T(8,128)S(1)} %get-tuple-element.114), channel_id=1, source_target_pairs={{0,1},{1,0},{2,3},{3,2},{4,5},{5,4},{6,7},{7,6},{8,9},{9,8},{10,11... | collective-permute-start | bytes 24584 | tf_op jit(solution)/shard_map/ppermute | solution.py:559
  95.7 2.6 %collective-permute-start.11 = (f32[80,128]{1,0:T(8,128)S(1)}, f32[80,128]{1,0:T(8,128)S(1)}, u32[]{:S(2)}, u32[]{:S(2)}) collective-permute-start(f32[80,128]{1,0:T(8,128)S(1)} %part_totals.1.mine), channel_id=1, source_target_pairs={{0,1},{1,0},{2,3},{3,2},{4,5},{5,4},{6,7},{7,6},{8,9},{9,8},{10,11... | collective-permute-start | bytes 122888 | tf_op jit(solution)/shard_map/ppermute | solution.py:559
